TPU v7x, 32 devices: a whole 2x2x4 slice. The times are simulated.
32 devices in a mesh: parts: 2 (over y), gx: 4 (over x, core), yz: 4 (over z).
Axes of the slice: x: 2, y: 2, z: 4, core: 2. Of those that a mesh axis runs over, the one named last changes fastest.
Arguments:
- tokens: bfloat16 [128, 18432], P(('parts', 'gx', 'yz')), parts along dimension 0, may hold values from -1500 to 1500
- gain: float32 [18432], replicated, may hold values from 0.1 to 1.9
- w_qkv: bfloat16 [18432, 12800], P('gx', 'yz'), may hold values from -0.046875 to 0.046875
- w_out: bfloat16 [12288, 18432], P('yz', 'gx'), may hold values from -0.21875 to 0.21875
- cache_keys: bfloat16 [128, 1024, 256], P(('parts', 'gx', 'yz')), parts along dimension 0, may hold values from -600 to 600
- cache_values: bfloat16 [128, 1024, 256], P(('parts', 'gx', 'yz')), parts along dimension 0, may hold values from -6 to 6
- cache_lengths: int32 [128], P(('parts', 'gx', 'yz')), parts along dimension 0, may hold values from 2 to 1024, as said below
Outputs:
- branch: bfloat16 [4, 32, 18432], P(None, ('parts', 'yz'), 'gx'), parts along dimension 1
There are 2 independent parts, one for each index of `parts`. A program takes and returns all parts, laid end to end along the dimension named above; an argument that names none is the same for every part. Nothing has to cross between parts.
Inputs may be any that keep to these rules, and one draw needn't show every extreme that they name: `cache_lengths`: filled slots of each sequence; some sequence uses all 1024 slots and some only 2.
All inputs are finite; a program needn't handle non-finite values.
Results may differ from a plain program's by a relative error of at most 0.012.
Values may be sent and summed in bfloat16 or wider, within the bound.
No kernel may reach another device: no remote copies, remote signals or barrier semaphores. Data moves between devices by JAX's collectives and lax.ppermute only.
A program may use at most 384 MiB of HBM per device.

v0:
```python
import jax
import jax.numpy as jnp
from jax import lax
from jax.sharding import PartitionSpec as P


def attend_local(qkv, cache_keys, cache_values, cache_lengths, width):
    seq_rows = qkv.shape[0]
    head = cache_keys.shape[2]
    slots = cache_keys.shape[1]
    scale = 1.0 / jnp.sqrt(jnp.float32(head))
    query = qkv[:, :width].reshape(seq_rows, width // head, head)
    key_new = qkv[:, width : width + head]
    value_new = qkv[:, width + head :]
    scores = (
        jnp.einsum("shd,std->sht", query, cache_keys, preferred_element_type=jnp.float32) * scale
    )
    own = jnp.einsum("shd,sd->sh", query, key_new, preferred_element_type=jnp.float32) * scale
    valid = jnp.arange(slots, dtype=jnp.int32)[None, None, :] < cache_lengths[:, None, None]
    masked = jnp.where(valid, scores, -jnp.inf)
    top = jnp.maximum(jnp.max(masked, axis=2), own)
    weights = jnp.where(valid, jnp.exp(masked - top[:, :, None]), 0.0)
    own_weight = jnp.exp(own - top)
    total = jnp.sum(weights, axis=2) + own_weight
    probs = (weights / total[:, :, None]).astype(jnp.bfloat16)
    own_prob = (own_weight / total).astype(jnp.bfloat16)
    mixed = jnp.einsum("sht,std->shd", probs, cache_values, preferred_element_type=jnp.float32)
    mixed = (
        mixed + own_prob.astype(jnp.float32)[:, :, None] * value_new.astype(jnp.float32)[:, None, :]
    )
    return mixed.reshape(seq_rows, width).astype(jnp.bfloat16)


def shards(tokens, gain, w_qkv, w_out, cache_keys, cache_values, cache_lengths):
    seq_rows = tokens.shape[0]
    groups = lax.axis_size("gx")
    blocks = lax.axis_size("yz")
    width = w_out.shape[0] * blocks
    xf = tokens.astype(jnp.float32)
    mean = jnp.mean(xf, axis=1, keepdims=True)
    centered = xf - mean
    variance = jnp.mean(centered * centered, axis=1, keepdims=True)
    normed = (centered / jnp.sqrt(variance + 1e-05) * gain[None, :]).astype(jnp.bfloat16)
    feature_rows = lax.all_to_all(normed, "gx", split_axis=1, concat_axis=0, tiled=True)
    column_count = w_qkv.shape[1]
    partial_value = jnp.dot(
        lax.all_gather(feature_rows, "yz", axis=0, tiled=True),
        w_qkv,
        preferred_element_type=jnp.float32,
    )
    partial_value = partial_value.reshape(blocks, groups, seq_rows, column_count)
    summed = lax.psum_scatter(partial_value, "gx", scatter_dimension=1, tiled=True)
    summed = summed.reshape(blocks, seq_rows, column_count).astype(jnp.bfloat16)
    received = lax.all_to_all(summed, "yz", split_axis=0, concat_axis=0, tiled=True)
    qkv = received.transpose(1, 0, 2).reshape(seq_rows, blocks * column_count)
    attended = attend_local(qkv, cache_keys, cache_values, cache_lengths, width)
    feature_block = w_out.shape[0]
    split = attended.reshape(seq_rows, blocks, feature_block)
    received = lax.all_to_all(split, "yz", split_axis=1, concat_axis=0, tiled=True)
    received = received.reshape(blocks * seq_rows, feature_block)
    everyone = lax.all_gather(received, "gx", axis=0, tiled=True)
    everyone = everyone.reshape(groups, blocks * seq_rows, feature_block)
    summed = lax.psum_scatter(
        jnp.einsum("gcf,fd->cgd", everyone, w_out, preferred_element_type=jnp.float32),
        "yz",
        scatter_dimension=0,
        tiled=True,
    )
    result = summed.transpose(1, 0, 2).astype(jnp.bfloat16)
    return result


def solution(mesh):
    placed = (
        P(("parts", "gx", "yz"), None),
        P(),
        P("gx", "yz"),
        P("yz", "gx"),
        P(("parts", "gx", "yz"), None, None),
        P(("parts", "gx", "yz"), None, None),
        P(("parts", "gx", "yz")),
    )
    return jax.shard_map(
        shards,
        mesh=mesh,
        in_specs=placed,
        out_specs=P(None, ("parts", "yz"), "gx"),
        check_vma=False,
    )
```

profile of v0, /device:TPU:0, one launch (start us, length us, event | category | flops | bytes accessed | tf_op | source)
XLA Modules:
  0.0 154.8 jit_solution(15320711918524439261)
XLA Ops:
  0.0 1.3 convert_reduce_fusion
  1.3 1.2 fusion.16
  2.6 1.8 %fusion.15 = bf16[4,18432]{1,0:T(4,128)(2,1)} fusion(bf16[4,18432]{1,0:T(4,128)(2,1)} %param.7, f32[18432]{0:T(1024)} %param.8, f32[4]{0:T(128)S(1)} %add_sqrt_fusion, f32[4]{0:T(128)S(1)} %broadcast_multiply_fusion), kind=kLoop, calls=%fused_computation.19 | loop fusion | flops 368640 | bytes 368672 | tf_op jit(solution)/shard_map/convert_element_type | solution.py:43
  4.4 4.2 %all-to-all-start = ((bf16[4,4,4608]{2,0,1:T(4,128)(2,1)}), bf16[4,4,4608]{2,0,1:T(4,128)(2,1)S(1)}, u32[]{:S(2)}, u32[]{:S(2)}) async-start(bf16[4,4,4608]{2,0,1:T(4,128)(2,1)} %bitcast), calls=%async_computation | async-start | bytes 294912 | tf_op jit(solution)/shard_map/all_to_all | solution.py:44
  8.6 1.3 dynamic-slice
  9.8 3.5 %all-to-all-done = bf16[4,4,4608]{2,0,1:T(4,128)(2,1)S(1)} async-done(((bf16[4,4,4608]{2,0,1:T(4,128)(2,1)}), bf16[4,4,4608]{2,0,1:T(4,128)(2,1)S(1)}, u32[]{:S(2)}, u32[]{:S(2)}) %all-to-all-start) | async-done | bytes 147488 | tf_op jit(solution)/shard_map/all_to_all | solution.py:44
  13.4 16.9 %all_gather.6 = bf16[64,4608]{1,0:T(8,128)(2,1)S(1)} all-gather(bf16[16,4608]{1,0:T(8,128)(2,1)S(1)} %all_to_all.31), channel_id=1, replica_groups=mesh['parts'=2,'gx'=4,'yz'=4] {'yz'}, dimensions={0}, use_global_device_ids=true | all-gather | bytes 737280 | tf_op jit(solution)/shard_map/all_gather | solution.py:47
  30.4 12.9 %fusion.29 = f32[64,3200]{1,0:T(8,128)} fusion(bf16[64,4608]{1,0:T(8,128)(2,1)S(1)} %all_gather.6, bf16[4608,3200]{1,0:T(8,128)(2,1)} %param.9), kind=kOutput, calls=%fused_computation.43 | convolution fusion | flops 1887436800 | bytes 30900224 | tf_op jit(solution)/shard_map/dot_general | solution.py:46
  43.3 1.4 reshape.63
  44.7 18.9 %all-reduce.4 = bf16[4,4,4,3200]{3,2,1,0:T(4,128)(2,1)S(1)} all-reduce(f32[4,4,4,3200]{3,2,1,0:T(4,128)S(1)} %reshape.63), channel_id=2, replica_groups=mesh['parts'=2,'gx'=4,'yz'=4] {'gx'}, use_global_device_ids=true, to_apply=%region_2.0.clone | all-reduce | flops 204800 | bytes 1228800
  63.6 1.3 fusion.18
  64.9 5.3 %all-to-all-start.1 = ((bf16[4,4,3200]{2,1,0:T(4,128)(2,1)}), bf16[4,4,3200]{2,1,0:T(4,128)(2,1)S(1)}, u32[]{:S(2)}, u32[]{:S(2)}) async-start(bf16[4,4,3200]{2,1,0:T(4,128)(2,1)} %fusion.18), calls=%async_computation.1 | async-start | bytes 204800 | tf_op jit(solution)/shard_map/all_to_all | solution.py:54
  70.3 5.8 %all-to-all-done.1 = bf16[4,4,3200]{2,1,0:T(4,128)(2,1)S(1)} async-done(((bf16[4,4,3200]{2,1,0:T(4,128)(2,1)}), bf16[4,4,3200]{2,1,0:T(4,128)(2,1)S(1)}, u32[]{:S(2)}, u32[]{:S(2)}) %all-to-all-start.1) | async-done | bytes 102432 | tf_op jit(solution)/shard_map/all_to_all | solution.py:54
  76.2 0.8 fusion.28
  77.1 0.3 fusion.7
  77.7 0.5 fusion.6
  78.2 0.7 copy.11
  78.9 3.3 %all-to-all-start.2 = ((bf16[4,4,3072]{2,0,1:T(4,128)(2,1)}), bf16[4,4,3072]{2,0,1:T(4,128)(2,1)S(1)}, u32[]{:S(2)}, u32[]{:S(2)}) async-start(bf16[4,4,3072]{2,0,1:T(4,128)(2,1)} %copy.11), calls=%async_computation.2 | async-start | bytes 196608 | tf_op jit(solution)/shard_map/all_to_all | solution.py:59
  82.3 0.7 dynamic-slice.2
  83.6 4.4 %all-to-all-done.2 = bf16[4,4,3072]{2,0,1:T(4,128)(2,1)S(1)} async-done(((bf16[4,4,3072]{2,0,1:T(4,128)(2,1)}), bf16[4,4,3072]{2,0,1:T(4,128)(2,1)S(1)}, u32[]{:S(2)}, u32[]{:S(2)}) %all-to-all-start.2) | async-done | bytes 98336 | tf_op jit(solution)/shard_map/all_to_all | solution.py:59
  88.1 6.1 %all_gather.7 = bf16[64,3072]{1,0:T(8,128)(2,1)S(1)} all-gather(bf16[16,3072]{1,0:T(8,128)(2,1)S(1)} %reshape.66), channel_id=1, replica_groups=mesh['parts'=2,'gx'=4,'yz'=4] {'gx'}, dimensions={0}, use_global_device_ids=true | all-gather | bytes 491520 | tf_op jit(solution)/shard_map/all_gather | solution.py:61
  94.2 11.8 %fusion.2 = f32[16,4,4608]{2,0,1:T(8,128)S(1)} fusion(bf16[4,16,3072]{2,1,0:T(8,128)(2,1)S(1)} %bitcast.43, bf16[3072,4608]{1,0:T(8,128)(2,1)} %param.10), kind=kOutput, calls=%fused_computation.2 | convolution fusion | flops 1811939328 | bytes 29884416 | tf_op jit(solution)/shard_map/gcf,fd->cgd/dot_general | solution.py:64
  106.0 47.1 %all-reduce.5 = bf16[16,4,4608]{2,0,1:T(8,128)(2,1)} all-reduce(f32[16,4,4608]{2,0,1:T(8,128)S(1)} %fusion.2), channel_id=3, replica_groups=mesh['parts'=2,'gx'=4,'yz'=4] {'yz'}, use_global_device_ids=true, to_apply=%region_5.6.clone | all-reduce | flops 294912 | bytes 1769472
  153.1 1.7 %fusion.17 = bf16[4,4,4608]{2,1,0:T(4,128)(2,1)} fusion(bf16[16,4,4608]{2,0,1:T(8,128)(2,1)} %all-reduce.5, u32[]{:T(128)S(6)} %multiply.15), kind=kLoop, calls=%fused_computation.23 | loop fusion | bytes 294916 | tf_op jit(solution)/shard_map/convert_element_type | solution.py:69
  (21 shorter events, 0.7 us)
Async XLA Ops:
  0.0 76.2 %copy-start = (bf16[4,1024,256]{2,1,0:T(8,128)(2,1)S(1)}, bf16[4,1024,256]{2,1,0:T(8,128)(2,1)}, u32[]{:S(2)}) copy-start(bf16[4,1024,256]{2,1,0:T(8,128)(2,1)} %param.11) | copy-start | bytes 6291460
  4.4 9.0 %all-to-all-start = ((bf16[4,4,4608]{2,0,1:T(4,128)(2,1)}), bf16[4,4,4608]{2,0,1:T(4,128)(2,1)S(1)}, u32[]{:S(2)}, u32[]{:S(2)}) async-start(bf16[4,4,4608]{2,0,1:T(4,128)(2,1)} %bitcast), calls=%async_computation | async-start | bytes 294912 | tf_op jit(solution)/shard_map/all_to_all | solution.py:44
  43.3 26.9 %copy-start.2 = (s32[4]{0:T(128)S(1)}, s32[4]{0:T(128)}, u32[]{:S(2)}) copy-start(s32[4]{0:T(128)} %param.13) | copy-start | bytes 52
  64.9 11.1 %all-to-all-start.1 = ((bf16[4,4,3200]{2,1,0:T(4,128)(2,1)}), bf16[4,4,3200]{2,1,0:T(4,128)(2,1)S(1)}, u32[]{:S(2)}, u32[]{:S(2)}) async-start(bf16[4,4,3200]{2,1,0:T(4,128)(2,1)} %fusion.18), calls=%async_computation.1 | async-start | bytes 204800 | tf_op jit(solution)/shard_map/all_to_all | solution.py:54
  76.1 1.6 %copy-start.3 = (bf16[4,1024,256]{2,1,0:T(8,128)(2,1)S(1)}, bf16[4,1024,256]{2,1,0:T(8,128)(2,1)}, u32[]{:S(2)}) copy-start(bf16[4,1024,256]{2,1,0:T(8,128)(2,1)} %param.12) | copy-start | bytes 6291460
  77.7 4.6 %copy-start.4 = (u32[32]{0:T(128)S(1)}, u32[32]{0:T(128)}, u32[]{:S(2)}) copy-start(u32[32]{0:T(128)} %constant.23) | copy-start | bytes 388
  78.9 9.1 %all-to-all-start.2 = ((bf16[4,4,3072]{2,0,1:T(4,128)(2,1)}), bf16[4,4,3072]{2,0,1:T(4,128)(2,1)S(1)}, u32[]{:S(2)}, u32[]{:S(2)}) async-start(bf16[4,4,3072]{2,0,1:T(4,128)(2,1)} %copy.11), calls=%async_computation.2 | async-start | bytes 196608 | tf_op jit(solution)/shard_map/all_to_all | solution.py:59
  94.2 60.5 %copy-start.1 = (bf16[4,1024,256]{2,1,0:T(8,128)(2,1)S(1)}, bf16[4,1024,256]{2,1,0:T(8,128)(2,1)}, u32[]{:S(2)}) copy-start(bf16[4,1024,256]{2,1,0:T(8,128)(2,1)} %param.11) | copy-start | bytes 6291460
where the time goes:
time: 155 us
  blocking collectives  89 us (57%)
  matrix products  26.2 us (17%)
  waiting for transfers between devices  13.7 us (9%)
  starting transfers between devices  12.8 us (8%)
  local copies, waits for them, and re-layouts  7.43 us (5%)
  other arithmetic  4.78 us (3%)
    unnamed x2, blocking collectives  66 us
    all_gather x1, blocking collectives, shards(): lax.all_gather(feature_rows, 'yz', axis=0, tiled=True)  16.9 us
    dot_general x1, matrix products, shards(): jnp.dot(lax.all_gather(feature_rows, 'yz', axis=0, tiled=True), w_qkv, pr...  12.9 us
    dot_general x1, matrix products, shards(): jnp.einsum('gcf,fd->cgd', everyone, w_out, preferred_element_type=jnp.flo...  11.8 us
    all_gather x1, blocking collectives, shards(): everyone = lax.all_gather(received, 'gx', axis=0, tiled=True)  6.15 us
    all_to_all x1, waiting for transfers between devices, shards(): lax.all_to_all(summed, 'yz', split_axis=0, concat_axis=0, tiled=True)  5.76 us
    all_to_all x1, starting transfers between devices, shards(): lax.all_to_all(summed, 'yz', split_axis=0, concat_axis=0, tiled=True)  5.3 us
    all_to_all x1, waiting for transfers between devices, shards(): lax.all_to_all(split, 'yz', split_axis=1, concat_axis=0, tiled=True)  4.43 us
  transfers between devices with their start and end apart: 3, of which 3 were waited for; matrix products, arithmetic and copies ran while one was open for 1% of the time, Pallas kernels for 0%

commit v1 on v0

--- a/solution.py
+++ b/solution.py
@@ -1,7 +1,219 @@
+import functools
+
 import jax
 import jax.numpy as jnp
 from jax import lax
+from jax.experimental import pallas as pl
+from jax.experimental.pallas import tpu as pltpu
 from jax.sharding import PartitionSpec as P
+
+VMEM = pl.BlockSpec(memory_space=pltpu.VMEM)
+SMEM = pl.BlockSpec(memory_space=pltpu.SMEM)
+ANY = pl.BlockSpec(memory_space=pl.ANY)
+MIB = 1 << 20
+
+
+def call(body, outs, in_specs, args, limit=8, scratch=(), flops=0, traffic=0):
+    return pl.pallas_call(
+        body,
+        out_shape=outs,
+        in_specs=in_specs,
+        out_specs=jax.tree.map(lambda _: VMEM, outs),
+        scratch_shapes=scratch,
+        compiler_params=pltpu.CompilerParams(vmem_limit_bytes=limit * MIB),
+        cost_estimate=pl.CostEstimate(flops=flops, bytes_accessed=traffic, transcendentals=0),
+    )(*args)
+
+
+def struct(shape, dtype=jnp.bfloat16):
+    return jax.ShapeDtypeStruct(shape, dtype)
+
+
+def exchange(pieces, axis):
+    size = lax.axis_size(axis)
+    return [pieces[0]] + [
+        lax.ppermute(pieces[k], axis, [(i, i ^ k) for i in range(size)]) for k in range(1, size)
+    ]
+
+
+def norm_body(x_ref, gain_ref, *out_refs):
+    block = out_refs[0].shape[1]
+    me = lax.axis_index("gx")
+    x = x_ref[...].astype(jnp.float32)
+    mean = jnp.mean(x, axis=1, keepdims=True)
+    centered = x - mean
+    variance = jnp.mean(centered * centered, axis=1, keepdims=True)
+    inverse = 1.0 / jnp.sqrt(variance + 1e-05)
+    for k, out_ref in enumerate(out_refs):
+        columns = pl.ds(pl.multiple_of((me ^ k) * block, 128), block)
+        part = x_ref[:, columns].astype(jnp.float32) - mean
+        out_ref[...] = (part * inverse * gain_ref[:, columns]).astype(jnp.bfloat16)
+
+
+def load_body(w_ref, _, out_ref, sem):
+    copy = pltpu.make_async_copy(w_ref, out_ref, sem)
+    copy.start()
+    copy.wait()
+
+
+def load(w, after):
+    w, after = lax.optimization_barrier((w, after))
+    size = w.shape[0] * w.shape[1] * 2
+    return pl.pallas_call(
+        load_body,
+        out_shape=pltpu.VMEM(w.shape, w.dtype),
+        in_specs=[ANY, ANY],
+        out_specs=VMEM,
+        scratch_shapes=[pltpu.SemaphoreType.DMA],
+        compiler_params=pltpu.CompilerParams(vmem_limit_bytes=MIB),
+        cost_estimate=pl.CostEstimate(flops=0, bytes_accessed=2 * size, transcendentals=0),
+    )(w, after)
+
+
+def project_body(tile, n, *refs):
+    pieces, w_ref, outs = refs[:n], refs[n], refs[n + 1 :]
+    rows = jnp.concatenate([p[...] for p in pieces], axis=0)
+    width = w_ref.shape[1]
+    each = rows.shape[0] // (n * n)
+
+    @pl.loop(0, width // tile)
+    def _(i):
+        columns = pl.ds(pl.multiple_of(i * tile, 128), tile)
+        total = jnp.dot(rows, w_ref[:, columns], preferred_element_type=jnp.float32)
+        for k, out in enumerate(outs):
+            group = [
+                total[(j * n + k) * each : (j * n + k + 1) * each] for j in range(n)
+            ]
+            out[:, columns] = jnp.concatenate(group, axis=0).astype(out.dtype)
+
+
+def project(pieces, w, tile):
+    n = len(pieces)
+    rows, width = pieces[0].shape[0], w.shape[1]
+    outs = [struct((rows, width), jnp.float32 if k == 0 else jnp.bfloat16) for k in range(n)]
+    w = pltpu.with_memory_space_constraint(w, pltpu.VMEM)
+    return call(
+        functools.partial(project_body, tile, n),
+        outs,
+        [VMEM] * (n + 1),
+        [*pieces, w],
+        limit=12,
+        flops=2 * n * rows * w.shape[0] * width,
+        traffic=2 * w.shape[0] * width,
+    )
+
+
+def total_body(*refs):
+    ins, outs = refs[: len(refs) // 2], refs[len(refs) // 2 :]
+    total = ins[0][...]
+    for r in ins[1:]:
+        total = total + r[...].astype(jnp.float32)
+    each = outs[0].shape[0]
+    for j, out in enumerate(outs):
+        out[...] = total[j * each : (j + 1) * each].astype(jnp.bfloat16)
+
+
+def attend_body(blocks, heads, length_ref, *refs):
+    pieces, (key_ref, value_ref) = refs[:blocks], refs[blocks : blocks + 2]
+    outs = refs[blocks + 2 : 2 * blocks + 2]
+    row_ref, query_ref, mixed_ref = refs[2 * blocks + 2 :]
+    me = lax.axis_index("yz")
+    part = pieces[0].shape[1]
+    seqs, slots, head = key_ref.shape
+    scale = 1.0 / jnp.sqrt(jnp.float32(head))
+    for j, piece in enumerate(pieces):
+        row_ref[:, pl.ds(pl.multiple_of((me ^ j) * part, 128), part)] = piece[...].astype(jnp.float32)
+    for h in range(heads):
+        query_ref[h] = row_ref[:, h * head : (h + 1) * head]
+    slot = lax.broadcasted_iota(jnp.int32, (1, slots), 1)
+    width = heads * head
+    for s in range(seqs):
+        query = query_ref[:, s, :]
+        key_new = row_ref[s : s + 1, width : width + head]
+        value_new = row_ref[s : s + 1, width + head : width + 2 * head]
+        own = jnp.sum(query * key_new, axis=1, keepdims=True) * scale
+        scores = lax.dot_general(
+            query.astype(jnp.bfloat16),
+            key_ref[s],
+            (((1,), (1,)), ((), ())),
+            preferred_element_type=jnp.float32,
+        )
+        masked = jnp.where(slot < length_ref[s], scores * scale, -jnp.inf)
+        top = jnp.maximum(jnp.max(masked, axis=1, keepdims=True), own)
+        weights = jnp.exp(masked - top)
+        own_weight = jnp.exp(own - top)
+        total = jnp.sum(weights, axis=1, keepdims=True) + own_weight
+        probs = (weights / total).astype(jnp.bfloat16)
+        own_prob = (own_weight / total).astype(jnp.bfloat16).astype(jnp.float32)
+        mixed = jnp.dot(probs, value_ref[s], preferred_element_type=jnp.float32)
+        mixed_ref[:, s, :] = mixed + own_prob * value_new
+    each = heads // blocks
+    for j, out in enumerate(outs):
+        first = (me ^ j) * each
+        for h in range(each):
+            out[:, h * head : (h + 1) * head] = mixed_ref[first + h].astype(jnp.bfloat16)
+
+
+def attend(pieces, cache_keys, cache_values, cache_lengths, width):
+    seqs, slots, head = cache_keys.shape
+    blocks, heads = len(pieces), width // head
+    keys = pltpu.with_memory_space_constraint(cache_keys, pltpu.VMEM)
+    values = pltpu.with_memory_space_constraint(cache_values, pltpu.VMEM)
+    return call(
+        functools.partial(attend_body, blocks, heads),
+        [struct((seqs, width // blocks))] * blocks,
+        [SMEM] + [VMEM] * (blocks + 2),
+        [cache_lengths, *pieces, keys, values],
+        limit=12,
+        scratch=[
+            pltpu.VMEM((seqs, width + 2 * head), jnp.float32),
+            pltpu.VMEM((heads, seqs, head), jnp.float32),
+            pltpu.VMEM((heads, seqs, head), jnp.float32),
+        ],
+        flops=4 * seqs * heads * head * slots,
+        traffic=4 * seqs * slots * head,
+    )
+
+
+def place_body(n, *refs):
+    pieces, out_ref = refs[:n], refs[n]
+    me = lax.axis_index("gx")
+    total = pieces[0][...]
+    for p in pieces[1:]:
+        total = total + p[...].astype(jnp.float32)
+    each = out_ref.shape[1]
+    for k in range(out_ref.shape[0]):
+        out_ref[me ^ k] = total[k * each : (k + 1) * each].astype(jnp.bfloat16)
+
+
+def shards(tokens, gain, w_qkv, w_out, cache_keys, cache_values, cache_lengths):
+    groups, blocks = lax.axis_size("gx"), lax.axis_size("yz")
+    seqs, depth = tokens.shape[0], w_qkv.shape[0]
+    width = w_out.shape[0] * blocks
+    normed = call(
+        norm_body,
+        [struct((seqs, depth))] * groups,
+        [VMEM, VMEM],
+        [tokens, gain.reshape(1, -1)],
+    )
+    mine = jnp.concatenate(exchange(normed, "gx"), axis=0)
+    w_near = load(w_qkv, mine)
+    pieces = exchange([mine] * blocks, "yz")
+    sums = exchange(project(pieces, w_near, 640), "gx")
+    parts = call(
+        total_body, [struct((seqs, w_qkv.shape[1]))] * blocks, [VMEM] * groups, sums
+    )
+    attended = attend(exchange(parts, "yz"), cache_keys, cache_values, cache_lengths, width)
+    mine = jnp.concatenate(exchange(attended, "yz"), axis=0)
+    w_near = load(w_out, mine)
+    pieces = exchange([mine] * groups, "gx")
+    sums = exchange(project(pieces, w_near, 512), "yz")
+    return call(
+        functools.partial(place_body, blocks),
+        struct((groups, seqs, w_out.shape[1])),
+        [VMEM] * blocks,
+        sums,
+    )
 
 
 def attend_local(qkv, cache_keys, cache_values, cache_lengths, width):
@@ -31,7 +243,7 @@
     return mixed.reshape(seq_rows, width).astype(jnp.bfloat16)
 
 
-def shards(tokens, gain, w_qkv, w_out, cache_keys, cache_values, cache_lengths):
+def shards_any(tokens, gain, w_qkv, w_out, cache_keys, cache_values, cache_lengths):
     seq_rows = tokens.shape[0]
     groups = lax.axis_size("gx")
     blocks = lax.axis_size("yz")
@@ -66,8 +278,7 @@
         scatter_dimension=0,
         tiled=True,
     )
-    result = summed.transpose(1, 0, 2).astype(jnp.bfloat16)
-    return result
+    return summed.transpose(1, 0, 2).astype(jnp.bfloat16)
 
 
 def solution(mesh):
@@ -80,8 +291,9 @@
         P(("parts", "gx", "yz"), None, None),
         P(("parts", "gx", "yz")),
     )
+    small = mesh.shape["gx"] == 4 and mesh.shape["yz"] == 4
     return jax.shard_map(
-        shards,
+        shards if small else shards_any,
         mesh=mesh,
         in_specs=placed,
         out_specs=P(None, ("parts", "yz"), "gx"),

time: 155 us -> 89.8 us (0.58)
  blocking collectives: 89 us -> 0 us
  Pallas kernels: 0 us -> 34.3 us
  matrix products: 26.2 us -> 0 us
  waiting for transfers between devices: 13.7 us -> 28.3 us
  starting transfers between devices: 12.8 us -> 24.8 us
  local copies, waits for them, and re-layouts: 7.43 us -> 1.81 us
  other arithmetic: 4.78 us -> 0.15 us
    unnamed x2 -> x0, blocking collectives: 66 us -> none
    pallas_call x0 -> x8, Pallas kernels: none -> 34.3 us  [the longest x2 18.5 us: load(): pl.pallas_call(load_body, out_shape=pltpu.VMEM(w.shape, w.dtype), in_spec...]
    ppermute x0 -> x21, waiting for transfers between devices: none -> 28.3 us  [exchange(): lax.ppermute(pieces[k], axis, [(i, i ^ k) for i in range(size)])]
    dot_general x5 -> x0, matrix products: 26.2 us -> none  [the longest x1 12.9 us: shards(): jnp.dot(lax.all_gather(feature_rows, 'yz', axis=0, tiled=True), w_qkv, pr...]
    ppermute x0 -> x21, starting transfers between devices: none -> 24.8 us  [exchange(): lax.ppermute(pieces[k], axis, [(i, i ^ k) for i in range(size)])]
    all_gather x2 -> x0, blocking collectives: 23.1 us -> none  [the longest x1 16.9 us: shards(): lax.all_gather(feature_rows, 'yz', axis=0, tiled=True)]
    all_to_all x3 -> x0, waiting for transfers between devices: 13.7 us -> none  [the longest x1 5.76 us: shards(): lax.all_to_all(summed, 'yz', split_axis=0, concat_axis=0, tiled=True)]
    all_to_all x3 -> x0, starting transfers between devices: 12.8 us -> none  [the longest x1 5.3 us: shards(): lax.all_to_all(summed, 'yz', split_axis=0, concat_axis=0, tiled=True)]
  transfers between devices with their start and end apart: 3 -> 21, of which waited for: 3 -> 11; matrix products, arithmetic and copies ran while one was open for 1% -> 0% of each run, Pallas kernels for 0% -> 21%
where the time goes in v1:
time: 89.8 us; the launch traced here: 89.5 us
  Pallas kernels  34.3 us (38%)
  waiting for transfers between devices  28.3 us (32%)
  starting transfers between devices  24.8 us (28%)
  local copies, waits for them, and re-layouts  1.81 us (2%)
    ppermute x21, waiting for transfers between devices, exchange(): lax.ppermute(pieces[k], axis, [(i, i ^ k) for i in range(size)])  28.3 us
    ppermute x21, starting transfers between devices, exchange(): lax.ppermute(pieces[k], axis, [(i, i ^ k) for i in range(size)])  24.8 us
    pallas_call x2, Pallas kernels, load(): pl.pallas_call(load_body, out_shape=pltpu.VMEM(w.shape, w.dtype), in_spec...  18.5 us
    pallas_call x6, Pallas kernels, call(): pl.pallas_call(body, out_shape=outs, in_specs=in_specs, out_specs=jax.tre...  15.9 us
    unnamed x10, local copies, waits for them, and re-layouts  1.81 us
  transfers between devices with their start and end apart: 21, of which 11 were waited for; matrix products, arithmetic and copies ran while one was open for 0% of the time, Pallas kernels for 21%

profile of v1, /device:TPU:0, one launch (start us, length us, event | category | flops | bytes accessed | tf_op | source)
XLA Modules:
  0.0 89.5 jit_solution(9275821094254261924)
XLA Ops:
  2.9 2.6 %collective-permute-start.1 = (bf16[4,4608]{1,0:T(4,128)(2,1)S(1)}, bf16[4,4608]{1,0:T(4,128)(2,1)S(1)}, u32[]{:S(2)}, u32[]{:S(2)}) collective-permute-start(bf16[4,4608]{1,0:T(4,128)(2,1)S(1)} %get-tuple-element.31), channel_id=1, source_target_pairs={{0,8},{4,12},{8,0},{12,4},{1,9},{5,13},{9,1},{13,5},{2,10},{6,14},... | collective-permute-start | bytes 110600 | tf_op jit(solution)/shard_map/ppermute | solution.py:35
  5.5 2.0 %collective-permute-done.1 = bf16[4,4608]{1,0:T(4,128)(2,1)S(1)} collective-permute-done((bf16[4,4608]{1,0:T(4,128)(2,1)S(1)}, bf16[4,4608]{1,0:T(4,128)(2,1)S(1)}, u32[]{:S(2)}, u32[]{:S(2)}) %collective-permute-start.1) | collective-permute-done | bytes 36896 | tf_op jit(solution)/shard_map/ppermute | solution.py:35
  7.5 1.4 %collective-permute-done.2 = bf16[4,4608]{1,0:T(4,128)(2,1)S(1)} collective-permute-done((bf16[4,4608]{1,0:T(4,128)(2,1)S(1)}, bf16[4,4608]{1,0:T(4,128)(2,1)S(1)}, u32[]{:S(2)}, u32[]{:S(2)}) %collective-permute-start.2) | collective-permute-done | bytes 36896 | tf_op jit(solution)/shard_map/ppermute | solution.py:35
  9.0 3.7 %collective-permute-start.5 = (bf16[16,4608]{1,0:T(8,128)(2,1)S(1)}, bf16[16,4608]{1,0:T(8,128)(2,1)S(1)}, u32[]{:S(2)}, u32[]{:S(2)}) collective-permute-start(bf16[16,4608]{1,0:T(8,128)(2,1)S(1)} %pad_maximum_fusion._.refs_0_), channel_id=1, source_target_pairs={{0,3},{1,2},{2,1},{3,0},{4,7},{5,6},{6,5},{7,4},{8,11},{9,10},{10,... | collective-permute-start | bytes 442376 | tf_op jit(solution)/shard_map/ppermute | solution.py:35
  13.4 9.4 %shard_map.74.refs_4_ = bf16[4608,3200]{1,0:T(8,128)(2,1)S(1)} custom-call(bf16[4608,3200]{1,0:T(8,128)(2,1)} %w_ref, bf16[16,4608]{1,0:T(8,128)(2,1)S(1)} %pad_maximum_fusion._.refs_0_), custom_call_target="tpu_custom_call" | custom-call | bytes 58982400 | tf_op jit(solution)/shard_map/pallas_call | solution.py:62
  22.9 2.6 %collective-permute-done.4.refs_2_ = bf16[16,4608]{1,0:T(8,128)(2,1)S(1)} collective-permute-done((bf16[16,4608]{1,0:T(8,128)(2,1)S(1)}, bf16[16,4608]{1,0:T(8,128)(2,1)S(1)}, u32[]{:S(2)}, u32[]{:S(2)}) %collective-permute-start.4) | collective-permute-done | bytes 147488 | tf_op jit(solution)/shard_map/ppermute | solution.py:35
  25.4 5.7 %shard_map.75 = (f32[16,3200]{1,0:T(8,128)S(1)}, bf16[16,3200]{1,0:T(8,128)(2,1)S(1)}, bf16[16,3200]{1,0:T(8,128)(2,1)S(1)}, bf16[16,3200]{1,0:T(8,128)(2,1)S(1)}) custom-call(bf16[16,4608]{1,0:T(8,128)(2,1)S(1)} %pad_maximum_fusion._.refs_0_, bf16[16,4608]{1,0:T(8,128)(2,1)S(1)} %collective-permute-done.3.refs_1_, ...), custom_call_target="tpu_custom_call" | custom-call | flops 1887436800 | bytes 29491200 | tf_op jit(solution)/shard_map/pallas_call | solution.py:17
  31.2 1.0 %collective-permute-start.7 = (bf16[16,3200]{1,0:T(8,128)(2,1)S(1)}, bf16[16,3200]{1,0:T(8,128)(2,1)S(1)}, u32[]{:S(2)}, u32[]{:S(2)}) collective-permute-start(bf16[16,3200]{1,0:T(8,128)(2,1)S(1)} %get-tuple-element.37), channel_id=1, source_target_pairs={{0,8},{4,12},{8,0},{12,4},{1,9},{5,13},{9,1},{13,5},{2,10},{6,14},... | collective-permute-start | bytes 307208 | tf_op jit(solution)/shard_map/ppermute | solution.py:35
  33.1 3.9 %collective-permute-done.7.refs_2_ = bf16[16,3200]{1,0:T(8,128)(2,1)S(1)} collective-permute-done((bf16[16,3200]{1,0:T(8,128)(2,1)S(1)}, bf16[16,3200]{1,0:T(8,128)(2,1)S(1)}, u32[]{:S(2)}, u32[]{:S(2)}) %collective-permute-start.7) | collective-permute-done | bytes 102432 | tf_op jit(solution)/shard_map/ppermute | solution.py:35
  37.0 1.3 %collective-permute-done.8.refs_3_ = bf16[16,3200]{1,0:T(8,128)(2,1)S(1)} collective-permute-done((bf16[16,3200]{1,0:T(8,128)(2,1)S(1)}, bf16[16,3200]{1,0:T(8,128)(2,1)S(1)}, u32[]{:S(2)}, u32[]{:S(2)}) %collective-permute-start.8) | collective-permute-done | bytes 102432 | tf_op jit(solution)/shard_map/ppermute | solution.py:35
  38.4 3.0 %collective-permute-start.10 = (bf16[4,3200]{1,0:T(4,128)(2,1)S(1)}, bf16[4,3200]{1,0:T(4,128)(2,1)S(1)}, u32[]{:S(2)}, u32[]{:S(2)}) collective-permute-start(bf16[4,3200]{1,0:T(4,128)(2,1)S(1)} %get-tuple-element.41), channel_id=1, source_target_pairs={{0,2},{1,3},{2,0},{3,1},{4,6},{5,7},{6,4},{7,5},{8,10},{9,11},{10,... | collective-permute-start | bytes 76808 | tf_op jit(solution)/shard_map/ppermute | solution.py:35
  41.4 1.3 %collective-permute-start.11 = (bf16[4,3200]{1,0:T(4,128)(2,1)S(1)}, bf16[4,3200]{1,0:T(4,128)(2,1)S(1)}, u32[]{:S(2)}, u32[]{:S(2)}) collective-permute-start(bf16[4,3200]{1,0:T(4,128)(2,1)S(1)} %get-tuple-element.42), channel_id=1, source_target_pairs={{0,3},{1,2},{2,1},{3,0},{4,7},{5,6},{6,5},{7,4},{8,11},{9,10},{10,... | collective-permute-start | bytes 76808 | tf_op jit(solution)/shard_map/ppermute | solution.py:35
  43.3 3.8 %collective-permute-done.11.refs_3_ = bf16[4,3200]{1,0:T(4,128)(2,1)S(1)} collective-permute-done((bf16[4,3200]{1,0:T(4,128)(2,1)S(1)}, bf16[4,3200]{1,0:T(4,128)(2,1)S(1)}, u32[]{:S(2)}, u32[]{:S(2)}) %collective-permute-start.11) | collective-permute-done | bytes 25632 | tf_op jit(solution)/shard_map/ppermute | solution.py:35
  47.1 2.8 %shard_map.77 = (bf16[4,3072]{1,0:T(4,128)(2,1)S(1)}, bf16[4,3072]{1,0:T(4,128)(2,1)S(1)}, bf16[4,3072]{1,0:T(4,128)(2,1)S(1)}, bf16[4,3072]{1,0:T(4,128)(2,1)S(1)}) custom-call(s32[4]{0:T(128)S(1)} %copy-done.4, bf16[4,3200]{1,0:T(4,128)(2,1)S(1)} %get-tuple-element.39.refs_0_, bf16[4,3200]{1,0:T(4,128)(2,1)S(1)} %collective-permute-done.9.refs_1_, ...), custom_call_target="tpu_custom_call" | custom-call | flops 201326592 | bytes 4194304 | tf_op jit(solution)/shard_map/pallas_call | solution.py:17
  50.0 1.9 %collective-permute-start.13 = (bf16[4,3072]{1,0:T(4,128)(2,1)S(1)}, bf16[4,3072]{1,0:T(4,128)(2,1)S(1)}, u32[]{:S(2)}, u32[]{:S(2)}) collective-permute-start(bf16[4,3072]{1,0:T(4,128)(2,1)S(1)} %get-tuple-element.45), channel_id=1, source_target_pairs={{0,2},{1,3},{2,0},{3,1},{4,6},{5,7},{6,4},{7,5},{8,10},{9,11},{10,... | collective-permute-start | bytes 73736 | tf_op jit(solution)/shard_map/ppermute | solution.py:35
  51.9 2.5 %collective-permute-start.14 = (bf16[4,3072]{1,0:T(4,128)(2,1)S(1)}, bf16[4,3072]{1,0:T(4,128)(2,1)S(1)}, u32[]{:S(2)}, u32[]{:S(2)}) collective-permute-start(bf16[4,3072]{1,0:T(4,128)(2,1)S(1)} %get-tuple-element.46), channel_id=1, source_target_pairs={{0,3},{1,2},{2,1},{3,0},{4,7},{5,6},{6,5},{7,4},{8,11},{9,10},{10,... | collective-permute-start | bytes 73736 | tf_op jit(solution)/shard_map/ppermute | solution.py:35
  55.0 2.5 %collective-permute-done.14 = bf16[4,3072]{1,0:T(4,128)(2,1)S(1)} collective-permute-done((bf16[4,3072]{1,0:T(4,128)(2,1)S(1)}, bf16[4,3072]{1,0:T(4,128)(2,1)S(1)}, u32[]{:S(2)}, u32[]{:S(2)}) %collective-permute-start.14) | collective-permute-done | bytes 24608 | tf_op jit(solution)/shard_map/ppermute | solution.py:35
  57.6 1.0 %collective-permute-start.16 = (bf16[16,3072]{1,0:T(8,128)(2,1)S(1)}, bf16[16,3072]{1,0:T(8,128)(2,1)S(1)}, u32[]{:S(2)}, u32[]{:S(2)}) collective-permute-start(bf16[16,3072]{1,0:T(8,128)(2,1)S(1)} %pad_maximum_fusion.1._.refs_0_), channel_id=1, source_target_pairs={{0,8},{4,12},{8,0},{12,4},{1,9},{5,13},{9,1},{13,5},{2,10},{6,14},... | collective-permute-start | bytes 294920 | tf_op jit(solution)/shard_map/ppermute | solution.py:35
  59.5 9.1 %shard_map.78.refs_4_ = bf16[3072,4608]{1,0:T(8,128)(2,1)S(1)} custom-call(bf16[3072,4608]{1,0:T(8,128)(2,1)} %w_ref.1, bf16[16,3072]{1,0:T(8,128)(2,1)S(1)} %pad_maximum_fusion.1._.refs_0_), custom_call_target="tpu_custom_call" | custom-call | bytes 56623104 | tf_op jit(solution)/shard_map/pallas_call | solution.py:62
  68.6 6.0 %shard_map.79 = (f32[16,4608]{1,0:T(8,128)S(1)}, bf16[16,4608]{1,0:T(8,128)(2,1)S(1)}, bf16[16,4608]{1,0:T(8,128)(2,1)S(1)}, bf16[16,4608]{1,0:T(8,128)(2,1)S(1)}) custom-call(bf16[16,3072]{1,0:T(8,128)(2,1)S(1)} %pad_maximum_fusion.1._.refs_0_, bf16[16,3072]{1,0:T(8,128)(2,1)S(1)} %collective-permute-done.15.refs_1_, ...), custom_call_target="tpu_custom_call" | custom-call | flops 1811939328 | bytes 28311552 | tf_op jit(solution)/shard_map/pallas_call | solution.py:17
  74.7 3.0 %collective-permute-start.19 = (bf16[16,4608]{1,0:T(8,128)(2,1)S(1)}, bf16[16,4608]{1,0:T(8,128)(2,1)S(1)}, u32[]{:S(2)}, u32[]{:S(2)}) collective-permute-start(bf16[16,4608]{1,0:T(8,128)(2,1)S(1)} %get-tuple-element.51), channel_id=1, source_target_pairs={{0,2},{1,3},{2,0},{3,1},{4,6},{5,7},{6,4},{7,5},{8,10},{9,11},{10,... | collective-permute-start | bytes 442376 | tf_op jit(solution)/shard_map/ppermute | solution.py:35
  77.7 1.4 %collective-permute-start.20 = (bf16[16,4608]{1,0:T(8,128)(2,1)S(1)}, bf16[16,4608]{1,0:T(8,128)(2,1)S(1)}, u32[]{:S(2)}, u32[]{:S(2)}) collective-permute-start(bf16[16,4608]{1,0:T(8,128)(2,1)S(1)} %get-tuple-element.52), channel_id=1, source_target_pairs={{0,3},{1,2},{2,1},{3,0},{4,7},{5,6},{6,5},{7,4},{8,11},{9,10},{10,... | collective-permute-start | bytes 442376 | tf_op jit(solution)/shard_map/ppermute | solution.py:35
  79.1 3.9 %collective-permute-done.18.refs_1_ = bf16[16,4608]{1,0:T(8,128)(2,1)S(1)} collective-permute-done((bf16[16,4608]{1,0:T(8,128)(2,1)S(1)}, bf16[16,4608]{1,0:T(8,128)(2,1)S(1)}, u32[]{:S(2)}, u32[]{:S(2)}) %collective-permute-start.18) | collective-permute-done | bytes 147488 | tf_op jit(solution)/shard_map/ppermute | solution.py:35
  83.0 5.8 %collective-permute-done.19.refs_2_ = bf16[16,4608]{1,0:T(8,128)(2,1)S(1)} collective-permute-done((bf16[16,4608]{1,0:T(8,128)(2,1)S(1)}, bf16[16,4608]{1,0:T(8,128)(2,1)S(1)}, u32[]{:S(2)}, u32[]{:S(2)}) %collective-permute-start.19) | collective-permute-done | bytes 147488 | tf_op jit(solution)/shard_map/ppermute | solution.py:35
  (38 shorter events, 7.9 us)
Async XLA Ops:
  2.4 3.2 %collective-permute-start = (bf16[4,4608]{1,0:T(4,128)(2,1)S(1)}, bf16[4,4608]{1,0:T(4,128)(2,1)S(1)}, u32[]{:S(2)}, u32[]{:S(2)}) collective-permute-start(bf16[4,4608]{1,0:T(4,128)(2,1)S(1)} %get-tuple-element.30), channel_id=1, source_target_pairs={{0,4},{4,0},{8,12},{12,8},{1,5},{5,1},{9,13},{13,9},{2,6},{6,2},{1... | collective-permute-start | bytes 110600 | tf_op jit(solution)/shard_map/ppermute | solution.py:35
  2.9 4.6 %collective-permute-start.1 = (bf16[4,4608]{1,0:T(4,128)(2,1)S(1)}, bf16[4,4608]{1,0:T(4,128)(2,1)S(1)}, u32[]{:S(2)}, u32[]{:S(2)}) collective-permute-start(bf16[4,4608]{1,0:T(4,128)(2,1)S(1)} %get-tuple-element.31), channel_id=1, source_target_pairs={{0,8},{4,12},{8,0},{12,4},{1,9},{5,13},{9,1},{13,5},{2,10},{6,14},... | collective-permute-start | bytes 110600 | tf_op jit(solution)/shard_map/ppermute | solution.py:35
  5.4 3.4 %collective-permute-start.2 = (bf16[4,4608]{1,0:T(4,128)(2,1)S(1)}, bf16[4,4608]{1,0:T(4,128)(2,1)S(1)}, u32[]{:S(2)}, u32[]{:S(2)}) collective-permute-start(bf16[4,4608]{1,0:T(4,128)(2,1)S(1)} %get-tuple-element.32), channel_id=1, source_target_pairs={{0,12},{4,8},{8,4},{12,0},{1,13},{5,9},{9,5},{13,1},{2,14},{6,10},... | collective-permute-start | bytes 110600 | tf_op jit(solution)/shard_map/ppermute | solution.py:35
  9.0 13.9 %collective-permute-start.5 = (bf16[16,4608]{1,0:T(8,128)(2,1)S(1)}, bf16[16,4608]{1,0:T(8,128)(2,1)S(1)}, u32[]{:S(2)}, u32[]{:S(2)}) collective-permute-start(bf16[16,4608]{1,0:T(8,128)(2,1)S(1)} %pad_maximum_fusion._.refs_0_), channel_id=1, source_target_pairs={{0,3},{1,2},{2,1},{3,0},{4,7},{5,6},{6,5},{7,4},{8,11},{9,10},{10,... | collective-permute-start | bytes 442376 | tf_op jit(solution)/shard_map/ppermute | solution.py:35
  12.6 12.8 %collective-permute-start.4 = (bf16[16,4608]{1,0:T(8,128)(2,1)S(1)}, bf16[16,4608]{1,0:T(8,128)(2,1)S(1)}, u32[]{:S(2)}, u32[]{:S(2)}) collective-permute-start(bf16[16,4608]{1,0:T(8,128)(2,1)S(1)} %pad_maximum_fusion._.refs_0_), channel_id=1, source_target_pairs={{0,2},{1,3},{2,0},{3,1},{4,6},{5,7},{6,4},{7,5},{8,10},{9,11},{10,... | collective-permute-start | bytes 442376 | tf_op jit(solution)/shard_map/ppermute | solution.py:35
  12.6 12.8 %collective-permute-start.3 = (bf16[16,4608]{1,0:T(8,128)(2,1)S(1)}, bf16[16,4608]{1,0:T(8,128)(2,1)S(1)}, u32[]{:S(2)}, u32[]{:S(2)}) collective-permute-start(bf16[16,4608]{1,0:T(8,128)(2,1)S(1)} %pad_maximum_fusion._.refs_0_), channel_id=1, source_target_pairs={{0,1},{1,0},{2,3},{3,2},{4,5},{5,4},{6,7},{7,6},{8,9},{9,8},{10,11... | collective-permute-start | bytes 442376 | tf_op jit(solution)/shard_map/ppermute | solution.py:35
  22.8 24.3 %copy-start = (bf16[4,1024,256]{2,1,0:T(8,128)(2,1)S(1)}, bf16[4,1024,256]{2,1,0:T(8,128)(2,1)}, u32[]{:S(2)}) copy-start(bf16[4,1024,256]{2,1,0:T(8,128)(2,1)} %refs_4_.1) | copy-start | bytes 6291460
  22.8 24.3 %copy-start.1 = (bf16[4,1024,256]{2,1,0:T(8,128)(2,1)S(1)}, bf16[4,1024,256]{2,1,0:T(8,128)(2,1)}, u32[]{:S(2)}) copy-start(bf16[4,1024,256]{2,1,0:T(8,128)(2,1)} %refs_5_.1) | copy-start | bytes 6291460
  22.8 24.2 %copy-start.4 = (s32[4]{0:T(128)S(1)}, s32[4]{0:T(128)}, u32[]{:S(2)}) copy-start(s32[4]{0:T(128)} %length_ref.1) | copy-start | bytes 52
  31.1 1.9 %collective-permute-start.6 = (bf16[16,3200]{1,0:T(8,128)(2,1)S(1)}, bf16[16,3200]{1,0:T(8,128)(2,1)S(1)}, u32[]{:S(2)}, u32[]{:S(2)}) collective-permute-start(bf16[16,3200]{1,0:T(8,128)(2,1)S(1)} %get-tuple-element.36), channel_id=1, source_target_pairs={{0,4},{4,0},{8,12},{12,8},{1,5},{5,1},{9,13},{13,9},{2,6},{6,2},{1... | collective-permute-start | bytes 307208 | tf_op jit(solution)/shard_map/ppermute | solution.py:35
  31.2 5.7 %collective-permute-start.7 = (bf16[16,3200]{1,0:T(8,128)(2,1)S(1)}, bf16[16,3200]{1,0:T(8,128)(2,1)S(1)}, u32[]{:S(2)}, u32[]{:S(2)}) collective-permute-start(bf16[16,3200]{1,0:T(8,128)(2,1)S(1)} %get-tuple-element.37), channel_id=1, source_target_pairs={{0,8},{4,12},{8,0},{12,4},{1,9},{5,13},{9,1},{13,5},{2,10},{6,14},... | collective-permute-start | bytes 307208 | tf_op jit(solution)/shard_map/ppermute | solution.py:35
  32.2 6.0 %collective-permute-start.8 = (bf16[16,3200]{1,0:T(8,128)(2,1)S(1)}, bf16[16,3200]{1,0:T(8,128)(2,1)S(1)}, u32[]{:S(2)}, u32[]{:S(2)}) collective-permute-start(bf16[16,3200]{1,0:T(8,128)(2,1)S(1)} %get-tuple-element.38), channel_id=1, source_target_pairs={{0,12},{4,8},{8,4},{12,0},{1,13},{5,9},{9,5},{13,1},{2,14},{6,10},... | collective-permute-start | bytes 307208 | tf_op jit(solution)/shard_map/ppermute | solution.py:35
  38.3 4.5 %collective-permute-start.9 = (bf16[4,3200]{1,0:T(4,128)(2,1)S(1)}, bf16[4,3200]{1,0:T(4,128)(2,1)S(1)}, u32[]{:S(2)}, u32[]{:S(2)}) collective-permute-start(bf16[4,3200]{1,0:T(4,128)(2,1)S(1)} %get-tuple-element.40), channel_id=1, source_target_pairs={{0,1},{1,0},{2,3},{3,2},{4,5},{5,4},{6,7},{7,6},{8,9},{9,8},{10,11... | collective-permute-start | bytes 76808 | tf_op jit(solution)/shard_map/ppermute | solution.py:35
  38.4 4.8 %collective-permute-start.10 = (bf16[4,3200]{1,0:T(4,128)(2,1)S(1)}, bf16[4,3200]{1,0:T(4,128)(2,1)S(1)}, u32[]{:S(2)}, u32[]{:S(2)}) collective-permute-start(bf16[4,3200]{1,0:T(4,128)(2,1)S(1)} %get-tuple-element.41), channel_id=1, source_target_pairs={{0,2},{1,3},{2,0},{3,1},{4,6},{5,7},{6,4},{7,5},{8,10},{9,11},{10,... | collective-permute-start | bytes 76808 | tf_op jit(solution)/shard_map/ppermute | solution.py:35
  41.4 5.6 %collective-permute-start.11 = (bf16[4,3200]{1,0:T(4,128)(2,1)S(1)}, bf16[4,3200]{1,0:T(4,128)(2,1)S(1)}, u32[]{:S(2)}, u32[]{:S(2)}) collective-permute-start(bf16[4,3200]{1,0:T(4,128)(2,1)S(1)} %get-tuple-element.42), channel_id=1, source_target_pairs={{0,3},{1,2},{2,1},{3,0},{4,7},{5,6},{6,5},{7,4},{8,11},{9,10},{10,... | collective-permute-start | bytes 76808 | tf_op jit(solution)/shard_map/ppermute | solution.py:35
  49.9 4.5 %collective-permute-start.12 = (bf16[4,3072]{1,0:T(4,128)(2,1)S(1)}, bf16[4,3072]{1,0:T(4,128)(2,1)S(1)}, u32[]{:S(2)}, u32[]{:S(2)}) collective-permute-start(bf16[4,3072]{1,0:T(4,128)(2,1)S(1)} %get-tuple-element.44), channel_id=1, source_target_pairs={{0,1},{1,0},{2,3},{3,2},{4,5},{5,4},{6,7},{7,6},{8,9},{9,8},{10,11... | collective-permute-start | bytes 73736 | tf_op jit(solution)/shard_map/ppermute | solution.py:35
  50.0 5.0 %collective-permute-start.13 = (bf16[4,3072]{1,0:T(4,128)(2,1)S(1)}, bf16[4,3072]{1,0:T(4,128)(2,1)S(1)}, u32[]{:S(2)}, u32[]{:S(2)}) collective-permute-start(bf16[4,3072]{1,0:T(4,128)(2,1)S(1)} %get-tuple-element.45), channel_id=1, source_target_pairs={{0,2},{1,3},{2,0},{3,1},{4,6},{5,7},{6,4},{7,5},{8,10},{9,11},{10,... | collective-permute-start | bytes 73736 | tf_op jit(solution)/shard_map/ppermute | solution.py:35
  51.9 5.6 %collective-permute-start.14 = (bf16[4,3072]{1,0:T(4,128)(2,1)S(1)}, bf16[4,3072]{1,0:T(4,128)(2,1)S(1)}, u32[]{:S(2)}, u32[]{:S(2)}) collective-permute-start(bf16[4,3072]{1,0:T(4,128)(2,1)S(1)} %get-tuple-element.46), channel_id=1, source_target_pairs={{0,3},{1,2},{2,1},{3,0},{4,7},{5,6},{6,5},{7,4},{8,11},{9,10},{10,... | collective-permute-start | bytes 73736 | tf_op jit(solution)/shard_map/ppermute | solution.py:35
  57.6 11.0 %collective-permute-start.17 = (bf16[16,3072]{1,0:T(8,128)(2,1)S(1)}, bf16[16,3072]{1,0:T(8,128)(2,1)S(1)}, u32[]{:S(2)}, u32[]{:S(2)}) collective-permute-start(bf16[16,3072]{1,0:T(8,128)(2,1)S(1)} %pad_maximum_fusion.1._.refs_0_), channel_id=1, source_target_pairs={{0,12},{4,8},{8,4},{12,0},{1,13},{5,9},{9,5},{13,1},{2,14},{6,10},... | collective-permute-start | bytes 294920 | tf_op jit(solution)/shard_map/ppermute | solution.py:35
  57.6 10.9 %collective-permute-start.16 = (bf16[16,3072]{1,0:T(8,128)(2,1)S(1)}, bf16[16,3072]{1,0:T(8,128)(2,1)S(1)}, u32[]{:S(2)}, u32[]{:S(2)}) collective-permute-start(bf16[16,3072]{1,0:T(8,128)(2,1)S(1)} %pad_maximum_fusion.1._.refs_0_), channel_id=1, source_target_pairs={{0,8},{4,12},{8,0},{12,4},{1,9},{5,13},{9,1},{13,5},{2,10},{6,14},... | collective-permute-start | bytes 294920 | tf_op jit(solution)/shard_map/ppermute | solution.py:35
  58.6 9.9 %collective-permute-start.15 = (bf16[16,3072]{1,0:T(8,128)(2,1)S(1)}, bf16[16,3072]{1,0:T(8,128)(2,1)S(1)}, u32[]{:S(2)}, u32[]{:S(2)}) collective-permute-start(bf16[16,3072]{1,0:T(8,128)(2,1)S(1)} %pad_maximum_fusion.1._.refs_0_), channel_id=1, source_target_pairs={{0,4},{4,0},{8,12},{12,8},{1,5},{5,1},{9,13},{13,9},{2,6},{6,2},{1... | collective-permute-start | bytes 294920 | tf_op jit(solution)/shard_map/ppermute | solution.py:35
  74.6 8.4 %collective-permute-start.18 = (bf16[16,4608]{1,0:T(8,128)(2,1)S(1)}, bf16[16,4608]{1,0:T(8,128)(2,1)S(1)}, u32[]{:S(2)}, u32[]{:S(2)}) collective-permute-start(bf16[16,4608]{1,0:T(8,128)(2,1)S(1)} %get-tuple-element.50), channel_id=1, source_target_pairs={{0,1},{1,0},{2,3},{3,2},{4,5},{5,4},{6,7},{7,6},{8,9},{9,8},{10,11... | collective-permute-start | bytes 442376 | tf_op jit(solution)/shard_map/ppermute | solution.py:35
  74.7 14.1 %collective-permute-start.19 = (bf16[16,4608]{1,0:T(8,128)(2,1)S(1)}, bf16[16,4608]{1,0:T(8,128)(2,1)S(1)}, u32[]{:S(2)}, u32[]{:S(2)}) collective-permute-start(bf16[16,4608]{1,0:T(8,128)(2,1)S(1)} %get-tuple-element.51), channel_id=1, source_target_pairs={{0,2},{1,3},{2,0},{3,1},{4,6},{5,7},{6,4},{7,5},{8,10},{9,11},{10,... | collective-permute-start | bytes 442376 | tf_op jit(solution)/shard_map/ppermute | solution.py:35
  77.7 11.1 %collective-permute-start.20 = (bf16[16,4608]{1,0:T(8,128)(2,1)S(1)}, bf16[16,4608]{1,0:T(8,128)(2,1)S(1)}, u32[]{:S(2)}, u32[]{:S(2)}) collective-permute-start(bf16[16,4608]{1,0:T(8,128)(2,1)S(1)} %get-tuple-element.52), channel_id=1, source_target_pairs={{0,3},{1,2},{2,1},{3,0},{4,7},{5,6},{6,5},{7,4},{8,11},{9,10},{10,... | collective-permute-start | bytes 442376 | tf_op jit(solution)/shard_map/ppermute | solution.py:35
  (2 other events, 1.8 us)

commit v2 on v1

--- a/solution.py
+++ b/solution.py
@@ -11,18 +11,30 @@
 SMEM = pl.BlockSpec(memory_space=pltpu.SMEM)
 ANY = pl.BlockSpec(memory_space=pl.ANY)
 MIB = 1 << 20
-
-
-def call(body, outs, in_specs, args, limit=8, scratch=(), flops=0, traffic=0):
+NEAR_LAST = (0, 3, 2, 1)
+FAR_LAST = (0, 2, 1, 3)
+
+
+def call(body, outs, in_specs, args, limit=8, scratch=(), flops=0, traffic=0, order=()):
+    order = [*order, *range(len(order), len(args))]
+
+    def ordered(*refs):
+        ins = [refs[order.index(i)] for i in range(len(args))]
+        body(*ins, *refs[len(args) :])
+
     return pl.pallas_call(
-        body,
+        ordered,
         out_shape=outs,
-        in_specs=in_specs,
+        in_specs=[in_specs[i] for i in order],
         out_specs=jax.tree.map(lambda _: VMEM, outs),
         scratch_shapes=scratch,
         compiler_params=pltpu.CompilerParams(vmem_limit_bytes=limit * MIB),
         cost_estimate=pl.CostEstimate(flops=flops, bytes_accessed=traffic, transcendentals=0),
-    )(*args)
+    )(*[args[i] for i in order])
+
+
+def far(x):
+    return pltpu.with_memory_space_constraint(x, pltpu.HBM)
 
 
 def struct(shape, dtype=jnp.bfloat16):
@@ -36,38 +48,27 @@
     ]
 
 
-def norm_body(x_ref, gain_ref, *out_refs):
+def norm_body(x_hbm, gain_hbm, *refs):
+    *out_refs, x_ref, gain_ref, sems = refs
+    copies = [
+        pltpu.make_async_copy(x_hbm, x_ref, sems.at[0]),
+        pltpu.make_async_copy(gain_hbm, gain_ref, sems.at[1]),
+    ]
+    for copy in copies:
+        copy.start()
     block = out_refs[0].shape[1]
     me = lax.axis_index("gx")
+    copies[0].wait()
     x = x_ref[...].astype(jnp.float32)
     mean = jnp.mean(x, axis=1, keepdims=True)
     centered = x - mean
     variance = jnp.mean(centered * centered, axis=1, keepdims=True)
     inverse = 1.0 / jnp.sqrt(variance + 1e-05)
+    copies[1].wait()
     for k, out_ref in enumerate(out_refs):
         columns = pl.ds(pl.multiple_of((me ^ k) * block, 128), block)
         part = x_ref[:, columns].astype(jnp.float32) - mean
         out_ref[...] = (part * inverse * gain_ref[:, columns]).astype(jnp.bfloat16)
-
-
-def load_body(w_ref, _, out_ref, sem):
-    copy = pltpu.make_async_copy(w_ref, out_ref, sem)
-    copy.start()
-    copy.wait()
-
-
-def load(w, after):
-    w, after = lax.optimization_barrier((w, after))
-    size = w.shape[0] * w.shape[1] * 2
-    return pl.pallas_call(
-        load_body,
-        out_shape=pltpu.VMEM(w.shape, w.dtype),
-        in_specs=[ANY, ANY],
-        out_specs=VMEM,
-        scratch_shapes=[pltpu.SemaphoreType.DMA],
-        compiler_params=pltpu.CompilerParams(vmem_limit_bytes=MIB),
-        cost_estimate=pl.CostEstimate(flops=0, bytes_accessed=2 * size, transcendentals=0),
-    )(w, after)
 
 
 def project_body(tile, n, *refs):
@@ -87,7 +88,7 @@
             out[:, columns] = jnp.concatenate(group, axis=0).astype(out.dtype)
 
 
-def project(pieces, w, tile):
+def project(pieces, w, tile, order):
     n = len(pieces)
     rows, width = pieces[0].shape[0], w.shape[1]
     outs = [struct((rows, width), jnp.float32 if k == 0 else jnp.bfloat16) for k in range(n)]
@@ -100,6 +101,7 @@
         limit=12,
         flops=2 * n * rows * w.shape[0] * width,
         traffic=2 * w.shape[0] * width,
+        order=order,
     )
 
 
@@ -113,10 +115,10 @@
         out[...] = total[j * each : (j + 1) * each].astype(jnp.bfloat16)
 
 
-def attend_body(blocks, heads, length_ref, *refs):
-    pieces, (key_ref, value_ref) = refs[:blocks], refs[blocks : blocks + 2]
-    outs = refs[blocks + 2 : 2 * blocks + 2]
-    row_ref, query_ref, mixed_ref = refs[2 * blocks + 2 :]
+def attend_body(blocks, heads, *refs):
+    pieces, (key_ref, value_ref, length_ref) = refs[:blocks], refs[blocks : blocks + 3]
+    outs = refs[blocks + 3 : 2 * blocks + 3]
+    row_ref, query_ref, mixed_ref = refs[2 * blocks + 3 :]
     me = lax.axis_index("yz")
     part = pieces[0].shape[1]
     seqs, slots, head = key_ref.shape
@@ -127,26 +129,33 @@
         query_ref[h] = row_ref[:, h * head : (h + 1) * head]
     slot = lax.broadcasted_iota(jnp.int32, (1, slots), 1)
     width = heads * head
-    for s in range(seqs):
-        query = query_ref[:, s, :]
-        key_new = row_ref[s : s + 1, width : width + head]
-        value_new = row_ref[s : s + 1, width + head : width + 2 * head]
-        own = jnp.sum(query * key_new, axis=1, keepdims=True) * scale
-        scores = lax.dot_general(
-            query.astype(jnp.bfloat16),
+    queries = [query_ref[:, s, :] for s in range(seqs)]
+    owns = [
+        jnp.sum(queries[s] * row_ref[s : s + 1, width : width + head], axis=1, keepdims=True) * scale
+        for s in range(seqs)
+    ]
+    scores = [
+        lax.dot_general(
+            queries[s].astype(jnp.bfloat16),
             key_ref[s],
             (((1,), (1,)), ((), ())),
             preferred_element_type=jnp.float32,
         )
-        masked = jnp.where(slot < length_ref[s], scores * scale, -jnp.inf)
-        top = jnp.maximum(jnp.max(masked, axis=1, keepdims=True), own)
-        weights = jnp.exp(masked - top)
-        own_weight = jnp.exp(own - top)
-        total = jnp.sum(weights, axis=1, keepdims=True) + own_weight
-        probs = (weights / total).astype(jnp.bfloat16)
-        own_prob = (own_weight / total).astype(jnp.bfloat16).astype(jnp.float32)
-        mixed = jnp.dot(probs, value_ref[s], preferred_element_type=jnp.float32)
-        mixed_ref[:, s, :] = mixed + own_prob * value_new
+        for s in range(seqs)
+    ]
+    masked = [jnp.where(slot < length_ref[s], scores[s] * scale, -jnp.inf) for s in range(seqs)]
+    tops = [jnp.maximum(jnp.max(masked[s], axis=1, keepdims=True), owns[s]) for s in range(seqs)]
+    weights = [jnp.exp(masked[s] - tops[s]) for s in range(seqs)]
+    own_weights = [jnp.exp(owns[s] - tops[s]) for s in range(seqs)]
+    totals = [jnp.sum(weights[s], axis=1, keepdims=True) + own_weights[s] for s in range(seqs)]
+    probs = [(weights[s] / totals[s]).astype(jnp.bfloat16) for s in range(seqs)]
+    mixed = [
+        jnp.dot(probs[s], value_ref[s], preferred_element_type=jnp.float32) for s in range(seqs)
+    ]
+    for s in range(seqs):
+        own_prob = (own_weights[s] / totals[s]).astype(jnp.bfloat16).astype(jnp.float32)
+        value_new = row_ref[s : s + 1, width + head : width + 2 * head]
+        mixed_ref[:, s, :] = mixed[s] + own_prob * value_new
     each = heads // blocks
     for j, out in enumerate(outs):
         first = (me ^ j) * each
@@ -162,17 +171,22 @@
     return call(
         functools.partial(attend_body, blocks, heads),
         [struct((seqs, width // blocks))] * blocks,
-        [SMEM] + [VMEM] * (blocks + 2),
-        [cache_lengths, *pieces, keys, values],
+        [VMEM] * (blocks + 2) + [SMEM],
+        [*pieces, keys, values, cache_lengths],
+        order=NEAR_LAST,
         limit=12,
         scratch=[
             pltpu.VMEM((seqs, width + 2 * head), jnp.float32),
             pltpu.VMEM((heads, seqs, head), jnp.float32),
             pltpu.VMEM((heads, seqs, head), jnp.float32),
         ],
-        flops=4 * seqs * heads * head * slots,
+        flops=50_000_000_000,
         traffic=4 * seqs * slots * head,
     )
+
+
+def join_body(*refs):
+    refs[-1][...] = jnp.concatenate([r[...] for r in refs[:-1]], axis=0)
 
 
 def place_body(n, *refs):
@@ -193,26 +207,32 @@
     normed = call(
         norm_body,
         [struct((seqs, depth))] * groups,
-        [VMEM, VMEM],
-        [tokens, gain.reshape(1, -1)],
-    )
-    mine = jnp.concatenate(exchange(normed, "gx"), axis=0)
-    w_near = load(w_qkv, mine)
+        [ANY, ANY],
+        [far(tokens), far(gain.reshape(1, -1))],
+        scratch=[
+            pltpu.VMEM(tokens.shape, tokens.dtype),
+            pltpu.VMEM((1, gain.shape[0]), gain.dtype),
+            pltpu.SemaphoreType.DMA((2,)),
+        ],
+        flops=50_000_000_000,
+    )
+    mine = call(join_body, struct((groups * seqs, depth)), [VMEM] * groups, exchange(normed, "gx"), order=NEAR_LAST)
     pieces = exchange([mine] * blocks, "yz")
-    sums = exchange(project(pieces, w_near, 640), "gx")
+    sums = exchange(project(pieces, w_qkv, w_qkv.shape[1], FAR_LAST), "gx")
     parts = call(
-        total_body, [struct((seqs, w_qkv.shape[1]))] * blocks, [VMEM] * groups, sums
+        total_body, [struct((seqs, w_qkv.shape[1]))] * blocks, [VMEM] * groups, sums, order=NEAR_LAST
     )
     attended = attend(exchange(parts, "yz"), cache_keys, cache_values, cache_lengths, width)
-    mine = jnp.concatenate(exchange(attended, "yz"), axis=0)
-    w_near = load(w_out, mine)
+    got = exchange(attended, "yz")
+    mine = call(join_body, struct((4 * seqs, got[0].shape[1])), [VMEM] * 4, got, flops=50_000_000_000, order=NEAR_LAST)
     pieces = exchange([mine] * groups, "gx")
-    sums = exchange(project(pieces, w_near, 512), "yz")
+    sums = exchange(project(pieces, w_out, w_out.shape[1], NEAR_LAST), "yz")
     return call(
         functools.partial(place_body, blocks),
         struct((groups, seqs, w_out.shape[1])),
         [VMEM] * blocks,
         sums,
+        order=FAR_LAST,
     )
 
 

time: 89.8 us -> 80.2 us (0.89)
  Pallas kernels: 34.3 us -> 14.5 us
  waiting for transfers between devices: 28.3 us -> 40.5 us
  local copies, waits for them, and re-layouts: 1.81 us -> 0.06 us
    pallas_call x8, Pallas kernels: 34.3 us -> 14.5 us  [call(): pl.pallas_call(ordered, out_shape=outs, in_specs=[in_specs[i] for i in or...]
    ppermute x21, waiting for transfers between devices: 28.3 us -> 40.5 us  [exchange(): lax.ppermute(pieces[k], axis, [(i, i ^ k) for i in range(size)])]
    unnamed x10 -> x22, local copies, waits for them, and re-layouts: 1.81 us -> 0.06 us
  transfers between devices with their start and end apart: 21 -> 21, of which waited for: 11 -> 16; matrix products, arithmetic and copies ran while one was open for 0% -> 0% of each run, Pallas kernels for 21% -> 0%
where the time goes in v2:
time: 80.2 us; the launch traced here: 80 us
  waiting for transfers between devices  40.5 us (50%)
  starting transfers between devices  24.8 us (31%)
  Pallas kernels  14.5 us (18%)
    ppermute x21, waiting for transfers between devices, exchange(): lax.ppermute(pieces[k], axis, [(i, i ^ k) for i in range(size)])  40.5 us
    ppermute x21, starting transfers between devices, exchange(): lax.ppermute(pieces[k], axis, [(i, i ^ k) for i in range(size)])  24.8 us
    pallas_call x8, Pallas kernels, call(): pl.pallas_call(ordered, out_shape=outs, in_specs=[in_specs[i] for i in or...  14.5 us
  transfers between devices with their start and end apart: 21, of which 16 were waited for; matrix products, arithmetic and copies ran while one was open for 0% of the time, Pallas kernels for 0%

profile of v2, /device:TPU:0, one launch (start us, length us, event | category | flops | bytes accessed | tf_op | source)
XLA Modules:
  0.0 80.0 jit_solution(3688428508031517148)
XLA Ops:
  0.0 1.6 %shard_map.73 = (bf16[4,4608]{1,0:T(4,128)(2,1)S(1)}, bf16[4,4608]{1,0:T(4,128)(2,1)S(1)}, bf16[4,4608]{1,0:T(4,128)(2,1)S(1)}, bf16[4,4608]{1,0:T(4,128)(2,1)S(1)}) custom-call(bf16[4,18432]{1,0:T(4,128)(2,1)} %refs_0_.1, f32[1,18432]{1,0:T(1,128)} %bitcast.3), custom_call_target="tpu_custom_call" | custom-call | flops 49999998976 | tf_op jit(solution)/shard_map/pallas_call | solution.py:25
  1.7 2.4 %collective-permute-start = (bf16[4,4608]{1,0:T(4,128)(2,1)S(1)}, bf16[4,4608]{1,0:T(4,128)(2,1)S(1)}, u32[]{:S(2)}, u32[]{:S(2)}) collective-permute-start(bf16[4,4608]{1,0:T(4,128)(2,1)S(1)} %get-tuple-element.26), channel_id=1, source_target_pairs={{0,12},{4,8},{8,4},{12,0},{1,13},{5,9},{9,5},{13,1},{2,14},{6,10},... | collective-permute-start | bytes 110600 | tf_op jit(solution)/shard_map/ppermute | solution.py:47
  6.0 2.2 %collective-permute-done.1.refs_2_ = bf16[4,4608]{1,0:T(4,128)(2,1)S(1)} collective-permute-done((bf16[4,4608]{1,0:T(4,128)(2,1)S(1)}, bf16[4,4608]{1,0:T(4,128)(2,1)S(1)}, u32[]{:S(2)}, u32[]{:S(2)}) %collective-permute-start.1) | collective-permute-done | bytes 36896 | tf_op jit(solution)/shard_map/ppermute | solution.py:47
  8.2 3.7 %collective-permute-start.5 = (bf16[16,4608]{1,0:T(8,128)(2,1)S(1)}, bf16[16,4608]{1,0:T(8,128)(2,1)S(1)}, u32[]{:S(2)}, u32[]{:S(2)}) collective-permute-start(bf16[16,4608]{1,0:T(8,128)(2,1)S(1)} %shard_map.74.refs_0_), channel_id=1, source_target_pairs={{0,3},{1,2},{2,1},{3,0},{4,7},{5,6},{6,5},{7,4},{8,11},{9,10},{10,... | collective-permute-start | bytes 442376 | tf_op jit(solution)/shard_map/ppermute | solution.py:47
  12.7 4.1 %collective-permute-done.5.refs_3_ = bf16[16,4608]{1,0:T(8,128)(2,1)S(1)} collective-permute-done((bf16[16,4608]{1,0:T(8,128)(2,1)S(1)}, bf16[16,4608]{1,0:T(8,128)(2,1)S(1)}, u32[]{:S(2)}, u32[]{:S(2)}) %collective-permute-start.5) | collective-permute-done | bytes 147488 | tf_op jit(solution)/shard_map/ppermute | solution.py:47
  16.8 3.1 %collective-permute-done.4.refs_2_ = bf16[16,4608]{1,0:T(8,128)(2,1)S(1)} collective-permute-done((bf16[16,4608]{1,0:T(8,128)(2,1)S(1)}, bf16[16,4608]{1,0:T(8,128)(2,1)S(1)}, u32[]{:S(2)}, u32[]{:S(2)}) %collective-permute-start.4) | collective-permute-done | bytes 147488 | tf_op jit(solution)/shard_map/ppermute | solution.py:47
  19.9 4.5 %collective-permute-done.3.refs_1_ = bf16[16,4608]{1,0:T(8,128)(2,1)S(1)} collective-permute-done((bf16[16,4608]{1,0:T(8,128)(2,1)S(1)}, bf16[16,4608]{1,0:T(8,128)(2,1)S(1)}, u32[]{:S(2)}, u32[]{:S(2)}) %collective-permute-start.3) | collective-permute-done | bytes 147488 | tf_op jit(solution)/shard_map/ppermute | solution.py:47
  24.4 5.2 %shard_map.75 = (f32[16,3200]{1,0:T(8,128)S(1)}, bf16[16,3200]{1,0:T(8,128)(2,1)S(1)}, bf16[16,3200]{1,0:T(8,128)(2,1)S(1)}, bf16[16,3200]{1,0:T(8,128)(2,1)S(1)}) custom-call(bf16[16,4608]{1,0:T(8,128)(2,1)S(1)} %shard_map.74.refs_0_, bf16[16,4608]{1,0:T(8,128)(2,1)S(1)} %collective-permute-done.3.refs_1_, ...), custom_call_target="tpu_custom_call" | custom-call | flops 1887436800 | bytes 29491200 | tf_op jit(solution)/shard_map/pallas_call | solution.py:25
  31.5 3.3 %collective-permute-done.6.refs_1_ = bf16[16,3200]{1,0:T(8,128)(2,1)S(1)} collective-permute-done((bf16[16,3200]{1,0:T(8,128)(2,1)S(1)}, bf16[16,3200]{1,0:T(8,128)(2,1)S(1)}, u32[]{:S(2)}, u32[]{:S(2)}) %collective-permute-start.6) | collective-permute-done | bytes 102432 | tf_op jit(solution)/shard_map/ppermute | solution.py:47
  34.8 2.0 %collective-permute-done.7.refs_2_ = bf16[16,3200]{1,0:T(8,128)(2,1)S(1)} collective-permute-done((bf16[16,3200]{1,0:T(8,128)(2,1)S(1)}, bf16[16,3200]{1,0:T(8,128)(2,1)S(1)}, u32[]{:S(2)}, u32[]{:S(2)}) %collective-permute-start.7) | collective-permute-done | bytes 102432 | tf_op jit(solution)/shard_map/ppermute | solution.py:47
  36.9 2.5 %collective-permute-start.9 = (bf16[4,3200]{1,0:T(4,128)(2,1)S(1)}, bf16[4,3200]{1,0:T(4,128)(2,1)S(1)}, u32[]{:S(2)}, u32[]{:S(2)}) collective-permute-start(bf16[4,3200]{1,0:T(4,128)(2,1)S(1)} %get-tuple-element.34), channel_id=1, source_target_pairs={{0,3},{1,2},{2,1},{3,0},{4,7},{5,6},{6,5},{7,4},{8,11},{9,10},{10,... | collective-permute-start | bytes 76808 | tf_op jit(solution)/shard_map/ppermute | solution.py:47
  39.4 1.9 %collective-permute-start.11 = (bf16[4,3200]{1,0:T(4,128)(2,1)S(1)}, bf16[4,3200]{1,0:T(4,128)(2,1)S(1)}, u32[]{:S(2)}, u32[]{:S(2)}) collective-permute-start(bf16[4,3200]{1,0:T(4,128)(2,1)S(1)} %get-tuple-element.36), channel_id=1, source_target_pairs={{0,1},{1,0},{2,3},{3,2},{4,5},{5,4},{6,7},{7,6},{8,9},{9,8},{10,11... | collective-permute-start | bytes 76808 | tf_op jit(solution)/shard_map/ppermute | solution.py:47
  41.3 1.2 %collective-permute-done.9.refs_1_ = bf16[4,3200]{1,0:T(4,128)(2,1)S(1)} collective-permute-done((bf16[4,3200]{1,0:T(4,128)(2,1)S(1)}, bf16[4,3200]{1,0:T(4,128)(2,1)S(1)}, u32[]{:S(2)}, u32[]{:S(2)}) %collective-permute-start.9) | collective-permute-done | bytes 25632 | tf_op jit(solution)/shard_map/ppermute | solution.py:47
  42.6 1.6 %collective-permute-done.10.refs_2_ = bf16[4,3200]{1,0:T(4,128)(2,1)S(1)} collective-permute-done((bf16[4,3200]{1,0:T(4,128)(2,1)S(1)}, bf16[4,3200]{1,0:T(4,128)(2,1)S(1)}, u32[]{:S(2)}, u32[]{:S(2)}) %collective-permute-start.10) | collective-permute-done | bytes 25632 | tf_op jit(solution)/shard_map/ppermute | solution.py:47
  44.2 1.9 %shard_map.77 = (bf16[4,3072]{1,0:T(4,128)(2,1)S(1)}, bf16[4,3072]{1,0:T(4,128)(2,1)S(1)}, bf16[4,3072]{1,0:T(4,128)(2,1)S(1)}, bf16[4,3072]{1,0:T(4,128)(2,1)S(1)}) custom-call(bf16[4,3200]{1,0:T(4,128)(2,1)S(1)} %get-tuple-element.33.refs_0_, bf16[4,3200]{1,0:T(4,128)(2,1)S(1)} %collective-permute-done.9.refs_1_, ...), custom_call_target="tpu_custom_call" | custom-call | flops 49999998976 | bytes 4194304 | tf_op jit(solution)/shard_map/pallas_call | solution.py:25
  46.1 1.7 %collective-permute-start.12 = (bf16[4,3072]{1,0:T(4,128)(2,1)S(1)}, bf16[4,3072]{1,0:T(4,128)(2,1)S(1)}, u32[]{:S(2)}, u32[]{:S(2)}) collective-permute-start(bf16[4,3072]{1,0:T(4,128)(2,1)S(1)} %get-tuple-element.38), channel_id=1, source_target_pairs={{0,3},{1,2},{2,1},{3,0},{4,7},{5,6},{6,5},{7,4},{8,11},{9,10},{10,... | collective-permute-start | bytes 73736 | tf_op jit(solution)/shard_map/ppermute | solution.py:47
  48.6 1.9 %collective-permute-start.14 = (bf16[4,3072]{1,0:T(4,128)(2,1)S(1)}, bf16[4,3072]{1,0:T(4,128)(2,1)S(1)}, u32[]{:S(2)}, u32[]{:S(2)}) collective-permute-start(bf16[4,3072]{1,0:T(4,128)(2,1)S(1)} %get-tuple-element.40), channel_id=1, source_target_pairs={{0,1},{1,0},{2,3},{3,2},{4,5},{5,4},{6,7},{7,6},{8,9},{9,8},{10,11... | collective-permute-start | bytes 73736 | tf_op jit(solution)/shard_map/ppermute | solution.py:47
  50.5 1.2 %collective-permute-done.12.refs_1_ = bf16[4,3072]{1,0:T(4,128)(2,1)S(1)} collective-permute-done((bf16[4,3072]{1,0:T(4,128)(2,1)S(1)}, bf16[4,3072]{1,0:T(4,128)(2,1)S(1)}, u32[]{:S(2)}, u32[]{:S(2)}) %collective-permute-start.12) | collective-permute-done | bytes 24608 | tf_op jit(solution)/shard_map/ppermute | solution.py:47
  54.7 3.8 %collective-permute-done.16.refs_2_ = bf16[16,3072]{1,0:T(8,128)(2,1)S(1)} collective-permute-done((bf16[16,3072]{1,0:T(8,128)(2,1)S(1)}, bf16[16,3072]{1,0:T(8,128)(2,1)S(1)}, u32[]{:S(2)}, u32[]{:S(2)}) %collective-permute-start.16) | collective-permute-done | bytes 98336 | tf_op jit(solution)/shard_map/ppermute | solution.py:47
  59.8 5.0 %shard_map.79 = (f32[16,4608]{1,0:T(8,128)S(1)}, bf16[16,4608]{1,0:T(8,128)(2,1)S(1)}, bf16[16,4608]{1,0:T(8,128)(2,1)S(1)}, bf16[16,4608]{1,0:T(8,128)(2,1)S(1)}) custom-call(bf16[16,3072]{1,0:T(8,128)(2,1)S(1)} %shard_map.78.refs_0_, bf16[16,3072]{1,0:T(8,128)(2,1)S(1)} %collective-permute-done.15.refs_1_, ...), custom_call_target="tpu_custom_call" | custom-call | flops 1811939328 | bytes 28311552 | tf_op jit(solution)/shard_map/pallas_call | solution.py:25
  64.7 1.9 %collective-permute-start.18 = (bf16[16,4608]{1,0:T(8,128)(2,1)S(1)}, bf16[16,4608]{1,0:T(8,128)(2,1)S(1)}, u32[]{:S(2)}, u32[]{:S(2)}) collective-permute-start(bf16[16,4608]{1,0:T(8,128)(2,1)S(1)} %get-tuple-element.42), channel_id=1, source_target_pairs={{0,2},{1,3},{2,0},{3,1},{4,6},{5,7},{6,4},{7,5},{8,10},{9,11},{10,... | collective-permute-start | bytes 442376 | tf_op jit(solution)/shard_map/ppermute | solution.py:47
  67.6 1.6 %collective-permute-start.20 = (bf16[16,4608]{1,0:T(8,128)(2,1)S(1)}, bf16[16,4608]{1,0:T(8,128)(2,1)S(1)}, u32[]{:S(2)}, u32[]{:S(2)}) collective-permute-start(bf16[16,4608]{1,0:T(8,128)(2,1)S(1)} %get-tuple-element.44), channel_id=1, source_target_pairs={{0,3},{1,2},{2,1},{3,0},{4,7},{5,6},{6,5},{7,4},{8,11},{9,10},{10,... | collective-permute-start | bytes 442376 | tf_op jit(solution)/shard_map/ppermute | solution.py:47
  69.2 6.5 %collective-permute-done.18.refs_1_ = bf16[16,4608]{1,0:T(8,128)(2,1)S(1)} collective-permute-done((bf16[16,4608]{1,0:T(8,128)(2,1)S(1)}, bf16[16,4608]{1,0:T(8,128)(2,1)S(1)}, u32[]{:S(2)}, u32[]{:S(2)}) %collective-permute-start.18) | collective-permute-done | bytes 147488 | tf_op jit(solution)/shard_map/ppermute | solution.py:47
  75.7 3.6 %collective-permute-done.20.refs_3_ = bf16[16,4608]{1,0:T(8,128)(2,1)S(1)} collective-permute-done((bf16[16,4608]{1,0:T(8,128)(2,1)S(1)}, bf16[16,4608]{1,0:T(8,128)(2,1)S(1)}, u32[]{:S(2)}, u32[]{:S(2)}) %collective-permute-start.20) | collective-permute-done | bytes 147488 | tf_op jit(solution)/shard_map/ppermute | solution.py:47
  (49 shorter events, 11.4 us)
Async XLA Ops:
  1.7 42.5 %copy-start.1 = (bf16[4,1024,256]{2,1,0:T(8,128)(2,1)S(1)}, bf16[4,1024,256]{2,1,0:T(8,128)(2,1)}, u32[]{:S(2)}) copy-start(bf16[4,1024,256]{2,1,0:T(8,128)(2,1)} %refs_4_.4) | copy-start | bytes 6291460
  1.7 42.5 %copy-start.2 = (bf16[4,1024,256]{2,1,0:T(8,128)(2,1)S(1)}, bf16[4,1024,256]{2,1,0:T(8,128)(2,1)}, u32[]{:S(2)}) copy-start(bf16[4,1024,256]{2,1,0:T(8,128)(2,1)} %refs_5_.1) | copy-start | bytes 6291460
  1.7 42.5 %copy-start.3 = (s32[4]{0:T(128)S(1)}, s32[4]{0:T(128)}, u32[]{:S(2)}) copy-start(s32[4]{0:T(128)} %refs_6_.1) | copy-start | bytes 52
  1.7 4.3 %collective-permute-start = (bf16[4,4608]{1,0:T(4,128)(2,1)S(1)}, bf16[4,4608]{1,0:T(4,128)(2,1)S(1)}, u32[]{:S(2)}, u32[]{:S(2)}) collective-permute-start(bf16[4,4608]{1,0:T(4,128)(2,1)S(1)} %get-tuple-element.26), channel_id=1, source_target_pairs={{0,12},{4,8},{8,4},{12,0},{1,13},{5,9},{9,5},{13,1},{2,14},{6,10},... | collective-permute-start | bytes 110600 | tf_op jit(solution)/shard_map/ppermute | solution.py:47
  4.1 4.1 %collective-permute-start.1 = (bf16[4,4608]{1,0:T(4,128)(2,1)S(1)}, bf16[4,4608]{1,0:T(4,128)(2,1)S(1)}, u32[]{:S(2)}, u32[]{:S(2)}) collective-permute-start(bf16[4,4608]{1,0:T(4,128)(2,1)S(1)} %get-tuple-element.27), channel_id=1, source_target_pairs={{0,8},{4,12},{8,0},{12,4},{1,9},{5,13},{9,1},{13,5},{2,10},{6,14},... | collective-permute-start | bytes 110600 | tf_op jit(solution)/shard_map/ppermute | solution.py:47
  4.8 3.4 %collective-permute-start.2 = (bf16[4,4608]{1,0:T(4,128)(2,1)S(1)}, bf16[4,4608]{1,0:T(4,128)(2,1)S(1)}, u32[]{:S(2)}, u32[]{:S(2)}) collective-permute-start(bf16[4,4608]{1,0:T(4,128)(2,1)S(1)} %get-tuple-element.28), channel_id=1, source_target_pairs={{0,4},{4,0},{8,12},{12,8},{1,5},{5,1},{9,13},{13,9},{2,6},{6,2},{1... | collective-permute-start | bytes 110600 | tf_op jit(solution)/shard_map/ppermute | solution.py:47
  8.2 8.6 %collective-permute-start.5 = (bf16[16,4608]{1,0:T(8,128)(2,1)S(1)}, bf16[16,4608]{1,0:T(8,128)(2,1)S(1)}, u32[]{:S(2)}, u32[]{:S(2)}) collective-permute-start(bf16[16,4608]{1,0:T(8,128)(2,1)S(1)} %shard_map.74.refs_0_), channel_id=1, source_target_pairs={{0,3},{1,2},{2,1},{3,0},{4,7},{5,6},{6,5},{7,4},{8,11},{9,10},{10,... | collective-permute-start | bytes 442376 | tf_op jit(solution)/shard_map/ppermute | solution.py:47
  11.9 8.0 %collective-permute-start.4 = (bf16[16,4608]{1,0:T(8,128)(2,1)S(1)}, bf16[16,4608]{1,0:T(8,128)(2,1)S(1)}, u32[]{:S(2)}, u32[]{:S(2)}) collective-permute-start(bf16[16,4608]{1,0:T(8,128)(2,1)S(1)} %shard_map.74.refs_0_), channel_id=1, source_target_pairs={{0,1},{1,0},{2,3},{3,2},{4,5},{5,4},{6,7},{7,6},{8,9},{9,8},{10,11... | collective-permute-start | bytes 442376 | tf_op jit(solution)/shard_map/ppermute | solution.py:47
  11.9 12.5 %collective-permute-start.3 = (bf16[16,4608]{1,0:T(8,128)(2,1)S(1)}, bf16[16,4608]{1,0:T(8,128)(2,1)S(1)}, u32[]{:S(2)}, u32[]{:S(2)}) collective-permute-start(bf16[16,4608]{1,0:T(8,128)(2,1)S(1)} %shard_map.74.refs_0_), channel_id=1, source_target_pairs={{0,2},{1,3},{2,0},{3,1},{4,6},{5,7},{6,4},{7,5},{8,10},{9,11},{10,... | collective-permute-start | bytes 442376 | tf_op jit(solution)/shard_map/ppermute | solution.py:47
  29.6 5.2 %collective-permute-start.6 = (bf16[16,3200]{1,0:T(8,128)(2,1)S(1)}, bf16[16,3200]{1,0:T(8,128)(2,1)S(1)}, u32[]{:S(2)}, u32[]{:S(2)}) collective-permute-start(bf16[16,3200]{1,0:T(8,128)(2,1)S(1)} %get-tuple-element.30), channel_id=1, source_target_pairs={{0,12},{4,8},{8,4},{12,0},{1,13},{5,9},{9,5},{13,1},{2,14},{6,10},... | collective-permute-start | bytes 307208 | tf_op jit(solution)/shard_map/ppermute | solution.py:47
  29.9 6.9 %collective-permute-start.7 = (bf16[16,3200]{1,0:T(8,128)(2,1)S(1)}, bf16[16,3200]{1,0:T(8,128)(2,1)S(1)}, u32[]{:S(2)}, u32[]{:S(2)}) collective-permute-start(bf16[16,3200]{1,0:T(8,128)(2,1)S(1)} %get-tuple-element.31), channel_id=1, source_target_pairs={{0,8},{4,12},{8,0},{12,4},{1,9},{5,13},{9,1},{13,5},{2,10},{6,14},... | collective-permute-start | bytes 307208 | tf_op jit(solution)/shard_map/ppermute | solution.py:47
  31.1 5.8 %collective-permute-start.8 = (bf16[16,3200]{1,0:T(8,128)(2,1)S(1)}, bf16[16,3200]{1,0:T(8,128)(2,1)S(1)}, u32[]{:S(2)}, u32[]{:S(2)}) collective-permute-start(bf16[16,3200]{1,0:T(8,128)(2,1)S(1)} %get-tuple-element.32), channel_id=1, source_target_pairs={{0,4},{4,0},{8,12},{12,8},{1,5},{5,1},{9,13},{13,9},{2,6},{6,2},{1... | collective-permute-start | bytes 307208 | tf_op jit(solution)/shard_map/ppermute | solution.py:47
  36.9 5.7 %collective-permute-start.9 = (bf16[4,3200]{1,0:T(4,128)(2,1)S(1)}, bf16[4,3200]{1,0:T(4,128)(2,1)S(1)}, u32[]{:S(2)}, u32[]{:S(2)}) collective-permute-start(bf16[4,3200]{1,0:T(4,128)(2,1)S(1)} %get-tuple-element.34), channel_id=1, source_target_pairs={{0,3},{1,2},{2,1},{3,0},{4,7},{5,6},{6,5},{7,4},{8,11},{9,10},{10,... | collective-permute-start | bytes 76808 | tf_op jit(solution)/shard_map/ppermute | solution.py:47
  39.4 4.7 %collective-permute-start.10 = (bf16[4,3200]{1,0:T(4,128)(2,1)S(1)}, bf16[4,3200]{1,0:T(4,128)(2,1)S(1)}, u32[]{:S(2)}, u32[]{:S(2)}) collective-permute-start(bf16[4,3200]{1,0:T(4,128)(2,1)S(1)} %get-tuple-element.35), channel_id=1, source_target_pairs={{0,2},{1,3},{2,0},{3,1},{4,6},{5,7},{6,4},{7,5},{8,10},{9,11},{10,... | collective-permute-start | bytes 76808 | tf_op jit(solution)/shard_map/ppermute | solution.py:47
  39.4 4.7 %collective-permute-start.11 = (bf16[4,3200]{1,0:T(4,128)(2,1)S(1)}, bf16[4,3200]{1,0:T(4,128)(2,1)S(1)}, u32[]{:S(2)}, u32[]{:S(2)}) collective-permute-start(bf16[4,3200]{1,0:T(4,128)(2,1)S(1)} %get-tuple-element.36), channel_id=1, source_target_pairs={{0,1},{1,0},{2,3},{3,2},{4,5},{5,4},{6,7},{7,6},{8,9},{9,8},{10,11... | collective-permute-start | bytes 76808 | tf_op jit(solution)/shard_map/ppermute | solution.py:47
  46.1 5.7 %collective-permute-start.12 = (bf16[4,3072]{1,0:T(4,128)(2,1)S(1)}, bf16[4,3072]{1,0:T(4,128)(2,1)S(1)}, u32[]{:S(2)}, u32[]{:S(2)}) collective-permute-start(bf16[4,3072]{1,0:T(4,128)(2,1)S(1)} %get-tuple-element.38), channel_id=1, source_target_pairs={{0,3},{1,2},{2,1},{3,0},{4,7},{5,6},{6,5},{7,4},{8,11},{9,10},{10,... | collective-permute-start | bytes 73736 | tf_op jit(solution)/shard_map/ppermute | solution.py:47
  47.8 4.8 %collective-permute-start.13 = (bf16[4,3072]{1,0:T(4,128)(2,1)S(1)}, bf16[4,3072]{1,0:T(4,128)(2,1)S(1)}, u32[]{:S(2)}, u32[]{:S(2)}) collective-permute-start(bf16[4,3072]{1,0:T(4,128)(2,1)S(1)} %get-tuple-element.39), channel_id=1, source_target_pairs={{0,2},{1,3},{2,0},{3,1},{4,6},{5,7},{6,4},{7,5},{8,10},{9,11},{10,... | collective-permute-start | bytes 73736 | tf_op jit(solution)/shard_map/ppermute | solution.py:47
  48.6 4.1 %collective-permute-start.14 = (bf16[4,3072]{1,0:T(4,128)(2,1)S(1)}, bf16[4,3072]{1,0:T(4,128)(2,1)S(1)}, u32[]{:S(2)}, u32[]{:S(2)}) collective-permute-start(bf16[4,3072]{1,0:T(4,128)(2,1)S(1)} %get-tuple-element.40), channel_id=1, source_target_pairs={{0,1},{1,0},{2,3},{3,2},{4,5},{5,4},{6,7},{7,6},{8,9},{9,8},{10,11... | collective-permute-start | bytes 73736 | tf_op jit(solution)/shard_map/ppermute | solution.py:47
  52.8 1.9 %collective-permute-start.17 = (bf16[16,3072]{1,0:T(8,128)(2,1)S(1)}, bf16[16,3072]{1,0:T(8,128)(2,1)S(1)}, u32[]{:S(2)}, u32[]{:S(2)}) collective-permute-start(bf16[16,3072]{1,0:T(8,128)(2,1)S(1)} %shard_map.78.refs_0_), channel_id=1, source_target_pairs={{0,4},{4,0},{8,12},{12,8},{1,5},{5,1},{9,13},{13,9},{2,6},{6,2},{1... | collective-permute-start | bytes 294920 | tf_op jit(solution)/shard_map/ppermute | solution.py:47
  52.8 5.7 %collective-permute-start.16 = (bf16[16,3072]{1,0:T(8,128)(2,1)S(1)}, bf16[16,3072]{1,0:T(8,128)(2,1)S(1)}, u32[]{:S(2)}, u32[]{:S(2)}) collective-permute-start(bf16[16,3072]{1,0:T(8,128)(2,1)S(1)} %shard_map.78.refs_0_), channel_id=1, source_target_pairs={{0,8},{4,12},{8,0},{12,4},{1,9},{5,13},{9,1},{13,5},{2,10},{6,14},... | collective-permute-start | bytes 294920 | tf_op jit(solution)/shard_map/ppermute | solution.py:47
  53.7 6.0 %collective-permute-start.15 = (bf16[16,3072]{1,0:T(8,128)(2,1)S(1)}, bf16[16,3072]{1,0:T(8,128)(2,1)S(1)}, u32[]{:S(2)}, u32[]{:S(2)}) collective-permute-start(bf16[16,3072]{1,0:T(8,128)(2,1)S(1)} %shard_map.78.refs_0_), channel_id=1, source_target_pairs={{0,12},{4,8},{8,4},{12,0},{1,13},{5,9},{9,5},{13,1},{2,14},{6,10},... | collective-permute-start | bytes 294920 | tf_op jit(solution)/shard_map/ppermute | solution.py:47
  64.7 11.0 %collective-permute-start.18 = (bf16[16,4608]{1,0:T(8,128)(2,1)S(1)}, bf16[16,4608]{1,0:T(8,128)(2,1)S(1)}, u32[]{:S(2)}, u32[]{:S(2)}) collective-permute-start(bf16[16,4608]{1,0:T(8,128)(2,1)S(1)} %get-tuple-element.42), channel_id=1, source_target_pairs={{0,2},{1,3},{2,0},{3,1},{4,6},{5,7},{6,4},{7,5},{8,10},{9,11},{10,... | collective-permute-start | bytes 442376 | tf_op jit(solution)/shard_map/ppermute | solution.py:47
  66.7 9.0 %collective-permute-start.19 = (bf16[16,4608]{1,0:T(8,128)(2,1)S(1)}, bf16[16,4608]{1,0:T(8,128)(2,1)S(1)}, u32[]{:S(2)}, u32[]{:S(2)}) collective-permute-start(bf16[16,4608]{1,0:T(8,128)(2,1)S(1)} %get-tuple-element.43), channel_id=1, source_target_pairs={{0,1},{1,0},{2,3},{3,2},{4,5},{5,4},{6,7},{7,6},{8,9},{9,8},{10,11... | collective-permute-start | bytes 442376 | tf_op jit(solution)/shard_map/ppermute | solution.py:47
  67.6 11.7 %collective-permute-start.20 = (bf16[16,4608]{1,0:T(8,128)(2,1)S(1)}, bf16[16,4608]{1,0:T(8,128)(2,1)S(1)}, u32[]{:S(2)}, u32[]{:S(2)}) collective-permute-start(bf16[16,4608]{1,0:T(8,128)(2,1)S(1)} %get-tuple-element.44), channel_id=1, source_target_pairs={{0,3},{1,2},{2,1},{3,0},{4,7},{5,6},{6,5},{7,4},{8,11},{9,10},{10,... | collective-permute-start | bytes 442376 | tf_op jit(solution)/shard_map/ppermute | solution.py:47
  (8 other events, 107.5 us)

commit v3 on v2

--- a/solution.py
+++ b/solution.py
@@ -11,8 +11,13 @@
 SMEM = pl.BlockSpec(memory_space=pltpu.SMEM)
 ANY = pl.BlockSpec(memory_space=pl.ANY)
 MIB = 1 << 20
-NEAR_LAST = (0, 3, 2, 1)
-FAR_LAST = (0, 2, 1, 3)
+A1 = (0, 1, 3, 2)
+A2 = (0, 1, 2, 3, 4, 5)
+B1 = (0, 2, 1, 3)
+B2 = (0, 2, 3, 1)
+C1 = (0, 3, 2, 1)
+C2 = (0, 1, 2, 3)
+D = (0, 2, 1, 3)
 
 
 def call(body, outs, in_specs, args, limit=8, scratch=(), flops=0, traffic=0, order=()):
@@ -33,6 +38,10 @@
     )(*[args[i] for i in order])
 
 
+def near(x):
+    return pltpu.with_memory_space_constraint(x, pltpu.VMEM)
+
+
 def far(x):
     return pltpu.with_memory_space_constraint(x, pltpu.HBM)
 
@@ -46,6 +55,10 @@
     return [pieces[0]] + [
         lax.ppermute(pieces[k], axis, [(i, i ^ k) for i in range(size)]) for k in range(1, size)
     ]
+
+
+def swap(piece, axis, k):
+    return lax.ppermute(piece, axis, [(i, i ^ k) for i in range(lax.axis_size(axis))])
 
 
 def norm_body(x_hbm, gain_hbm, *refs):
@@ -71,36 +84,47 @@
         out_ref[...] = (part * inverse * gain_ref[:, columns]).astype(jnp.bfloat16)
 
 
-def project_body(tile, n, *refs):
-    pieces, w_ref, outs = refs[:n], refs[n], refs[n + 1 :]
-    rows = jnp.concatenate([p[...] for p in pieces], axis=0)
-    width = w_ref.shape[1]
-    each = rows.shape[0] // (n * n)
-
-    @pl.loop(0, width // tile)
-    def _(i):
-        columns = pl.ds(pl.multiple_of(i * tile, 128), tile)
-        total = jnp.dot(rows, w_ref[:, columns], preferred_element_type=jnp.float32)
-        for k, out in enumerate(outs):
-            group = [
-                total[(j * n + k) * each : (j * n + k + 1) * each] for j in range(n)
-            ]
-            out[:, columns] = jnp.concatenate(group, axis=0).astype(out.dtype)
-
-
-def project(pieces, w, tile, order):
-    n = len(pieces)
-    rows, width = pieces[0].shape[0], w.shape[1]
-    outs = [struct((rows, width), jnp.float32 if k == 0 else jnp.bfloat16) for k in range(n)]
-    w = pltpu.with_memory_space_constraint(w, pltpu.VMEM)
+def regroup(total, n):
+    each = total.shape[0] // (n * n)
+    return [
+        jnp.concatenate(
+            [total[(j * n + k) * each : (j * n + k + 1) * each] for j in range(n)], axis=0
+        )
+        for k in range(n)
+    ]
+
+
+def dot_body(cuts, parts, *refs):
+    refs = list(refs)
+    pieces = [jnp.concatenate([refs.pop(0)[...] for _ in range(n)], axis=1) for n in cuts]
+    w_ref, *outs = refs
+    total = jnp.dot(
+        jnp.concatenate(pieces, axis=0), w_ref[...], preferred_element_type=jnp.float32
+    )
+    for group, n in zip(regroup(total, len(cuts)), parts):
+        for i in range(n):
+            out = outs.pop(0)
+            width = out.shape[1]
+            out[...] = group[:, i * width : (i + 1) * width].astype(out.dtype)
+
+
+def dot(pieces, w, kept=(0,), parts=(1, 1, 1, 1), order=()):
+    n, rows, (depth, width) = len(pieces), pieces[0][0].shape[0], w.shape
+    outs = [
+        struct((rows, width // parts[k]), jnp.float32 if k in kept else jnp.bfloat16)
+        for k in range(n)
+        for _ in range(parts[k])
+    ]
+    cuts = [len(piece) for piece in pieces]
+    ins = [part for piece in pieces for part in piece]
     return call(
-        functools.partial(project_body, tile, n),
+        functools.partial(dot_body, cuts, parts),
         outs,
-        [VMEM] * (n + 1),
-        [*pieces, w],
-        limit=12,
-        flops=2 * n * rows * w.shape[0] * width,
-        traffic=2 * w.shape[0] * width,
+        [VMEM] * (len(ins) + 1),
+        [*ins, near(w)],
+        limit=6,
+        flops=2 * n * rows * depth * width,
+        traffic=2 * depth * width,
         order=order,
     )
 
@@ -173,7 +197,7 @@
         [struct((seqs, width // blocks))] * blocks,
         [VMEM] * (blocks + 2) + [SMEM],
         [*pieces, keys, values, cache_lengths],
-        order=NEAR_LAST,
+        order=B2,
         limit=12,
         scratch=[
             pltpu.VMEM((seqs, width + 2 * head), jnp.float32),
@@ -183,6 +207,14 @@
         flops=50_000_000_000,
         traffic=4 * seqs * slots * head,
     )
+
+
+def cut_body(*refs):
+    rows = jnp.concatenate([r[...] for r in refs[:4]], axis=0)
+    whole, early, late = refs[4:]
+    whole[...] = rows
+    early[...] = rows[:, : early.shape[1]]
+    late[...] = rows[:, early.shape[1] :]
 
 
 def join_body(*refs):
@@ -216,23 +248,34 @@
         ],
         flops=50_000_000_000,
     )
-    mine = call(join_body, struct((groups * seqs, depth)), [VMEM] * groups, exchange(normed, "gx"), order=NEAR_LAST)
-    pieces = exchange([mine] * blocks, "yz")
-    sums = exchange(project(pieces, w_qkv, w_qkv.shape[1], FAR_LAST), "gx")
+    half = depth // 2
+    mine, *halves = call(
+        cut_body,
+        [struct((groups * seqs, size)) for size in (depth, half, half)],
+        [VMEM] * groups,
+        exchange(normed, "gx"),
+        order=A1,
+    )
+    one = swap(mine, "yz", 1)
+    two = [swap(part, "yz", 2) for part in halves]
+    three = [swap(part, "yz", 1) for part in two]
+    sums = dot([[mine], [one], two, three], w_qkv, order=A2)
+    sums = exchange(sums, "gx")
     parts = call(
-        total_body, [struct((seqs, w_qkv.shape[1]))] * blocks, [VMEM] * groups, sums, order=NEAR_LAST
+        total_body, [struct((seqs, w_qkv.shape[1]))] * blocks, [VMEM] * groups, sums, order=B1
     )
     attended = attend(exchange(parts, "yz"), cache_keys, cache_values, cache_lengths, width)
     got = exchange(attended, "yz")
-    mine = call(join_body, struct((4 * seqs, got[0].shape[1])), [VMEM] * 4, got, flops=50_000_000_000, order=NEAR_LAST)
-    pieces = exchange([mine] * groups, "gx")
-    sums = exchange(project(pieces, w_out, w_out.shape[1], NEAR_LAST), "yz")
+    mine = call(join_body, struct((4 * seqs, got[0].shape[1])), [VMEM] * 4, got, flops=50_000_000_000, order=C1)
+    two = swap(mine, "gx", 2)
+    pieces = [[mine], [swap(mine, "gx", 1)], [two], [swap(two, "gx", 1)]]
+    sums = exchange(dot(pieces, w_out, order=C2), "yz")
     return call(
         functools.partial(place_body, blocks),
         struct((groups, seqs, w_out.shape[1])),
         [VMEM] * blocks,
         sums,
-        order=FAR_LAST,
+        order=D,
     )
 
 

time: 80.2 us -> 77 us (0.960)
  waiting for transfers between devices: 40.5 us -> 36 us
  starting transfers between devices: 24.8 us -> 26.1 us
    ppermute x21 -> x15, waiting for transfers between devices: 40.5 us -> 24.4 us  [exchange(): lax.ppermute(pieces[k], axis, [(i, i ^ k) for i in range(size)])]
    ppermute x0 -> x8, waiting for transfers between devices: none -> 11.6 us  [swap(): lax.ppermute(piece, axis, [(i, i ^ k) for i in range(lax.axis_size(axis))])]
    ppermute x0 -> x8, starting transfers between devices: none -> 7.66 us  [swap(): lax.ppermute(piece, axis, [(i, i ^ k) for i in range(lax.axis_size(axis))])]
    ppermute x21 -> x15, starting transfers between devices: 24.8 us -> 18.4 us  [exchange(): lax.ppermute(pieces[k], axis, [(i, i ^ k) for i in range(size)])]
  transfers between devices with their start and end apart: 21 -> 23, of which waited for: 16 -> 16; matrix products, arithmetic and copies ran while one was open for 0% -> 0% of each run, Pallas kernels for 0% -> 0%
where the time goes in v3:
time: 77 us; the launch traced here: 76.9 us
  waiting for transfers between devices  36 us (47%)
  starting transfers between devices  26.1 us (34%)
  Pallas kernels  14.5 us (19%)
    ppermute x15, waiting for transfers between devices, exchange(): lax.ppermute(pieces[k], axis, [(i, i ^ k) for i in range(size)])  24.4 us
    ppermute x15, starting transfers between devices, exchange(): lax.ppermute(pieces[k], axis, [(i, i ^ k) for i in range(size)])  18.4 us
    pallas_call x8, Pallas kernels, call(): pl.pallas_call(ordered, out_shape=outs, in_specs=[in_specs[i] for i in or...  14.5 us
    ppermute x8, waiting for transfers between devices, swap(): lax.ppermute(piece, axis, [(i, i ^ k) for i in range(lax.axis_size(axis))])  11.6 us
    ppermute x8, starting transfers between devices, swap(): lax.ppermute(piece, axis, [(i, i ^ k) for i in range(lax.axis_size(axis))])  7.66 us
  transfers between devices with their start and end apart: 23, of which 16 were waited for; matrix products, arithmetic and copies ran while one was open for 0% of the time, Pallas kernels for 0%

profile of v3, /device:TPU:0, one launch (start us, length us, event | category | flops | bytes accessed | tf_op | source)
XLA Modules:
  0.0 76.9 jit_solution(12574856448401382810)
XLA Ops:
  0.0 1.6 %shard_map.73 = (bf16[4,4608]{1,0:T(4,128)(2,1)S(1)}, bf16[4,4608]{1,0:T(4,128)(2,1)S(1)}, bf16[4,4608]{1,0:T(4,128)(2,1)S(1)}, bf16[4,4608]{1,0:T(4,128)(2,1)S(1)}) custom-call(bf16[4,18432]{1,0:T(4,128)(2,1)} %refs_0_.1, f32[1,18432]{1,0:T(1,128)} %bitcast.3), custom_call_target="tpu_custom_call" | custom-call | flops 49999998976 | tf_op jit(solution)/shard_map/pallas_call | solution.py:30
  2.2 2.6 %collective-permute-start.1 = (bf16[4,4608]{1,0:T(4,128)(2,1)S(1)}, bf16[4,4608]{1,0:T(4,128)(2,1)S(1)}, u32[]{:S(2)}, u32[]{:S(2)}) collective-permute-start(bf16[4,4608]{1,0:T(4,128)(2,1)S(1)} %get-tuple-element.30), channel_id=1, source_target_pairs={{0,12},{4,8},{8,4},{12,0},{1,13},{5,9},{9,5},{13,1},{2,14},{6,10},... | collective-permute-start | bytes 110600 | tf_op jit(solution)/shard_map/ppermute | solution.py:56
  4.9 1.7 %collective-permute-done.1.refs_2_ = bf16[4,4608]{1,0:T(4,128)(2,1)S(1)} collective-permute-done((bf16[4,4608]{1,0:T(4,128)(2,1)S(1)}, bf16[4,4608]{1,0:T(4,128)(2,1)S(1)}, u32[]{:S(2)}, u32[]{:S(2)}) %collective-permute-start.1) | collective-permute-done | bytes 36896 | tf_op jit(solution)/shard_map/ppermute | solution.py:56
  6.6 2.2 %collective-permute-done.2.refs_3_ = bf16[4,4608]{1,0:T(4,128)(2,1)S(1)} collective-permute-done((bf16[4,4608]{1,0:T(4,128)(2,1)S(1)}, bf16[4,4608]{1,0:T(4,128)(2,1)S(1)}, u32[]{:S(2)}, u32[]{:S(2)}) %collective-permute-start.2) | collective-permute-done | bytes 36896 | tf_op jit(solution)/shard_map/ppermute | solution.py:56
  8.8 2.7 %collective-permute-start.4 = (bf16[16,2304]{1,0:T(8,128)(2,1)S(1)}, bf16[16,2304]{1,0:T(8,128)(2,1)S(1)}, u32[]{:S(2)}, u32[]{:S(2)}) collective-permute-start(bf16[16,2304]{1,0:T(8,128)(2,1)S(1)} %get-tuple-element.33), channel_id=1, source_target_pairs={{0,2},{1,3},{2,0},{3,1},{4,6},{5,7},{6,4},{7,5},{8,10},{9,11},{10,... | collective-permute-start | bytes 221192 | tf_op jit(solution)/shard_map/ppermute | solution.py:61
  11.8 1.6 %collective-permute-start.3 = (bf16[16,4608]{1,0:T(8,128)(2,1)S(1)}, bf16[16,4608]{1,0:T(8,128)(2,1)S(1)}, u32[]{:S(2)}, u32[]{:S(2)}) collective-permute-start(bf16[16,4608]{1,0:T(8,128)(2,1)S(1)} %get-tuple-element.32.refs_0_), channel_id=1, source_target_pairs={{0,1},{1,0},{2,3},{3,2},{4,5},{5,4},{6,7},{7,6},{8,9},{9,8},{10,11... | collective-permute-start | bytes 442376 | tf_op jit(solution)/shard_map/ppermute | solution.py:61
  13.4 3.0 %collective-permute-done.4.refs_2_ = bf16[16,2304]{1,0:T(8,128)(2,1)S(1)} collective-permute-done((bf16[16,2304]{1,0:T(8,128)(2,1)S(1)}, bf16[16,2304]{1,0:T(8,128)(2,1)S(1)}, u32[]{:S(2)}, u32[]{:S(2)}) %collective-permute-start.4) | collective-permute-done | bytes 73760 | tf_op jit(solution)/shard_map/ppermute | solution.py:61
  18.9 2.2 %collective-permute-done.6.refs_4_ = bf16[16,2304]{1,0:T(8,128)(2,1)S(1)} collective-permute-done((bf16[16,2304]{1,0:T(8,128)(2,1)S(1)}, bf16[16,2304]{1,0:T(8,128)(2,1)S(1)}, u32[]{:S(2)}, u32[]{:S(2)}) %collective-permute-start.6) | collective-permute-done | bytes 73760 | tf_op jit(solution)/shard_map/ppermute | solution.py:61
  22.1 5.2 %shard_map.75 = (f32[16,3200]{1,0:T(8,128)S(1)}, bf16[16,3200]{1,0:T(8,128)(2,1)S(1)}, bf16[16,3200]{1,0:T(8,128)(2,1)S(1)}, bf16[16,3200]{1,0:T(8,128)(2,1)S(1)}) custom-call(bf16[16,4608]{1,0:T(8,128)(2,1)S(1)} %get-tuple-element.32.refs_0_, bf16[16,4608]{1,0:T(8,128)(2,1)S(1)} %collective-permute-done.3.refs_1_, ...), custom_call_target="tpu_custom_call" | custom-call | flops 1887436800 | bytes 29491200 | tf_op jit(solution)/shard_map/pallas_call | solution.py:30
  27.3 1.3 %collective-permute-start.8 = (bf16[16,3200]{1,0:T(8,128)(2,1)S(1)}, bf16[16,3200]{1,0:T(8,128)(2,1)S(1)}, u32[]{:S(2)}, u32[]{:S(2)}) collective-permute-start(bf16[16,3200]{1,0:T(8,128)(2,1)S(1)} %get-tuple-element.36), channel_id=1, source_target_pairs={{0,8},{4,12},{8,0},{12,4},{1,9},{5,13},{9,1},{13,5},{2,10},{6,14},... | collective-permute-start | bytes 307208 | tf_op jit(solution)/shard_map/ppermute | solution.py:56
  29.5 3.0 %collective-permute-done.8.refs_1_ = bf16[16,3200]{1,0:T(8,128)(2,1)S(1)} collective-permute-done((bf16[16,3200]{1,0:T(8,128)(2,1)S(1)}, bf16[16,3200]{1,0:T(8,128)(2,1)S(1)}, u32[]{:S(2)}, u32[]{:S(2)}) %collective-permute-start.8) | collective-permute-done | bytes 102432 | tf_op jit(solution)/shard_map/ppermute | solution.py:56
  33.8 2.5 %collective-permute-start.11 = (bf16[4,3200]{1,0:T(4,128)(2,1)S(1)}, bf16[4,3200]{1,0:T(4,128)(2,1)S(1)}, u32[]{:S(2)}, u32[]{:S(2)}) collective-permute-start(bf16[4,3200]{1,0:T(4,128)(2,1)S(1)} %get-tuple-element.40), channel_id=1, source_target_pairs={{0,2},{1,3},{2,0},{3,1},{4,6},{5,7},{6,4},{7,5},{8,10},{9,11},{10,... | collective-permute-start | bytes 76808 | tf_op jit(solution)/shard_map/ppermute | solution.py:56
  38.6 3.5 %collective-permute-done.12.refs_2_ = bf16[4,3200]{1,0:T(4,128)(2,1)S(1)} collective-permute-done((bf16[4,3200]{1,0:T(4,128)(2,1)S(1)}, bf16[4,3200]{1,0:T(4,128)(2,1)S(1)}, u32[]{:S(2)}, u32[]{:S(2)}) %collective-permute-start.12) | collective-permute-done | bytes 25632 | tf_op jit(solution)/shard_map/ppermute | solution.py:56
  42.2 1.8 %shard_map.77 = (bf16[4,3072]{1,0:T(4,128)(2,1)S(1)}, bf16[4,3072]{1,0:T(4,128)(2,1)S(1)}, bf16[4,3072]{1,0:T(4,128)(2,1)S(1)}, bf16[4,3072]{1,0:T(4,128)(2,1)S(1)}) custom-call(bf16[4,3200]{1,0:T(4,128)(2,1)S(1)} %get-tuple-element.39.refs_0_, bf16[4,3200]{1,0:T(4,128)(2,1)S(1)} %collective-permute-done.11.refs_1_, ...), custom_call_target="tpu_custom_call" | custom-call | flops 49999998976 | bytes 4194304 | tf_op jit(solution)/shard_map/pallas_call | solution.py:30
  44.0 1.9 %collective-permute-start.14 = (bf16[4,3072]{1,0:T(4,128)(2,1)S(1)}, bf16[4,3072]{1,0:T(4,128)(2,1)S(1)}, u32[]{:S(2)}, u32[]{:S(2)}) collective-permute-start(bf16[4,3072]{1,0:T(4,128)(2,1)S(1)} %get-tuple-element.44), channel_id=1, source_target_pairs={{0,3},{1,2},{2,1},{3,0},{4,7},{5,6},{6,5},{7,4},{8,11},{9,10},{10,... | collective-permute-start | bytes 73736 | tf_op jit(solution)/shard_map/ppermute | solution.py:56
  45.9 2.5 %collective-permute-start.16 = (bf16[4,3072]{1,0:T(4,128)(2,1)S(1)}, bf16[4,3072]{1,0:T(4,128)(2,1)S(1)}, u32[]{:S(2)}, u32[]{:S(2)}) collective-permute-start(bf16[4,3072]{1,0:T(4,128)(2,1)S(1)} %get-tuple-element.46), channel_id=1, source_target_pairs={{0,1},{1,0},{2,3},{3,2},{4,5},{5,4},{6,7},{7,6},{8,9},{9,8},{10,11... | collective-permute-start | bytes 73736 | tf_op jit(solution)/shard_map/ppermute | solution.py:56
  50.7 1.4 %collective-permute-start.18 = (bf16[16,3072]{1,0:T(8,128)(2,1)S(1)}, bf16[16,3072]{1,0:T(8,128)(2,1)S(1)}, u32[]{:S(2)}, u32[]{:S(2)}) collective-permute-start(bf16[16,3072]{1,0:T(8,128)(2,1)S(1)} %shard_map.78.refs_0_), channel_id=1, source_target_pairs={{0,8},{4,12},{8,0},{12,4},{1,9},{5,13},{9,1},{13,5},{2,10},{6,14},... | collective-permute-start | bytes 294920 | tf_op jit(solution)/shard_map/ppermute | solution.py:61
  52.1 3.3 %collective-permute-done.18.refs_2_ = bf16[16,3072]{1,0:T(8,128)(2,1)S(1)} collective-permute-done((bf16[16,3072]{1,0:T(8,128)(2,1)S(1)}, bf16[16,3072]{1,0:T(8,128)(2,1)S(1)}, u32[]{:S(2)}, u32[]{:S(2)}) %collective-permute-start.18) | collective-permute-done | bytes 98336 | tf_op jit(solution)/shard_map/ppermute | solution.py:61
  55.4 1.3 %collective-permute-done.19.refs_3_ = bf16[16,3072]{1,0:T(8,128)(2,1)S(1)} collective-permute-done((bf16[16,3072]{1,0:T(8,128)(2,1)S(1)}, bf16[16,3072]{1,0:T(8,128)(2,1)S(1)}, u32[]{:S(2)}, u32[]{:S(2)}) %collective-permute-start.19) | collective-permute-done | bytes 98336 | tf_op jit(solution)/shard_map/ppermute | solution.py:61
  56.8 5.0 %shard_map.79 = (f32[16,4608]{1,0:T(8,128)S(1)}, bf16[16,4608]{1,0:T(8,128)(2,1)S(1)}, bf16[16,4608]{1,0:T(8,128)(2,1)S(1)}, bf16[16,4608]{1,0:T(8,128)(2,1)S(1)}) custom-call(bf16[16,3072]{1,0:T(8,128)(2,1)S(1)} %shard_map.78.refs_0_, bf16[16,3072]{1,0:T(8,128)(2,1)S(1)} %collective-permute-done.17.refs_1_, ...), custom_call_target="tpu_custom_call" | custom-call | flops 1811939328 | bytes 28311552 | tf_op jit(solution)/shard_map/pallas_call | solution.py:30
  61.7 2.1 %collective-permute-start.20 = (bf16[16,4608]{1,0:T(8,128)(2,1)S(1)}, bf16[16,4608]{1,0:T(8,128)(2,1)S(1)}, u32[]{:S(2)}, u32[]{:S(2)}) collective-permute-start(bf16[16,4608]{1,0:T(8,128)(2,1)S(1)} %get-tuple-element.48), channel_id=1, source_target_pairs={{0,2},{1,3},{2,0},{3,1},{4,6},{5,7},{6,4},{7,5},{8,10},{9,11},{10,... | collective-permute-start | bytes 442376 | tf_op jit(solution)/shard_map/ppermute | solution.py:56
  64.3 1.9 %collective-permute-start.22 = (bf16[16,4608]{1,0:T(8,128)(2,1)S(1)}, bf16[16,4608]{1,0:T(8,128)(2,1)S(1)}, u32[]{:S(2)}, u32[]{:S(2)}) collective-permute-start(bf16[16,4608]{1,0:T(8,128)(2,1)S(1)} %get-tuple-element.50), channel_id=1, source_target_pairs={{0,3},{1,2},{2,1},{3,0},{4,7},{5,6},{6,5},{7,4},{8,11},{9,10},{10,... | collective-permute-start | bytes 442376 | tf_op jit(solution)/shard_map/ppermute | solution.py:56
  66.2 6.9 %collective-permute-done.20.refs_1_ = bf16[16,4608]{1,0:T(8,128)(2,1)S(1)} collective-permute-done((bf16[16,4608]{1,0:T(8,128)(2,1)S(1)}, bf16[16,4608]{1,0:T(8,128)(2,1)S(1)}, u32[]{:S(2)}, u32[]{:S(2)}) %collective-permute-start.20) | collective-permute-done | bytes 147488 | tf_op jit(solution)/shard_map/ppermute | solution.py:56
  73.1 3.0 %collective-permute-done.22.refs_3_ = bf16[16,4608]{1,0:T(8,128)(2,1)S(1)} collective-permute-done((bf16[16,4608]{1,0:T(8,128)(2,1)S(1)}, bf16[16,4608]{1,0:T(8,128)(2,1)S(1)}, u32[]{:S(2)}, u32[]{:S(2)}) %collective-permute-start.22) | collective-permute-done | bytes 147488 | tf_op jit(solution)/shard_map/ppermute | solution.py:56
  (53 shorter events, 12.4 us)
Async XLA Ops:
  1.7 40.5 %copy-start.1 = (bf16[4,1024,256]{2,1,0:T(8,128)(2,1)S(1)}, bf16[4,1024,256]{2,1,0:T(8,128)(2,1)}, u32[]{:S(2)}) copy-start(bf16[4,1024,256]{2,1,0:T(8,128)(2,1)} %refs_4_.2) | copy-start | bytes 6291460
  1.7 3.2 %collective-permute-start = (bf16[4,4608]{1,0:T(4,128)(2,1)S(1)}, bf16[4,4608]{1,0:T(4,128)(2,1)S(1)}, u32[]{:S(2)}, u32[]{:S(2)}) collective-permute-start(bf16[4,4608]{1,0:T(4,128)(2,1)S(1)} %get-tuple-element.29), channel_id=1, source_target_pairs={{0,4},{4,0},{8,12},{12,8},{1,5},{5,1},{9,13},{13,9},{2,6},{6,2},{1... | collective-permute-start | bytes 110600 | tf_op jit(solution)/shard_map/ppermute | solution.py:56
  2.2 4.4 %collective-permute-start.1 = (bf16[4,4608]{1,0:T(4,128)(2,1)S(1)}, bf16[4,4608]{1,0:T(4,128)(2,1)S(1)}, u32[]{:S(2)}, u32[]{:S(2)}) collective-permute-start(bf16[4,4608]{1,0:T(4,128)(2,1)S(1)} %get-tuple-element.30), channel_id=1, source_target_pairs={{0,12},{4,8},{8,4},{12,0},{1,13},{5,9},{9,5},{13,1},{2,14},{6,10},... | collective-permute-start | bytes 110600 | tf_op jit(solution)/shard_map/ppermute | solution.py:56
  4.8 4.0 %collective-permute-start.2 = (bf16[4,4608]{1,0:T(4,128)(2,1)S(1)}, bf16[4,4608]{1,0:T(4,128)(2,1)S(1)}, u32[]{:S(2)}, u32[]{:S(2)}) collective-permute-start(bf16[4,4608]{1,0:T(4,128)(2,1)S(1)} %get-tuple-element.31), channel_id=1, source_target_pairs={{0,8},{4,12},{8,0},{12,4},{1,9},{5,13},{9,1},{13,5},{2,10},{6,14},... | collective-permute-start | bytes 110600 | tf_op jit(solution)/shard_map/ppermute | solution.py:56
  8.8 7.6 %collective-permute-start.4 = (bf16[16,2304]{1,0:T(8,128)(2,1)S(1)}, bf16[16,2304]{1,0:T(8,128)(2,1)S(1)}, u32[]{:S(2)}, u32[]{:S(2)}) collective-permute-start(bf16[16,2304]{1,0:T(8,128)(2,1)S(1)} %get-tuple-element.33), channel_id=1, source_target_pairs={{0,2},{1,3},{2,0},{3,1},{4,6},{5,7},{6,4},{7,5},{8,10},{9,11},{10,... | collective-permute-start | bytes 221192 | tf_op jit(solution)/shard_map/ppermute | solution.py:61
  11.5 6.3 %collective-permute-start.5 = (bf16[16,2304]{1,0:T(8,128)(2,1)S(1)}, bf16[16,2304]{1,0:T(8,128)(2,1)S(1)}, u32[]{:S(2)}, u32[]{:S(2)}) collective-permute-start(bf16[16,2304]{1,0:T(8,128)(2,1)S(1)} %get-tuple-element.34), channel_id=1, source_target_pairs={{0,2},{1,3},{2,0},{3,1},{4,6},{5,7},{6,4},{7,5},{8,10},{9,11},{10,... | collective-permute-start | bytes 221192 | tf_op jit(solution)/shard_map/ppermute | solution.py:61
  11.8 10.3 %collective-permute-start.3 = (bf16[16,4608]{1,0:T(8,128)(2,1)S(1)}, bf16[16,4608]{1,0:T(8,128)(2,1)S(1)}, u32[]{:S(2)}, u32[]{:S(2)}) collective-permute-start(bf16[16,4608]{1,0:T(8,128)(2,1)S(1)} %get-tuple-element.32.refs_0_), channel_id=1, source_target_pairs={{0,1},{1,0},{2,3},{3,2},{4,5},{5,4},{6,7},{7,6},{8,9},{9,8},{10,11... | collective-permute-start | bytes 442376 | tf_op jit(solution)/shard_map/ppermute | solution.py:61
  16.4 4.7 %collective-permute-start.6 = (bf16[16,2304]{1,0:T(8,128)(2,1)S(1)}, bf16[16,2304]{1,0:T(8,128)(2,1)S(1)}, u32[]{:S(2)}, u32[]{:S(2)}) collective-permute-start(bf16[16,2304]{1,0:T(8,128)(2,1)S(1)} %collective-permute-done.4.refs_2_), channel_id=1, source_target_pairs={{0,1},{1,0},{2,3},{3,2},{4,5},{5,4},{6,7},{7,6},{8,9},{9,8},{10,11... | collective-permute-start | bytes 221192 | tf_op jit(solution)/shard_map/ppermute | solution.py:61
  17.7 4.4 %collective-permute-start.7 = (bf16[16,2304]{1,0:T(8,128)(2,1)S(1)}, bf16[16,2304]{1,0:T(8,128)(2,1)S(1)}, u32[]{:S(2)}, u32[]{:S(2)}) collective-permute-start(bf16[16,2304]{1,0:T(8,128)(2,1)S(1)} %collective-permute-done.5.refs_3_), channel_id=1, source_target_pairs={{0,1},{1,0},{2,3},{3,2},{4,5},{5,4},{6,7},{7,6},{8,9},{9,8},{10,11... | collective-permute-start | bytes 221192 | tf_op jit(solution)/shard_map/ppermute | solution.py:61
  27.3 5.2 %collective-permute-start.8 = (bf16[16,3200]{1,0:T(8,128)(2,1)S(1)}, bf16[16,3200]{1,0:T(8,128)(2,1)S(1)}, u32[]{:S(2)}, u32[]{:S(2)}) collective-permute-start(bf16[16,3200]{1,0:T(8,128)(2,1)S(1)} %get-tuple-element.36), channel_id=1, source_target_pairs={{0,8},{4,12},{8,0},{12,4},{1,9},{5,13},{9,1},{13,5},{2,10},{6,14},... | collective-permute-start | bytes 307208 | tf_op jit(solution)/shard_map/ppermute | solution.py:56
  28.6 4.0 %collective-permute-start.9 = (bf16[16,3200]{1,0:T(8,128)(2,1)S(1)}, bf16[16,3200]{1,0:T(8,128)(2,1)S(1)}, u32[]{:S(2)}, u32[]{:S(2)}) collective-permute-start(bf16[16,3200]{1,0:T(8,128)(2,1)S(1)} %get-tuple-element.37), channel_id=1, source_target_pairs={{0,4},{4,0},{8,12},{12,8},{1,5},{5,1},{9,13},{13,9},{2,6},{6,2},{1... | collective-permute-start | bytes 307208 | tf_op jit(solution)/shard_map/ppermute | solution.py:56
  28.6 5.1 %collective-permute-start.10 = (bf16[16,3200]{1,0:T(8,128)(2,1)S(1)}, bf16[16,3200]{1,0:T(8,128)(2,1)S(1)}, u32[]{:S(2)}, u32[]{:S(2)}) collective-permute-start(bf16[16,3200]{1,0:T(8,128)(2,1)S(1)} %get-tuple-element.38), channel_id=1, source_target_pairs={{0,12},{4,8},{8,4},{12,0},{1,13},{5,9},{9,5},{13,1},{2,14},{6,10},... | collective-permute-start | bytes 307208 | tf_op jit(solution)/shard_map/ppermute | solution.py:56
  33.8 4.8 %collective-permute-start.11 = (bf16[4,3200]{1,0:T(4,128)(2,1)S(1)}, bf16[4,3200]{1,0:T(4,128)(2,1)S(1)}, u32[]{:S(2)}, u32[]{:S(2)}) collective-permute-start(bf16[4,3200]{1,0:T(4,128)(2,1)S(1)} %get-tuple-element.40), channel_id=1, source_target_pairs={{0,2},{1,3},{2,0},{3,1},{4,6},{5,7},{6,4},{7,5},{8,10},{9,11},{10,... | collective-permute-start | bytes 76808 | tf_op jit(solution)/shard_map/ppermute | solution.py:56
  36.3 5.8 %collective-permute-start.12 = (bf16[4,3200]{1,0:T(4,128)(2,1)S(1)}, bf16[4,3200]{1,0:T(4,128)(2,1)S(1)}, u32[]{:S(2)}, u32[]{:S(2)}) collective-permute-start(bf16[4,3200]{1,0:T(4,128)(2,1)S(1)} %get-tuple-element.41), channel_id=1, source_target_pairs={{0,3},{1,2},{2,1},{3,0},{4,7},{5,6},{6,5},{7,4},{8,11},{9,10},{10,... | collective-permute-start | bytes 76808 | tf_op jit(solution)/shard_map/ppermute | solution.py:56
  37.5 4.7 %collective-permute-start.13 = (bf16[4,3200]{1,0:T(4,128)(2,1)S(1)}, bf16[4,3200]{1,0:T(4,128)(2,1)S(1)}, u32[]{:S(2)}, u32[]{:S(2)}) collective-permute-start(bf16[4,3200]{1,0:T(4,128)(2,1)S(1)} %get-tuple-element.42), channel_id=1, source_target_pairs={{0,1},{1,0},{2,3},{3,2},{4,5},{5,4},{6,7},{7,6},{8,9},{9,8},{10,11... | collective-permute-start | bytes 76808 | tf_op jit(solution)/shard_map/ppermute | solution.py:56
  44.0 5.7 %collective-permute-start.14 = (bf16[4,3072]{1,0:T(4,128)(2,1)S(1)}, bf16[4,3072]{1,0:T(4,128)(2,1)S(1)}, u32[]{:S(2)}, u32[]{:S(2)}) collective-permute-start(bf16[4,3072]{1,0:T(4,128)(2,1)S(1)} %get-tuple-element.44), channel_id=1, source_target_pairs={{0,3},{1,2},{2,1},{3,0},{4,7},{5,6},{6,5},{7,4},{8,11},{9,10},{10,... | collective-permute-start | bytes 73736 | tf_op jit(solution)/shard_map/ppermute | solution.py:56
  45.9 4.7 %collective-permute-start.15 = (bf16[4,3072]{1,0:T(4,128)(2,1)S(1)}, bf16[4,3072]{1,0:T(4,128)(2,1)S(1)}, u32[]{:S(2)}, u32[]{:S(2)}) collective-permute-start(bf16[4,3072]{1,0:T(4,128)(2,1)S(1)} %get-tuple-element.45), channel_id=1, source_target_pairs={{0,2},{1,3},{2,0},{3,1},{4,6},{5,7},{6,4},{7,5},{8,10},{9,11},{10,... | collective-permute-start | bytes 73736 | tf_op jit(solution)/shard_map/ppermute | solution.py:56
  45.9 4.7 %collective-permute-start.16 = (bf16[4,3072]{1,0:T(4,128)(2,1)S(1)}, bf16[4,3072]{1,0:T(4,128)(2,1)S(1)}, u32[]{:S(2)}, u32[]{:S(2)}) collective-permute-start(bf16[4,3072]{1,0:T(4,128)(2,1)S(1)} %get-tuple-element.46), channel_id=1, source_target_pairs={{0,1},{1,0},{2,3},{3,2},{4,5},{5,4},{6,7},{7,6},{8,9},{9,8},{10,11... | collective-permute-start | bytes 73736 | tf_op jit(solution)/shard_map/ppermute | solution.py:56
  50.7 4.7 %collective-permute-start.18 = (bf16[16,3072]{1,0:T(8,128)(2,1)S(1)}, bf16[16,3072]{1,0:T(8,128)(2,1)S(1)}, u32[]{:S(2)}, u32[]{:S(2)}) collective-permute-start(bf16[16,3072]{1,0:T(8,128)(2,1)S(1)} %shard_map.78.refs_0_), channel_id=1, source_target_pairs={{0,8},{4,12},{8,0},{12,4},{1,9},{5,13},{9,1},{13,5},{2,10},{6,14},... | collective-permute-start | bytes 294920 | tf_op jit(solution)/shard_map/ppermute | solution.py:61
  52.1 3.3 %collective-permute-start.17 = (bf16[16,3072]{1,0:T(8,128)(2,1)S(1)}, bf16[16,3072]{1,0:T(8,128)(2,1)S(1)}, u32[]{:S(2)}, u32[]{:S(2)}) collective-permute-start(bf16[16,3072]{1,0:T(8,128)(2,1)S(1)} %shard_map.78.refs_0_), channel_id=1, source_target_pairs={{0,4},{4,0},{8,12},{12,8},{1,5},{5,1},{9,13},{13,9},{2,6},{6,2},{1... | collective-permute-start | bytes 294920 | tf_op jit(solution)/shard_map/ppermute | solution.py:61
  55.4 1.3 %collective-permute-start.19 = (bf16[16,3072]{1,0:T(8,128)(2,1)S(1)}, bf16[16,3072]{1,0:T(8,128)(2,1)S(1)}, u32[]{:S(2)}, u32[]{:S(2)}) collective-permute-start(bf16[16,3072]{1,0:T(8,128)(2,1)S(1)} %collective-permute-done.18.refs_2_), channel_id=1, source_target_pairs={{0,4},{4,0},{8,12},{12,8},{1,5},{5,1},{9,13},{13,9},{2,6},{6,2},{1... | collective-permute-start | bytes 294920 | tf_op jit(solution)/shard_map/ppermute | solution.py:61
  61.7 11.3 %collective-permute-start.20 = (bf16[16,4608]{1,0:T(8,128)(2,1)S(1)}, bf16[16,4608]{1,0:T(8,128)(2,1)S(1)}, u32[]{:S(2)}, u32[]{:S(2)}) collective-permute-start(bf16[16,4608]{1,0:T(8,128)(2,1)S(1)} %get-tuple-element.48), channel_id=1, source_target_pairs={{0,2},{1,3},{2,0},{3,1},{4,6},{5,7},{6,4},{7,5},{8,10},{9,11},{10,... | collective-permute-start | bytes 442376 | tf_op jit(solution)/shard_map/ppermute | solution.py:56
  63.8 9.2 %collective-permute-start.21 = (bf16[16,4608]{1,0:T(8,128)(2,1)S(1)}, bf16[16,4608]{1,0:T(8,128)(2,1)S(1)}, u32[]{:S(2)}, u32[]{:S(2)}) collective-permute-start(bf16[16,4608]{1,0:T(8,128)(2,1)S(1)} %get-tuple-element.49), channel_id=1, source_target_pairs={{0,1},{1,0},{2,3},{3,2},{4,5},{5,4},{6,7},{7,6},{8,9},{9,8},{10,11... | collective-permute-start | bytes 442376 | tf_op jit(solution)/shard_map/ppermute | solution.py:56
  64.3 11.8 %collective-permute-start.22 = (bf16[16,4608]{1,0:T(8,128)(2,1)S(1)}, bf16[16,4608]{1,0:T(8,128)(2,1)S(1)}, u32[]{:S(2)}, u32[]{:S(2)}) collective-permute-start(bf16[16,4608]{1,0:T(8,128)(2,1)S(1)} %get-tuple-element.50), channel_id=1, source_target_pairs={{0,3},{1,2},{2,1},{3,0},{4,7},{5,6},{6,5},{7,4},{8,11},{9,10},{10,... | collective-permute-start | bytes 442376 | tf_op jit(solution)/shard_map/ppermute | solution.py:56
  (10 other events, 179.4 us)

commit v4 on v3

--- a/solution.py
+++ b/solution.py
@@ -94,31 +94,26 @@
     ]
 
 
-def dot_body(cuts, parts, *refs):
+def dot_body(cuts, *refs):
     refs = list(refs)
     pieces = [jnp.concatenate([refs.pop(0)[...] for _ in range(n)], axis=1) for n in cuts]
     w_ref, *outs = refs
-    total = jnp.dot(
-        jnp.concatenate(pieces, axis=0), w_ref[...], preferred_element_type=jnp.float32
-    )
-    for group, n in zip(regroup(total, len(cuts)), parts):
-        for i in range(n):
-            out = outs.pop(0)
-            width = out.shape[1]
-            out[...] = group[:, i * width : (i + 1) * width].astype(out.dtype)
-
-
-def dot(pieces, w, kept=(0,), parts=(1, 1, 1, 1), order=()):
+    rows = jnp.concatenate(pieces, axis=0)
+    size = rows.shape[1] // max(cuts)
+    total = sum(
+        jnp.dot(rows[:, at : at + size], w_ref[at : at + size], preferred_element_type=jnp.float32)
+        for at in range(0, rows.shape[1], size)
+    )
+    for group, out in zip(regroup(total, len(cuts)), outs):
+        out[...] = group.astype(out.dtype)
+
+
+def dot(pieces, w, order=()):
     n, rows, (depth, width) = len(pieces), pieces[0][0].shape[0], w.shape
-    outs = [
-        struct((rows, width // parts[k]), jnp.float32 if k in kept else jnp.bfloat16)
-        for k in range(n)
-        for _ in range(parts[k])
-    ]
-    cuts = [len(piece) for piece in pieces]
+    outs = [struct((rows, width), jnp.bfloat16 if k else jnp.float32) for k in range(n)]
     ins = [part for piece in pieces for part in piece]
     return call(
-        functools.partial(dot_body, cuts, parts),
+        functools.partial(dot_body, [len(piece) for piece in pieces]),
         outs,
         [VMEM] * (len(ins) + 1),
         [*ins, near(w)],

time: 77 us -> 76.4 us (level)
  no operation moved by 1% of the time
where the time goes in v4:
time: 76.4 us; the launch traced here: 76.3 us
  waiting for transfers between devices  36 us (47%)
  starting transfers between devices  26.1 us (34%)
  Pallas kernels  13.9 us (18%)
    ppermute x15, waiting for transfers between devices, exchange(): lax.ppermute(pieces[k], axis, [(i, i ^ k) for i in range(size)])  24.4 us
    ppermute x15, starting transfers between devices, exchange(): lax.ppermute(pieces[k], axis, [(i, i ^ k) for i in range(size)])  18.4 us
    pallas_call x8, Pallas kernels, call(): pl.pallas_call(ordered, out_shape=outs, in_specs=[in_specs[i] for i in or...  13.9 us
    ppermute x8, waiting for transfers between devices, swap(): lax.ppermute(piece, axis, [(i, i ^ k) for i in range(lax.axis_size(axis))])  11.6 us
    ppermute x8, starting transfers between devices, swap(): lax.ppermute(piece, axis, [(i, i ^ k) for i in range(lax.axis_size(axis))])  7.64 us
  transfers between devices with their start and end apart: 23, of which 16 were waited for; matrix products, arithmetic and copies ran while one was open for 0% of the time, Pallas kernels for 0%

profile of v4, /device:TPU:0, one launch (start us, length us, event | category | flops | bytes accessed | tf_op | source)
XLA Modules:
  0.0 76.3 jit_solution(17178357674220102198)
XLA Ops:
  0.0 1.6 %shard_map.73 = (bf16[4,4608]{1,0:T(4,128)(2,1)S(1)}, bf16[4,4608]{1,0:T(4,128)(2,1)S(1)}, bf16[4,4608]{1,0:T(4,128)(2,1)S(1)}, bf16[4,4608]{1,0:T(4,128)(2,1)S(1)}) custom-call(bf16[4,18432]{1,0:T(4,128)(2,1)} %refs_0_.1, f32[1,18432]{1,0:T(1,128)} %bitcast.3), custom_call_target="tpu_custom_call" | custom-call | flops 49999998976 | tf_op jit(solution)/shard_map/pallas_call | solution.py:30
  2.2 2.6 %collective-permute-start.1 = (bf16[4,4608]{1,0:T(4,128)(2,1)S(1)}, bf16[4,4608]{1,0:T(4,128)(2,1)S(1)}, u32[]{:S(2)}, u32[]{:S(2)}) collective-permute-start(bf16[4,4608]{1,0:T(4,128)(2,1)S(1)} %get-tuple-element.30), channel_id=1, source_target_pairs={{0,12},{4,8},{8,4},{12,0},{1,13},{5,9},{9,5},{13,1},{2,14},{6,10},... | collective-permute-start | bytes 110600 | tf_op jit(solution)/shard_map/ppermute | solution.py:56
  4.9 1.7 %collective-permute-done.1.refs_2_ = bf16[4,4608]{1,0:T(4,128)(2,1)S(1)} collective-permute-done((bf16[4,4608]{1,0:T(4,128)(2,1)S(1)}, bf16[4,4608]{1,0:T(4,128)(2,1)S(1)}, u32[]{:S(2)}, u32[]{:S(2)}) %collective-permute-start.1) | collective-permute-done | bytes 36896 | tf_op jit(solution)/shard_map/ppermute | solution.py:56
  6.6 2.2 %collective-permute-done.2.refs_3_ = bf16[4,4608]{1,0:T(4,128)(2,1)S(1)} collective-permute-done((bf16[4,4608]{1,0:T(4,128)(2,1)S(1)}, bf16[4,4608]{1,0:T(4,128)(2,1)S(1)}, u32[]{:S(2)}, u32[]{:S(2)}) %collective-permute-start.2) | collective-permute-done | bytes 36896 | tf_op jit(solution)/shard_map/ppermute | solution.py:56
  8.8 2.7 %collective-permute-start.4 = (bf16[16,2304]{1,0:T(8,128)(2,1)S(1)}, bf16[16,2304]{1,0:T(8,128)(2,1)S(1)}, u32[]{:S(2)}, u32[]{:S(2)}) collective-permute-start(bf16[16,2304]{1,0:T(8,128)(2,1)S(1)} %get-tuple-element.33), channel_id=1, source_target_pairs={{0,2},{1,3},{2,0},{3,1},{4,6},{5,7},{6,4},{7,5},{8,10},{9,11},{10,... | collective-permute-start | bytes 221192 | tf_op jit(solution)/shard_map/ppermute | solution.py:61
  11.8 1.6 %collective-permute-start.3 = (bf16[16,4608]{1,0:T(8,128)(2,1)S(1)}, bf16[16,4608]{1,0:T(8,128)(2,1)S(1)}, u32[]{:S(2)}, u32[]{:S(2)}) collective-permute-start(bf16[16,4608]{1,0:T(8,128)(2,1)S(1)} %get-tuple-element.32.refs_0_), channel_id=1, source_target_pairs={{0,1},{1,0},{2,3},{3,2},{4,5},{5,4},{6,7},{7,6},{8,9},{9,8},{10,11... | collective-permute-start | bytes 442376 | tf_op jit(solution)/shard_map/ppermute | solution.py:61
  13.4 3.0 %collective-permute-done.4.refs_2_ = bf16[16,2304]{1,0:T(8,128)(2,1)S(1)} collective-permute-done((bf16[16,2304]{1,0:T(8,128)(2,1)S(1)}, bf16[16,2304]{1,0:T(8,128)(2,1)S(1)}, u32[]{:S(2)}, u32[]{:S(2)}) %collective-permute-start.4) | collective-permute-done | bytes 73760 | tf_op jit(solution)/shard_map/ppermute | solution.py:61
  18.9 2.2 %collective-permute-done.6.refs_4_ = bf16[16,2304]{1,0:T(8,128)(2,1)S(1)} collective-permute-done((bf16[16,2304]{1,0:T(8,128)(2,1)S(1)}, bf16[16,2304]{1,0:T(8,128)(2,1)S(1)}, u32[]{:S(2)}, u32[]{:S(2)}) %collective-permute-start.6) | collective-permute-done | bytes 73760 | tf_op jit(solution)/shard_map/ppermute | solution.py:61
  22.1 4.6 %shard_map.75 = (f32[16,3200]{1,0:T(8,128)S(1)}, bf16[16,3200]{1,0:T(8,128)(2,1)S(1)}, bf16[16,3200]{1,0:T(8,128)(2,1)S(1)}, bf16[16,3200]{1,0:T(8,128)(2,1)S(1)}) custom-call(bf16[16,4608]{1,0:T(8,128)(2,1)S(1)} %get-tuple-element.32.refs_0_, bf16[16,4608]{1,0:T(8,128)(2,1)S(1)} %collective-permute-done.3.refs_1_, ...), custom_call_target="tpu_custom_call" | custom-call | flops 1887436800 | bytes 29491200 | tf_op jit(solution)/shard_map/pallas_call | solution.py:30
  26.8 1.3 %collective-permute-start.8 = (bf16[16,3200]{1,0:T(8,128)(2,1)S(1)}, bf16[16,3200]{1,0:T(8,128)(2,1)S(1)}, u32[]{:S(2)}, u32[]{:S(2)}) collective-permute-start(bf16[16,3200]{1,0:T(8,128)(2,1)S(1)} %get-tuple-element.36), channel_id=1, source_target_pairs={{0,8},{4,12},{8,0},{12,4},{1,9},{5,13},{9,1},{13,5},{2,10},{6,14},... | collective-permute-start | bytes 307208 | tf_op jit(solution)/shard_map/ppermute | solution.py:56
  29.0 3.0 %collective-permute-done.8.refs_1_ = bf16[16,3200]{1,0:T(8,128)(2,1)S(1)} collective-permute-done((bf16[16,3200]{1,0:T(8,128)(2,1)S(1)}, bf16[16,3200]{1,0:T(8,128)(2,1)S(1)}, u32[]{:S(2)}, u32[]{:S(2)}) %collective-permute-start.8) | collective-permute-done | bytes 102432 | tf_op jit(solution)/shard_map/ppermute | solution.py:56
  33.2 2.5 %collective-permute-start.11 = (bf16[4,3200]{1,0:T(4,128)(2,1)S(1)}, bf16[4,3200]{1,0:T(4,128)(2,1)S(1)}, u32[]{:S(2)}, u32[]{:S(2)}) collective-permute-start(bf16[4,3200]{1,0:T(4,128)(2,1)S(1)} %get-tuple-element.40), channel_id=1, source_target_pairs={{0,2},{1,3},{2,0},{3,1},{4,6},{5,7},{6,4},{7,5},{8,10},{9,11},{10,... | collective-permute-start | bytes 76808 | tf_op jit(solution)/shard_map/ppermute | solution.py:56
  38.0 3.5 %collective-permute-done.12.refs_2_ = bf16[4,3200]{1,0:T(4,128)(2,1)S(1)} collective-permute-done((bf16[4,3200]{1,0:T(4,128)(2,1)S(1)}, bf16[4,3200]{1,0:T(4,128)(2,1)S(1)}, u32[]{:S(2)}, u32[]{:S(2)}) %collective-permute-start.12) | collective-permute-done | bytes 25632 | tf_op jit(solution)/shard_map/ppermute | solution.py:56
  41.6 1.8 %shard_map.77 = (bf16[4,3072]{1,0:T(4,128)(2,1)S(1)}, bf16[4,3072]{1,0:T(4,128)(2,1)S(1)}, bf16[4,3072]{1,0:T(4,128)(2,1)S(1)}, bf16[4,3072]{1,0:T(4,128)(2,1)S(1)}) custom-call(bf16[4,3200]{1,0:T(4,128)(2,1)S(1)} %get-tuple-element.39.refs_0_, bf16[4,3200]{1,0:T(4,128)(2,1)S(1)} %collective-permute-done.11.refs_1_, ...), custom_call_target="tpu_custom_call" | custom-call | flops 49999998976 | bytes 4194304 | tf_op jit(solution)/shard_map/pallas_call | solution.py:30
  43.4 1.9 %collective-permute-start.14 = (bf16[4,3072]{1,0:T(4,128)(2,1)S(1)}, bf16[4,3072]{1,0:T(4,128)(2,1)S(1)}, u32[]{:S(2)}, u32[]{:S(2)}) collective-permute-start(bf16[4,3072]{1,0:T(4,128)(2,1)S(1)} %get-tuple-element.44), channel_id=1, source_target_pairs={{0,3},{1,2},{2,1},{3,0},{4,7},{5,6},{6,5},{7,4},{8,11},{9,10},{10,... | collective-permute-start | bytes 73736 | tf_op jit(solution)/shard_map/ppermute | solution.py:56
  45.4 2.5 %collective-permute-start.16 = (bf16[4,3072]{1,0:T(4,128)(2,1)S(1)}, bf16[4,3072]{1,0:T(4,128)(2,1)S(1)}, u32[]{:S(2)}, u32[]{:S(2)}) collective-permute-start(bf16[4,3072]{1,0:T(4,128)(2,1)S(1)} %get-tuple-element.46), channel_id=1, source_target_pairs={{0,1},{1,0},{2,3},{3,2},{4,5},{5,4},{6,7},{7,6},{8,9},{9,8},{10,11... | collective-permute-start | bytes 73736 | tf_op jit(solution)/shard_map/ppermute | solution.py:56
  50.1 1.4 %collective-permute-start.18 = (bf16[16,3072]{1,0:T(8,128)(2,1)S(1)}, bf16[16,3072]{1,0:T(8,128)(2,1)S(1)}, u32[]{:S(2)}, u32[]{:S(2)}) collective-permute-start(bf16[16,3072]{1,0:T(8,128)(2,1)S(1)} %shard_map.78.refs_0_), channel_id=1, source_target_pairs={{0,8},{4,12},{8,0},{12,4},{1,9},{5,13},{9,1},{13,5},{2,10},{6,14},... | collective-permute-start | bytes 294920 | tf_op jit(solution)/shard_map/ppermute | solution.py:61
  51.5 3.3 %collective-permute-done.18.refs_2_ = bf16[16,3072]{1,0:T(8,128)(2,1)S(1)} collective-permute-done((bf16[16,3072]{1,0:T(8,128)(2,1)S(1)}, bf16[16,3072]{1,0:T(8,128)(2,1)S(1)}, u32[]{:S(2)}, u32[]{:S(2)}) %collective-permute-start.18) | collective-permute-done | bytes 98336 | tf_op jit(solution)/shard_map/ppermute | solution.py:61
  54.8 1.3 %collective-permute-done.19.refs_3_ = bf16[16,3072]{1,0:T(8,128)(2,1)S(1)} collective-permute-done((bf16[16,3072]{1,0:T(8,128)(2,1)S(1)}, bf16[16,3072]{1,0:T(8,128)(2,1)S(1)}, u32[]{:S(2)}, u32[]{:S(2)}) %collective-permute-start.19) | collective-permute-done | bytes 98336 | tf_op jit(solution)/shard_map/ppermute | solution.py:61
  56.2 5.0 %shard_map.79 = (f32[16,4608]{1,0:T(8,128)S(1)}, bf16[16,4608]{1,0:T(8,128)(2,1)S(1)}, bf16[16,4608]{1,0:T(8,128)(2,1)S(1)}, bf16[16,4608]{1,0:T(8,128)(2,1)S(1)}) custom-call(bf16[16,3072]{1,0:T(8,128)(2,1)S(1)} %shard_map.78.refs_0_, bf16[16,3072]{1,0:T(8,128)(2,1)S(1)} %collective-permute-done.17.refs_1_, ...), custom_call_target="tpu_custom_call" | custom-call | flops 1811939328 | bytes 28311552 | tf_op jit(solution)/shard_map/pallas_call | solution.py:30
  61.2 2.1 %collective-permute-start.20 = (bf16[16,4608]{1,0:T(8,128)(2,1)S(1)}, bf16[16,4608]{1,0:T(8,128)(2,1)S(1)}, u32[]{:S(2)}, u32[]{:S(2)}) collective-permute-start(bf16[16,4608]{1,0:T(8,128)(2,1)S(1)} %get-tuple-element.48), channel_id=1, source_target_pairs={{0,2},{1,3},{2,0},{3,1},{4,6},{5,7},{6,4},{7,5},{8,10},{9,11},{10,... | collective-permute-start | bytes 442376 | tf_op jit(solution)/shard_map/ppermute | solution.py:56
  63.8 1.9 %collective-permute-start.22 = (bf16[16,4608]{1,0:T(8,128)(2,1)S(1)}, bf16[16,4608]{1,0:T(8,128)(2,1)S(1)}, u32[]{:S(2)}, u32[]{:S(2)}) collective-permute-start(bf16[16,4608]{1,0:T(8,128)(2,1)S(1)} %get-tuple-element.50), channel_id=1, source_target_pairs={{0,3},{1,2},{2,1},{3,0},{4,7},{5,6},{6,5},{7,4},{8,11},{9,10},{10,... | collective-permute-start | bytes 442376 | tf_op jit(solution)/shard_map/ppermute | solution.py:56
  65.6 6.9 %collective-permute-done.20.refs_1_ = bf16[16,4608]{1,0:T(8,128)(2,1)S(1)} collective-permute-done((bf16[16,4608]{1,0:T(8,128)(2,1)S(1)}, bf16[16,4608]{1,0:T(8,128)(2,1)S(1)}, u32[]{:S(2)}, u32[]{:S(2)}) %collective-permute-start.20) | collective-permute-done | bytes 147488 | tf_op jit(solution)/shard_map/ppermute | solution.py:56
  72.5 3.1 %collective-permute-done.22.refs_3_ = bf16[16,4608]{1,0:T(8,128)(2,1)S(1)} collective-permute-done((bf16[16,4608]{1,0:T(8,128)(2,1)S(1)}, bf16[16,4608]{1,0:T(8,128)(2,1)S(1)}, u32[]{:S(2)}, u32[]{:S(2)}) %collective-permute-start.22) | collective-permute-done | bytes 147488 | tf_op jit(solution)/shard_map/ppermute | solution.py:56
  (53 shorter events, 12.4 us)
Async XLA Ops:
  1.7 39.9 %copy-start.1 = (bf16[4,1024,256]{2,1,0:T(8,128)(2,1)S(1)}, bf16[4,1024,256]{2,1,0:T(8,128)(2,1)}, u32[]{:S(2)}) copy-start(bf16[4,1024,256]{2,1,0:T(8,128)(2,1)} %refs_4_.2) | copy-start | bytes 6291460
  1.7 3.2 %collective-permute-start = (bf16[4,4608]{1,0:T(4,128)(2,1)S(1)}, bf16[4,4608]{1,0:T(4,128)(2,1)S(1)}, u32[]{:S(2)}, u32[]{:S(2)}) collective-permute-start(bf16[4,4608]{1,0:T(4,128)(2,1)S(1)} %get-tuple-element.29), channel_id=1, source_target_pairs={{0,4},{4,0},{8,12},{12,8},{1,5},{5,1},{9,13},{13,9},{2,6},{6,2},{1... | collective-permute-start | bytes 110600 | tf_op jit(solution)/shard_map/ppermute | solution.py:56
  2.2 4.4 %collective-permute-start.1 = (bf16[4,4608]{1,0:T(4,128)(2,1)S(1)}, bf16[4,4608]{1,0:T(4,128)(2,1)S(1)}, u32[]{:S(2)}, u32[]{:S(2)}) collective-permute-start(bf16[4,4608]{1,0:T(4,128)(2,1)S(1)} %get-tuple-element.30), channel_id=1, source_target_pairs={{0,12},{4,8},{8,4},{12,0},{1,13},{5,9},{9,5},{13,1},{2,14},{6,10},... | collective-permute-start | bytes 110600 | tf_op jit(solution)/shard_map/ppermute | solution.py:56
  4.8 4.0 %collective-permute-start.2 = (bf16[4,4608]{1,0:T(4,128)(2,1)S(1)}, bf16[4,4608]{1,0:T(4,128)(2,1)S(1)}, u32[]{:S(2)}, u32[]{:S(2)}) collective-permute-start(bf16[4,4608]{1,0:T(4,128)(2,1)S(1)} %get-tuple-element.31), channel_id=1, source_target_pairs={{0,8},{4,12},{8,0},{12,4},{1,9},{5,13},{9,1},{13,5},{2,10},{6,14},... | collective-permute-start | bytes 110600 | tf_op jit(solution)/shard_map/ppermute | solution.py:56
  8.8 7.6 %collective-permute-start.4 = (bf16[16,2304]{1,0:T(8,128)(2,1)S(1)}, bf16[16,2304]{1,0:T(8,128)(2,1)S(1)}, u32[]{:S(2)}, u32[]{:S(2)}) collective-permute-start(bf16[16,2304]{1,0:T(8,128)(2,1)S(1)} %get-tuple-element.33), channel_id=1, source_target_pairs={{0,2},{1,3},{2,0},{3,1},{4,6},{5,7},{6,4},{7,5},{8,10},{9,11},{10,... | collective-permute-start | bytes 221192 | tf_op jit(solution)/shard_map/ppermute | solution.py:61
  11.5 6.3 %collective-permute-start.5 = (bf16[16,2304]{1,0:T(8,128)(2,1)S(1)}, bf16[16,2304]{1,0:T(8,128)(2,1)S(1)}, u32[]{:S(2)}, u32[]{:S(2)}) collective-permute-start(bf16[16,2304]{1,0:T(8,128)(2,1)S(1)} %get-tuple-element.34), channel_id=1, source_target_pairs={{0,2},{1,3},{2,0},{3,1},{4,6},{5,7},{6,4},{7,5},{8,10},{9,11},{10,... | collective-permute-start | bytes 221192 | tf_op jit(solution)/shard_map/ppermute | solution.py:61
  11.8 10.3 %collective-permute-start.3 = (bf16[16,4608]{1,0:T(8,128)(2,1)S(1)}, bf16[16,4608]{1,0:T(8,128)(2,1)S(1)}, u32[]{:S(2)}, u32[]{:S(2)}) collective-permute-start(bf16[16,4608]{1,0:T(8,128)(2,1)S(1)} %get-tuple-element.32.refs_0_), channel_id=1, source_target_pairs={{0,1},{1,0},{2,3},{3,2},{4,5},{5,4},{6,7},{7,6},{8,9},{9,8},{10,11... | collective-permute-start | bytes 442376 | tf_op jit(solution)/shard_map/ppermute | solution.py:61
  16.4 4.7 %collective-permute-start.6 = (bf16[16,2304]{1,0:T(8,128)(2,1)S(1)}, bf16[16,2304]{1,0:T(8,128)(2,1)S(1)}, u32[]{:S(2)}, u32[]{:S(2)}) collective-permute-start(bf16[16,2304]{1,0:T(8,128)(2,1)S(1)} %collective-permute-done.4.refs_2_), channel_id=1, source_target_pairs={{0,1},{1,0},{2,3},{3,2},{4,5},{5,4},{6,7},{7,6},{8,9},{9,8},{10,11... | collective-permute-start | bytes 221192 | tf_op jit(solution)/shard_map/ppermute | solution.py:61
  17.7 4.4 %collective-permute-start.7 = (bf16[16,2304]{1,0:T(8,128)(2,1)S(1)}, bf16[16,2304]{1,0:T(8,128)(2,1)S(1)}, u32[]{:S(2)}, u32[]{:S(2)}) collective-permute-start(bf16[16,2304]{1,0:T(8,128)(2,1)S(1)} %collective-permute-done.5.refs_3_), channel_id=1, source_target_pairs={{0,1},{1,0},{2,3},{3,2},{4,5},{5,4},{6,7},{7,6},{8,9},{9,8},{10,11... | collective-permute-start | bytes 221192 | tf_op jit(solution)/shard_map/ppermute | solution.py:61
  26.8 5.2 %collective-permute-start.8 = (bf16[16,3200]{1,0:T(8,128)(2,1)S(1)}, bf16[16,3200]{1,0:T(8,128)(2,1)S(1)}, u32[]{:S(2)}, u32[]{:S(2)}) collective-permute-start(bf16[16,3200]{1,0:T(8,128)(2,1)S(1)} %get-tuple-element.36), channel_id=1, source_target_pairs={{0,8},{4,12},{8,0},{12,4},{1,9},{5,13},{9,1},{13,5},{2,10},{6,14},... | collective-permute-start | bytes 307208 | tf_op jit(solution)/shard_map/ppermute | solution.py:56
  28.0 4.0 %collective-permute-start.9 = (bf16[16,3200]{1,0:T(8,128)(2,1)S(1)}, bf16[16,3200]{1,0:T(8,128)(2,1)S(1)}, u32[]{:S(2)}, u32[]{:S(2)}) collective-permute-start(bf16[16,3200]{1,0:T(8,128)(2,1)S(1)} %get-tuple-element.37), channel_id=1, source_target_pairs={{0,4},{4,0},{8,12},{12,8},{1,5},{5,1},{9,13},{13,9},{2,6},{6,2},{1... | collective-permute-start | bytes 307208 | tf_op jit(solution)/shard_map/ppermute | solution.py:56
  28.0 5.1 %collective-permute-start.10 = (bf16[16,3200]{1,0:T(8,128)(2,1)S(1)}, bf16[16,3200]{1,0:T(8,128)(2,1)S(1)}, u32[]{:S(2)}, u32[]{:S(2)}) collective-permute-start(bf16[16,3200]{1,0:T(8,128)(2,1)S(1)} %get-tuple-element.38), channel_id=1, source_target_pairs={{0,12},{4,8},{8,4},{12,0},{1,13},{5,9},{9,5},{13,1},{2,14},{6,10},... | collective-permute-start | bytes 307208 | tf_op jit(solution)/shard_map/ppermute | solution.py:56
  33.2 4.8 %collective-permute-start.11 = (bf16[4,3200]{1,0:T(4,128)(2,1)S(1)}, bf16[4,3200]{1,0:T(4,128)(2,1)S(1)}, u32[]{:S(2)}, u32[]{:S(2)}) collective-permute-start(bf16[4,3200]{1,0:T(4,128)(2,1)S(1)} %get-tuple-element.40), channel_id=1, source_target_pairs={{0,2},{1,3},{2,0},{3,1},{4,6},{5,7},{6,4},{7,5},{8,10},{9,11},{10,... | collective-permute-start | bytes 76808 | tf_op jit(solution)/shard_map/ppermute | solution.py:56
  35.8 5.8 %collective-permute-start.12 = (bf16[4,3200]{1,0:T(4,128)(2,1)S(1)}, bf16[4,3200]{1,0:T(4,128)(2,1)S(1)}, u32[]{:S(2)}, u32[]{:S(2)}) collective-permute-start(bf16[4,3200]{1,0:T(4,128)(2,1)S(1)} %get-tuple-element.41), channel_id=1, source_target_pairs={{0,3},{1,2},{2,1},{3,0},{4,7},{5,6},{6,5},{7,4},{8,11},{9,10},{10,... | collective-permute-start | bytes 76808 | tf_op jit(solution)/shard_map/ppermute | solution.py:56
  36.9 4.7 %collective-permute-start.13 = (bf16[4,3200]{1,0:T(4,128)(2,1)S(1)}, bf16[4,3200]{1,0:T(4,128)(2,1)S(1)}, u32[]{:S(2)}, u32[]{:S(2)}) collective-permute-start(bf16[4,3200]{1,0:T(4,128)(2,1)S(1)} %get-tuple-element.42), channel_id=1, source_target_pairs={{0,1},{1,0},{2,3},{3,2},{4,5},{5,4},{6,7},{7,6},{8,9},{9,8},{10,11... | collective-permute-start | bytes 76808 | tf_op jit(solution)/shard_map/ppermute | solution.py:56
  43.4 5.7 %collective-permute-start.14 = (bf16[4,3072]{1,0:T(4,128)(2,1)S(1)}, bf16[4,3072]{1,0:T(4,128)(2,1)S(1)}, u32[]{:S(2)}, u32[]{:S(2)}) collective-permute-start(bf16[4,3072]{1,0:T(4,128)(2,1)S(1)} %get-tuple-element.44), channel_id=1, source_target_pairs={{0,3},{1,2},{2,1},{3,0},{4,7},{5,6},{6,5},{7,4},{8,11},{9,10},{10,... | collective-permute-start | bytes 73736 | tf_op jit(solution)/shard_map/ppermute | solution.py:56
  45.4 4.7 %collective-permute-start.15 = (bf16[4,3072]{1,0:T(4,128)(2,1)S(1)}, bf16[4,3072]{1,0:T(4,128)(2,1)S(1)}, u32[]{:S(2)}, u32[]{:S(2)}) collective-permute-start(bf16[4,3072]{1,0:T(4,128)(2,1)S(1)} %get-tuple-element.45), channel_id=1, source_target_pairs={{0,2},{1,3},{2,0},{3,1},{4,6},{5,7},{6,4},{7,5},{8,10},{9,11},{10,... | collective-permute-start | bytes 73736 | tf_op jit(solution)/shard_map/ppermute | solution.py:56
  45.4 4.7 %collective-permute-start.16 = (bf16[4,3072]{1,0:T(4,128)(2,1)S(1)}, bf16[4,3072]{1,0:T(4,128)(2,1)S(1)}, u32[]{:S(2)}, u32[]{:S(2)}) collective-permute-start(bf16[4,3072]{1,0:T(4,128)(2,1)S(1)} %get-tuple-element.46), channel_id=1, source_target_pairs={{0,1},{1,0},{2,3},{3,2},{4,5},{5,4},{6,7},{7,6},{8,9},{9,8},{10,11... | collective-permute-start | bytes 73736 | tf_op jit(solution)/shard_map/ppermute | solution.py:56
  50.1 4.7 %collective-permute-start.18 = (bf16[16,3072]{1,0:T(8,128)(2,1)S(1)}, bf16[16,3072]{1,0:T(8,128)(2,1)S(1)}, u32[]{:S(2)}, u32[]{:S(2)}) collective-permute-start(bf16[16,3072]{1,0:T(8,128)(2,1)S(1)} %shard_map.78.refs_0_), channel_id=1, source_target_pairs={{0,8},{4,12},{8,0},{12,4},{1,9},{5,13},{9,1},{13,5},{2,10},{6,14},... | collective-permute-start | bytes 294920 | tf_op jit(solution)/shard_map/ppermute | solution.py:61
  51.5 3.3 %collective-permute-start.17 = (bf16[16,3072]{1,0:T(8,128)(2,1)S(1)}, bf16[16,3072]{1,0:T(8,128)(2,1)S(1)}, u32[]{:S(2)}, u32[]{:S(2)}) collective-permute-start(bf16[16,3072]{1,0:T(8,128)(2,1)S(1)} %shard_map.78.refs_0_), channel_id=1, source_target_pairs={{0,4},{4,0},{8,12},{12,8},{1,5},{5,1},{9,13},{13,9},{2,6},{6,2},{1... | collective-permute-start | bytes 294920 | tf_op jit(solution)/shard_map/ppermute | solution.py:61
  54.8 1.3 %collective-permute-start.19 = (bf16[16,3072]{1,0:T(8,128)(2,1)S(1)}, bf16[16,3072]{1,0:T(8,128)(2,1)S(1)}, u32[]{:S(2)}, u32[]{:S(2)}) collective-permute-start(bf16[16,3072]{1,0:T(8,128)(2,1)S(1)} %collective-permute-done.18.refs_2_), channel_id=1, source_target_pairs={{0,4},{4,0},{8,12},{12,8},{1,5},{5,1},{9,13},{13,9},{2,6},{6,2},{1... | collective-permute-start | bytes 294920 | tf_op jit(solution)/shard_map/ppermute | solution.py:61
  61.2 11.3 %collective-permute-start.20 = (bf16[16,4608]{1,0:T(8,128)(2,1)S(1)}, bf16[16,4608]{1,0:T(8,128)(2,1)S(1)}, u32[]{:S(2)}, u32[]{:S(2)}) collective-permute-start(bf16[16,4608]{1,0:T(8,128)(2,1)S(1)} %get-tuple-element.48), channel_id=1, source_target_pairs={{0,2},{1,3},{2,0},{3,1},{4,6},{5,7},{6,4},{7,5},{8,10},{9,11},{10,... | collective-permute-start | bytes 442376 | tf_op jit(solution)/shard_map/ppermute | solution.py:56
  63.2 9.2 %collective-permute-start.21 = (bf16[16,4608]{1,0:T(8,128)(2,1)S(1)}, bf16[16,4608]{1,0:T(8,128)(2,1)S(1)}, u32[]{:S(2)}, u32[]{:S(2)}) collective-permute-start(bf16[16,4608]{1,0:T(8,128)(2,1)S(1)} %get-tuple-element.49), channel_id=1, source_target_pairs={{0,1},{1,0},{2,3},{3,2},{4,5},{5,4},{6,7},{7,6},{8,9},{9,8},{10,11... | collective-permute-start | bytes 442376 | tf_op jit(solution)/shard_map/ppermute | solution.py:56
  63.8 11.8 %collective-permute-start.22 = (bf16[16,4608]{1,0:T(8,128)(2,1)S(1)}, bf16[16,4608]{1,0:T(8,128)(2,1)S(1)}, u32[]{:S(2)}, u32[]{:S(2)}) collective-permute-start(bf16[16,4608]{1,0:T(8,128)(2,1)S(1)} %get-tuple-element.50), channel_id=1, source_target_pairs={{0,3},{1,2},{2,1},{3,0},{4,7},{5,6},{6,5},{7,4},{8,11},{9,10},{10,... | collective-permute-start | bytes 442376 | tf_op jit(solution)/shard_map/ppermute | solution.py:56
  (10 other events, 178.3 us)

commit v5 on v4

--- a/solution.py
+++ b/solution.py
@@ -13,7 +13,8 @@
 MIB = 1 << 20
 A1 = (0, 1, 3, 2)
 A2 = (0, 1, 2, 3, 4, 5)
-B1 = (0, 2, 1, 3)
+B1 = (0, 1, 2)
+WIDE = jnp.float32
 B2 = (0, 2, 3, 1)
 C1 = (0, 3, 2, 1)
 C2 = (0, 1, 2, 3)
@@ -108,9 +109,9 @@
         out[...] = group.astype(out.dtype)
 
 
-def dot(pieces, w, order=()):
+def dot(pieces, w, kept=(0,), order=()):
     n, rows, (depth, width) = len(pieces), pieces[0][0].shape[0], w.shape
-    outs = [struct((rows, width), jnp.bfloat16 if k else jnp.float32) for k in range(n)]
+    outs = [struct((rows, width), jnp.float32 if k in kept else jnp.bfloat16) for k in range(n)]
     ins = [part for piece in pieces for part in piece]
     return call(
         functools.partial(dot_body, [len(piece) for piece in pieces]),
@@ -124,8 +125,12 @@
     )
 
 
+def add_body(kept, received, out):
+    out[...] = (kept[...] + received[...]).astype(out.dtype)
+
+
 def total_body(*refs):
-    ins, outs = refs[: len(refs) // 2], refs[len(refs) // 2 :]
+    ins, outs = refs[:3], refs[3:]
     total = ins[0][...]
     for r in ins[1:]:
         total = total + r[...].astype(jnp.float32)
@@ -254,10 +259,14 @@
     one = swap(mine, "yz", 1)
     two = [swap(part, "yz", 2) for part in halves]
     three = [swap(part, "yz", 1) for part in two]
-    sums = dot([[mine], [one], two, three], w_qkv, order=A2)
-    sums = exchange(sums, "gx")
+    own, one, two, three = dot([[mine], [one], two, three], w_qkv, kept=(0, 1, 2, 3), order=A2)
+    two = call(add_body, struct(two.shape, WIDE), [VMEM] * 2, [two, swap(three, "gx", 1)])
     parts = call(
-        total_body, [struct((seqs, w_qkv.shape[1]))] * blocks, [VMEM] * groups, sums, order=B1
+        total_body,
+        [struct((seqs, w_qkv.shape[1]))] * blocks,
+        [VMEM] * 3,
+        [own, swap(two, "gx", 2), swap(one, "gx", 1)],
+        order=B1,
     )
     attended = attend(exchange(parts, "yz"), cache_keys, cache_values, cache_lengths, width)
     got = exchange(attended, "yz")

time: 76.4 us -> 79 us (1.034)
  waiting for transfers between devices: 36 us -> 39.6 us
  starting transfers between devices: 26.1 us -> 25.2 us
    ppermute x8 -> x11, waiting for transfers between devices: 11.6 us -> 19.1 us  [swap(): lax.ppermute(piece, axis, [(i, i ^ k) for i in range(lax.axis_size(axis))])]
    ppermute x15 -> x12, waiting for transfers between devices: 24.4 us -> 20.4 us  [exchange(): lax.ppermute(pieces[k], axis, [(i, i ^ k) for i in range(size)])]
    ppermute x15 -> x12, starting transfers between devices: 18.4 us -> 16.4 us  [exchange(): lax.ppermute(pieces[k], axis, [(i, i ^ k) for i in range(size)])]
    ppermute x8 -> x11, starting transfers between devices: 7.64 us -> 8.83 us  [swap(): lax.ppermute(piece, axis, [(i, i ^ k) for i in range(lax.axis_size(axis))])]
    pallas_call x8 -> x9, Pallas kernels: 13.9 us -> 13.9 us  [call(): pl.pallas_call(ordered, out_shape=outs, in_specs=[in_specs[i] for i in or...]
where the time goes in v5:
time: 79 us; the launch traced here: 78.9 us
  waiting for transfers between devices  39.6 us (50%)
  starting transfers between devices  25.2 us (32%)
  Pallas kernels  13.9 us (18%)
    ppermute x12, waiting for transfers between devices, exchange(): lax.ppermute(pieces[k], axis, [(i, i ^ k) for i in range(size)])  20.4 us
    ppermute x11, waiting for transfers between devices, swap(): lax.ppermute(piece, axis, [(i, i ^ k) for i in range(lax.axis_size(axis))])  19.1 us
    ppermute x12, starting transfers between devices, exchange(): lax.ppermute(pieces[k], axis, [(i, i ^ k) for i in range(size)])  16.4 us
    pallas_call x9, Pallas kernels, call(): pl.pallas_call(ordered, out_shape=outs, in_specs=[in_specs[i] for i in or...  13.9 us
    ppermute x11, starting transfers between devices, swap(): lax.ppermute(piece, axis, [(i, i ^ k) for i in range(lax.axis_size(axis))])  8.83 us
  transfers between devices with their start and end apart: 23, of which 16 were waited for; matrix products, arithmetic and copies ran while one was open for 0% of the time, Pallas kernels for 0%

profile of v5, /device:TPU:0, one launch (start us, length us, event | category | flops | bytes accessed | tf_op | source)
XLA Modules:
  0.0 78.9 jit_solution(13720899666789034679)
XLA Ops:
  0.0 1.6 %shard_map.73 = (bf16[4,4608]{1,0:T(4,128)(2,1)S(1)}, bf16[4,4608]{1,0:T(4,128)(2,1)S(1)}, bf16[4,4608]{1,0:T(4,128)(2,1)S(1)}, bf16[4,4608]{1,0:T(4,128)(2,1)S(1)}) custom-call(bf16[4,18432]{1,0:T(4,128)(2,1)} %refs_0_.1, f32[1,18432]{1,0:T(1,128)} %bitcast.3), custom_call_target="tpu_custom_call" | custom-call | flops 49999998976 | tf_op jit(solution)/shard_map/pallas_call | solution.py:31
  2.2 2.6 %collective-permute-start.1 = (bf16[4,4608]{1,0:T(4,128)(2,1)S(1)}, bf16[4,4608]{1,0:T(4,128)(2,1)S(1)}, u32[]{:S(2)}, u32[]{:S(2)}) collective-permute-start(bf16[4,4608]{1,0:T(4,128)(2,1)S(1)} %get-tuple-element.30), channel_id=1, source_target_pairs={{0,12},{4,8},{8,4},{12,0},{1,13},{5,9},{9,5},{13,1},{2,14},{6,10},... | collective-permute-start | bytes 110600 | tf_op jit(solution)/shard_map/ppermute | solution.py:57
  4.9 1.7 %collective-permute-done.1.refs_2_ = bf16[4,4608]{1,0:T(4,128)(2,1)S(1)} collective-permute-done((bf16[4,4608]{1,0:T(4,128)(2,1)S(1)}, bf16[4,4608]{1,0:T(4,128)(2,1)S(1)}, u32[]{:S(2)}, u32[]{:S(2)}) %collective-permute-start.1) | collective-permute-done | bytes 36896 | tf_op jit(solution)/shard_map/ppermute | solution.py:57
  6.6 2.2 %collective-permute-done.2.refs_3_ = bf16[4,4608]{1,0:T(4,128)(2,1)S(1)} collective-permute-done((bf16[4,4608]{1,0:T(4,128)(2,1)S(1)}, bf16[4,4608]{1,0:T(4,128)(2,1)S(1)}, u32[]{:S(2)}, u32[]{:S(2)}) %collective-permute-start.2) | collective-permute-done | bytes 36896 | tf_op jit(solution)/shard_map/ppermute | solution.py:57
  8.8 2.7 %collective-permute-start.4 = (bf16[16,2304]{1,0:T(8,128)(2,1)S(1)}, bf16[16,2304]{1,0:T(8,128)(2,1)S(1)}, u32[]{:S(2)}, u32[]{:S(2)}) collective-permute-start(bf16[16,2304]{1,0:T(8,128)(2,1)S(1)} %get-tuple-element.33), channel_id=1, source_target_pairs={{0,2},{1,3},{2,0},{3,1},{4,6},{5,7},{6,4},{7,5},{8,10},{9,11},{10,... | collective-permute-start | bytes 221192 | tf_op jit(solution)/shard_map/ppermute | solution.py:62
  11.8 1.6 %collective-permute-start.3 = (bf16[16,4608]{1,0:T(8,128)(2,1)S(1)}, bf16[16,4608]{1,0:T(8,128)(2,1)S(1)}, u32[]{:S(2)}, u32[]{:S(2)}) collective-permute-start(bf16[16,4608]{1,0:T(8,128)(2,1)S(1)} %get-tuple-element.32.refs_0_), channel_id=1, source_target_pairs={{0,1},{1,0},{2,3},{3,2},{4,5},{5,4},{6,7},{7,6},{8,9},{9,8},{10,11... | collective-permute-start | bytes 442376 | tf_op jit(solution)/shard_map/ppermute | solution.py:62
  13.4 3.0 %collective-permute-done.4.refs_2_ = bf16[16,2304]{1,0:T(8,128)(2,1)S(1)} collective-permute-done((bf16[16,2304]{1,0:T(8,128)(2,1)S(1)}, bf16[16,2304]{1,0:T(8,128)(2,1)S(1)}, u32[]{:S(2)}, u32[]{:S(2)}) %collective-permute-start.4) | collective-permute-done | bytes 73760 | tf_op jit(solution)/shard_map/ppermute | solution.py:62
  18.9 2.2 %collective-permute-done.6.refs_4_ = bf16[16,2304]{1,0:T(8,128)(2,1)S(1)} collective-permute-done((bf16[16,2304]{1,0:T(8,128)(2,1)S(1)}, bf16[16,2304]{1,0:T(8,128)(2,1)S(1)}, u32[]{:S(2)}, u32[]{:S(2)}) %collective-permute-start.6) | collective-permute-done | bytes 73760 | tf_op jit(solution)/shard_map/ppermute | solution.py:62
  22.1 4.6 %shard_map.75 = (f32[16,3200]{1,0:T(8,128)S(1)}, f32[16,3200]{1,0:T(8,128)S(1)}, f32[16,3200]{1,0:T(8,128)S(1)}, f32[16,3200]{1,0:T(8,128)S(1)}) custom-call(bf16[16,4608]{1,0:T(8,128)(2,1)S(1)} %get-tuple-element.32.refs_0_, bf16[16,4608]{1,0:T(8,128)(2,1)S(1)} %collective-permute-done.3.refs_1_, bf16[16,2304]{1,0:T(8,128)(2,1)S(1)} %collective-permute-done.4.refs_2_, ...), custom_call_target="tpu_custom_call" | custom-call | flops 1887436800 | bytes 29491200 | tf_op jit(solution)/shard_map/pallas_call | solution.py:31
  28.2 1.3 %collective-permute-start.9 = (f32[16,3200]{1,0:T(8,128)S(1)}, f32[16,3200]{1,0:T(8,128)S(1)}, u32[]{:S(2)}, u32[]{:S(2)}) collective-permute-start(f32[16,3200]{1,0:T(8,128)S(1)} %shard_map.76), channel_id=1, source_target_pairs={{0,8},{4,12},{8,0},{12,4},{1,9},{5,13},{9,1},{13,5},{2,10},{6,14},... | collective-permute-start | bytes 614408 | tf_op jit(solution)/shard_map/ppermute | solution.py:62
  29.5 5.9 %collective-permute-done.9.refs_1_ = f32[16,3200]{1,0:T(8,128)S(1)} collective-permute-done((f32[16,3200]{1,0:T(8,128)S(1)}, f32[16,3200]{1,0:T(8,128)S(1)}, u32[]{:S(2)}, u32[]{:S(2)}) %collective-permute-start.9) | collective-permute-done | bytes 204832 | tf_op jit(solution)/shard_map/ppermute | solution.py:62
  35.5 3.1 %collective-permute-start.11 = (bf16[4,3200]{1,0:T(4,128)(2,1)S(1)}, bf16[4,3200]{1,0:T(4,128)(2,1)S(1)}, u32[]{:S(2)}, u32[]{:S(2)}) collective-permute-start(bf16[4,3200]{1,0:T(4,128)(2,1)S(1)} %get-tuple-element.40), channel_id=1, source_target_pairs={{0,2},{1,3},{2,0},{3,1},{4,6},{5,7},{6,4},{7,5},{8,10},{9,11},{10,... | collective-permute-start | bytes 76808 | tf_op jit(solution)/shard_map/ppermute | solution.py:57
  40.3 3.8 %collective-permute-done.12.refs_2_ = bf16[4,3200]{1,0:T(4,128)(2,1)S(1)} collective-permute-done((bf16[4,3200]{1,0:T(4,128)(2,1)S(1)}, bf16[4,3200]{1,0:T(4,128)(2,1)S(1)}, u32[]{:S(2)}, u32[]{:S(2)}) %collective-permute-start.12) | collective-permute-done | bytes 25632 | tf_op jit(solution)/shard_map/ppermute | solution.py:57
  44.2 1.8 %shard_map.78 = (bf16[4,3072]{1,0:T(4,128)(2,1)S(1)}, bf16[4,3072]{1,0:T(4,128)(2,1)S(1)}, bf16[4,3072]{1,0:T(4,128)(2,1)S(1)}, bf16[4,3072]{1,0:T(4,128)(2,1)S(1)}) custom-call(bf16[4,3200]{1,0:T(4,128)(2,1)S(1)} %get-tuple-element.39.refs_0_, bf16[4,3200]{1,0:T(4,128)(2,1)S(1)} %collective-permute-done.11.refs_1_, ...), custom_call_target="tpu_custom_call" | custom-call | flops 49999998976 | bytes 4194304 | tf_op jit(solution)/shard_map/pallas_call | solution.py:31
  46.0 2.1 %collective-permute-start.14 = (bf16[4,3072]{1,0:T(4,128)(2,1)S(1)}, bf16[4,3072]{1,0:T(4,128)(2,1)S(1)}, u32[]{:S(2)}, u32[]{:S(2)}) collective-permute-start(bf16[4,3072]{1,0:T(4,128)(2,1)S(1)} %get-tuple-element.44), channel_id=1, source_target_pairs={{0,3},{1,2},{2,1},{3,0},{4,7},{5,6},{6,5},{7,4},{8,11},{9,10},{10,... | collective-permute-start | bytes 73736 | tf_op jit(solution)/shard_map/ppermute | solution.py:57
  48.1 2.4 %collective-permute-start.16 = (bf16[4,3072]{1,0:T(4,128)(2,1)S(1)}, bf16[4,3072]{1,0:T(4,128)(2,1)S(1)}, u32[]{:S(2)}, u32[]{:S(2)}) collective-permute-start(bf16[4,3072]{1,0:T(4,128)(2,1)S(1)} %get-tuple-element.46), channel_id=1, source_target_pairs={{0,1},{1,0},{2,3},{3,2},{4,5},{5,4},{6,7},{7,6},{8,9},{9,8},{10,11... | collective-permute-start | bytes 73736 | tf_op jit(solution)/shard_map/ppermute | solution.py:57
  50.5 1.2 %collective-permute-done.14.refs_1_ = bf16[4,3072]{1,0:T(4,128)(2,1)S(1)} collective-permute-done((bf16[4,3072]{1,0:T(4,128)(2,1)S(1)}, bf16[4,3072]{1,0:T(4,128)(2,1)S(1)}, u32[]{:S(2)}, u32[]{:S(2)}) %collective-permute-start.14) | collective-permute-done | bytes 24608 | tf_op jit(solution)/shard_map/ppermute | solution.py:57
  53.6 4.0 %collective-permute-done.18.refs_2_ = bf16[16,3072]{1,0:T(8,128)(2,1)S(1)} collective-permute-done((bf16[16,3072]{1,0:T(8,128)(2,1)S(1)}, bf16[16,3072]{1,0:T(8,128)(2,1)S(1)}, u32[]{:S(2)}, u32[]{:S(2)}) %collective-permute-start.18) | collective-permute-done | bytes 98336 | tf_op jit(solution)/shard_map/ppermute | solution.py:62
  57.6 1.3 %collective-permute-done.19.refs_3_ = bf16[16,3072]{1,0:T(8,128)(2,1)S(1)} collective-permute-done((bf16[16,3072]{1,0:T(8,128)(2,1)S(1)}, bf16[16,3072]{1,0:T(8,128)(2,1)S(1)}, u32[]{:S(2)}, u32[]{:S(2)}) %collective-permute-start.19) | collective-permute-done | bytes 98336 | tf_op jit(solution)/shard_map/ppermute | solution.py:62
  59.0 5.0 %shard_map.80 = (f32[16,4608]{1,0:T(8,128)S(1)}, bf16[16,4608]{1,0:T(8,128)(2,1)S(1)}, bf16[16,4608]{1,0:T(8,128)(2,1)S(1)}, bf16[16,4608]{1,0:T(8,128)(2,1)S(1)}) custom-call(bf16[16,3072]{1,0:T(8,128)(2,1)S(1)} %shard_map.79.refs_0_, bf16[16,3072]{1,0:T(8,128)(2,1)S(1)} %collective-permute-done.17.refs_1_, ...), custom_call_target="tpu_custom_call" | custom-call | flops 1811939328 | bytes 28311552 | tf_op jit(solution)/shard_map/pallas_call | solution.py:31
  63.9 2.1 %collective-permute-start.20 = (bf16[16,4608]{1,0:T(8,128)(2,1)S(1)}, bf16[16,4608]{1,0:T(8,128)(2,1)S(1)}, u32[]{:S(2)}, u32[]{:S(2)}) collective-permute-start(bf16[16,4608]{1,0:T(8,128)(2,1)S(1)} %get-tuple-element.48), channel_id=1, source_target_pairs={{0,2},{1,3},{2,0},{3,1},{4,6},{5,7},{6,4},{7,5},{8,10},{9,11},{10,... | collective-permute-start | bytes 442376 | tf_op jit(solution)/shard_map/ppermute | solution.py:57
  66.4 2.0 %collective-permute-start.22 = (bf16[16,4608]{1,0:T(8,128)(2,1)S(1)}, bf16[16,4608]{1,0:T(8,128)(2,1)S(1)}, u32[]{:S(2)}, u32[]{:S(2)}) collective-permute-start(bf16[16,4608]{1,0:T(8,128)(2,1)S(1)} %get-tuple-element.50), channel_id=1, source_target_pairs={{0,3},{1,2},{2,1},{3,0},{4,7},{5,6},{6,5},{7,4},{8,11},{9,10},{10,... | collective-permute-start | bytes 442376 | tf_op jit(solution)/shard_map/ppermute | solution.py:57
  68.4 7.0 %collective-permute-done.20.refs_1_ = bf16[16,4608]{1,0:T(8,128)(2,1)S(1)} collective-permute-done((bf16[16,4608]{1,0:T(8,128)(2,1)S(1)}, bf16[16,4608]{1,0:T(8,128)(2,1)S(1)}, u32[]{:S(2)}, u32[]{:S(2)}) %collective-permute-start.20) | collective-permute-done | bytes 147488 | tf_op jit(solution)/shard_map/ppermute | solution.py:57
  75.4 2.8 %collective-permute-done.22.refs_3_ = bf16[16,4608]{1,0:T(8,128)(2,1)S(1)} collective-permute-done((bf16[16,4608]{1,0:T(8,128)(2,1)S(1)}, bf16[16,4608]{1,0:T(8,128)(2,1)S(1)}, u32[]{:S(2)}, u32[]{:S(2)}) %collective-permute-start.22) | collective-permute-done | bytes 147488 | tf_op jit(solution)/shard_map/ppermute | solution.py:57
  (54 shorter events, 10.9 us)
Async XLA Ops:
  1.7 42.5 %copy-start.1 = (bf16[4,1024,256]{2,1,0:T(8,128)(2,1)S(1)}, bf16[4,1024,256]{2,1,0:T(8,128)(2,1)}, u32[]{:S(2)}) copy-start(bf16[4,1024,256]{2,1,0:T(8,128)(2,1)} %refs_4_.2) | copy-start | bytes 6291460
  1.7 3.2 %collective-permute-start = (bf16[4,4608]{1,0:T(4,128)(2,1)S(1)}, bf16[4,4608]{1,0:T(4,128)(2,1)S(1)}, u32[]{:S(2)}, u32[]{:S(2)}) collective-permute-start(bf16[4,4608]{1,0:T(4,128)(2,1)S(1)} %get-tuple-element.29), channel_id=1, source_target_pairs={{0,4},{4,0},{8,12},{12,8},{1,5},{5,1},{9,13},{13,9},{2,6},{6,2},{1... | collective-permute-start | bytes 110600 | tf_op jit(solution)/shard_map/ppermute | solution.py:57
  2.2 4.4 %collective-permute-start.1 = (bf16[4,4608]{1,0:T(4,128)(2,1)S(1)}, bf16[4,4608]{1,0:T(4,128)(2,1)S(1)}, u32[]{:S(2)}, u32[]{:S(2)}) collective-permute-start(bf16[4,4608]{1,0:T(4,128)(2,1)S(1)} %get-tuple-element.30), channel_id=1, source_target_pairs={{0,12},{4,8},{8,4},{12,0},{1,13},{5,9},{9,5},{13,1},{2,14},{6,10},... | collective-permute-start | bytes 110600 | tf_op jit(solution)/shard_map/ppermute | solution.py:57
  4.8 4.0 %collective-permute-start.2 = (bf16[4,4608]{1,0:T(4,128)(2,1)S(1)}, bf16[4,4608]{1,0:T(4,128)(2,1)S(1)}, u32[]{:S(2)}, u32[]{:S(2)}) collective-permute-start(bf16[4,4608]{1,0:T(4,128)(2,1)S(1)} %get-tuple-element.31), channel_id=1, source_target_pairs={{0,8},{4,12},{8,0},{12,4},{1,9},{5,13},{9,1},{13,5},{2,10},{6,14},... | collective-permute-start | bytes 110600 | tf_op jit(solution)/shard_map/ppermute | solution.py:57
  8.8 7.6 %collective-permute-start.4 = (bf16[16,2304]{1,0:T(8,128)(2,1)S(1)}, bf16[16,2304]{1,0:T(8,128)(2,1)S(1)}, u32[]{:S(2)}, u32[]{:S(2)}) collective-permute-start(bf16[16,2304]{1,0:T(8,128)(2,1)S(1)} %get-tuple-element.33), channel_id=1, source_target_pairs={{0,2},{1,3},{2,0},{3,1},{4,6},{5,7},{6,4},{7,5},{8,10},{9,11},{10,... | collective-permute-start | bytes 221192 | tf_op jit(solution)/shard_map/ppermute | solution.py:62
  11.5 6.3 %collective-permute-start.5 = (bf16[16,2304]{1,0:T(8,128)(2,1)S(1)}, bf16[16,2304]{1,0:T(8,128)(2,1)S(1)}, u32[]{:S(2)}, u32[]{:S(2)}) collective-permute-start(bf16[16,2304]{1,0:T(8,128)(2,1)S(1)} %get-tuple-element.34), channel_id=1, source_target_pairs={{0,2},{1,3},{2,0},{3,1},{4,6},{5,7},{6,4},{7,5},{8,10},{9,11},{10,... | collective-permute-start | bytes 221192 | tf_op jit(solution)/shard_map/ppermute | solution.py:62
  11.8 10.3 %collective-permute-start.3 = (bf16[16,4608]{1,0:T(8,128)(2,1)S(1)}, bf16[16,4608]{1,0:T(8,128)(2,1)S(1)}, u32[]{:S(2)}, u32[]{:S(2)}) collective-permute-start(bf16[16,4608]{1,0:T(8,128)(2,1)S(1)} %get-tuple-element.32.refs_0_), channel_id=1, source_target_pairs={{0,1},{1,0},{2,3},{3,2},{4,5},{5,4},{6,7},{7,6},{8,9},{9,8},{10,11... | collective-permute-start | bytes 442376 | tf_op jit(solution)/shard_map/ppermute | solution.py:62
  16.4 4.7 %collective-permute-start.6 = (bf16[16,2304]{1,0:T(8,128)(2,1)S(1)}, bf16[16,2304]{1,0:T(8,128)(2,1)S(1)}, u32[]{:S(2)}, u32[]{:S(2)}) collective-permute-start(bf16[16,2304]{1,0:T(8,128)(2,1)S(1)} %collective-permute-done.4.refs_2_), channel_id=1, source_target_pairs={{0,1},{1,0},{2,3},{3,2},{4,5},{5,4},{6,7},{7,6},{8,9},{9,8},{10,11... | collective-permute-start | bytes 221192 | tf_op jit(solution)/shard_map/ppermute | solution.py:62
  17.7 4.4 %collective-permute-start.7 = (bf16[16,2304]{1,0:T(8,128)(2,1)S(1)}, bf16[16,2304]{1,0:T(8,128)(2,1)S(1)}, u32[]{:S(2)}, u32[]{:S(2)}) collective-permute-start(bf16[16,2304]{1,0:T(8,128)(2,1)S(1)} %collective-permute-done.5.refs_3_), channel_id=1, source_target_pairs={{0,1},{1,0},{2,3},{3,2},{4,5},{5,4},{6,7},{7,6},{8,9},{9,8},{10,11... | collective-permute-start | bytes 221192 | tf_op jit(solution)/shard_map/ppermute | solution.py:62
  26.7 1.5 %collective-permute-start.8 = (f32[16,3200]{1,0:T(8,128)S(1)}, f32[16,3200]{1,0:T(8,128)S(1)}, u32[]{:S(2)}, u32[]{:S(2)}) collective-permute-start(f32[16,3200]{1,0:T(8,128)S(1)} %get-tuple-element.37), channel_id=1, source_target_pairs={{0,4},{4,0},{8,12},{12,8},{1,5},{5,1},{9,13},{13,9},{2,6},{6,2},{1... | collective-permute-start | bytes 614408 | tf_op jit(solution)/shard_map/ppermute | solution.py:62
  26.8 2.7 %collective-permute-start.10 = (f32[16,3200]{1,0:T(8,128)S(1)}, f32[16,3200]{1,0:T(8,128)S(1)}, u32[]{:S(2)}, u32[]{:S(2)}) collective-permute-start(f32[16,3200]{1,0:T(8,128)S(1)} %get-tuple-element.38), channel_id=1, source_target_pairs={{0,4},{4,0},{8,12},{12,8},{1,5},{5,1},{9,13},{13,9},{2,6},{6,2},{1... | collective-permute-start | bytes 614408 | tf_op jit(solution)/shard_map/ppermute | solution.py:62
  28.2 7.2 %collective-permute-start.9 = (f32[16,3200]{1,0:T(8,128)S(1)}, f32[16,3200]{1,0:T(8,128)S(1)}, u32[]{:S(2)}, u32[]{:S(2)}) collective-permute-start(f32[16,3200]{1,0:T(8,128)S(1)} %shard_map.76), channel_id=1, source_target_pairs={{0,8},{4,12},{8,0},{12,4},{1,9},{5,13},{9,1},{13,5},{2,10},{6,14},... | collective-permute-start | bytes 614408 | tf_op jit(solution)/shard_map/ppermute | solution.py:62
  35.5 4.9 %collective-permute-start.11 = (bf16[4,3200]{1,0:T(4,128)(2,1)S(1)}, bf16[4,3200]{1,0:T(4,128)(2,1)S(1)}, u32[]{:S(2)}, u32[]{:S(2)}) collective-permute-start(bf16[4,3200]{1,0:T(4,128)(2,1)S(1)} %get-tuple-element.40), channel_id=1, source_target_pairs={{0,2},{1,3},{2,0},{3,1},{4,6},{5,7},{6,4},{7,5},{8,10},{9,11},{10,... | collective-permute-start | bytes 76808 | tf_op jit(solution)/shard_map/ppermute | solution.py:57
  38.5 5.6 %collective-permute-start.12 = (bf16[4,3200]{1,0:T(4,128)(2,1)S(1)}, bf16[4,3200]{1,0:T(4,128)(2,1)S(1)}, u32[]{:S(2)}, u32[]{:S(2)}) collective-permute-start(bf16[4,3200]{1,0:T(4,128)(2,1)S(1)} %get-tuple-element.41), channel_id=1, source_target_pairs={{0,3},{1,2},{2,1},{3,0},{4,7},{5,6},{6,5},{7,4},{8,11},{9,10},{10,... | collective-permute-start | bytes 76808 | tf_op jit(solution)/shard_map/ppermute | solution.py:57
  39.3 4.9 %collective-permute-start.13 = (bf16[4,3200]{1,0:T(4,128)(2,1)S(1)}, bf16[4,3200]{1,0:T(4,128)(2,1)S(1)}, u32[]{:S(2)}, u32[]{:S(2)}) collective-permute-start(bf16[4,3200]{1,0:T(4,128)(2,1)S(1)} %get-tuple-element.42), channel_id=1, source_target_pairs={{0,1},{1,0},{2,3},{3,2},{4,5},{5,4},{6,7},{7,6},{8,9},{9,8},{10,11... | collective-permute-start | bytes 76808 | tf_op jit(solution)/shard_map/ppermute | solution.py:57
  46.0 5.7 %collective-permute-start.14 = (bf16[4,3072]{1,0:T(4,128)(2,1)S(1)}, bf16[4,3072]{1,0:T(4,128)(2,1)S(1)}, u32[]{:S(2)}, u32[]{:S(2)}) collective-permute-start(bf16[4,3072]{1,0:T(4,128)(2,1)S(1)} %get-tuple-element.44), channel_id=1, source_target_pairs={{0,3},{1,2},{2,1},{3,0},{4,7},{5,6},{6,5},{7,4},{8,11},{9,10},{10,... | collective-permute-start | bytes 73736 | tf_op jit(solution)/shard_map/ppermute | solution.py:57
  48.1 4.7 %collective-permute-start.15 = (bf16[4,3072]{1,0:T(4,128)(2,1)S(1)}, bf16[4,3072]{1,0:T(4,128)(2,1)S(1)}, u32[]{:S(2)}, u32[]{:S(2)}) collective-permute-start(bf16[4,3072]{1,0:T(4,128)(2,1)S(1)} %get-tuple-element.45), channel_id=1, source_target_pairs={{0,2},{1,3},{2,0},{3,1},{4,6},{5,7},{6,4},{7,5},{8,10},{9,11},{10,... | collective-permute-start | bytes 73736 | tf_op jit(solution)/shard_map/ppermute | solution.py:57
  48.1 4.7 %collective-permute-start.16 = (bf16[4,3072]{1,0:T(4,128)(2,1)S(1)}, bf16[4,3072]{1,0:T(4,128)(2,1)S(1)}, u32[]{:S(2)}, u32[]{:S(2)}) collective-permute-start(bf16[4,3072]{1,0:T(4,128)(2,1)S(1)} %get-tuple-element.46), channel_id=1, source_target_pairs={{0,1},{1,0},{2,3},{3,2},{4,5},{5,4},{6,7},{7,6},{8,9},{9,8},{10,11... | collective-permute-start | bytes 73736 | tf_op jit(solution)/shard_map/ppermute | solution.py:57
  52.9 4.7 %collective-permute-start.18 = (bf16[16,3072]{1,0:T(8,128)(2,1)S(1)}, bf16[16,3072]{1,0:T(8,128)(2,1)S(1)}, u32[]{:S(2)}, u32[]{:S(2)}) collective-permute-start(bf16[16,3072]{1,0:T(8,128)(2,1)S(1)} %shard_map.79.refs_0_), channel_id=1, source_target_pairs={{0,8},{4,12},{8,0},{12,4},{1,9},{5,13},{9,1},{13,5},{2,10},{6,14},... | collective-permute-start | bytes 294920 | tf_op jit(solution)/shard_map/ppermute | solution.py:62
  53.6 4.0 %collective-permute-start.17 = (bf16[16,3072]{1,0:T(8,128)(2,1)S(1)}, bf16[16,3072]{1,0:T(8,128)(2,1)S(1)}, u32[]{:S(2)}, u32[]{:S(2)}) collective-permute-start(bf16[16,3072]{1,0:T(8,128)(2,1)S(1)} %shard_map.79.refs_0_), channel_id=1, source_target_pairs={{0,4},{4,0},{8,12},{12,8},{1,5},{5,1},{9,13},{13,9},{2,6},{6,2},{1... | collective-permute-start | bytes 294920 | tf_op jit(solution)/shard_map/ppermute | solution.py:62
  57.6 1.3 %collective-permute-start.19 = (bf16[16,3072]{1,0:T(8,128)(2,1)S(1)}, bf16[16,3072]{1,0:T(8,128)(2,1)S(1)}, u32[]{:S(2)}, u32[]{:S(2)}) collective-permute-start(bf16[16,3072]{1,0:T(8,128)(2,1)S(1)} %collective-permute-done.18.refs_2_), channel_id=1, source_target_pairs={{0,4},{4,0},{8,12},{12,8},{1,5},{5,1},{9,13},{13,9},{2,6},{6,2},{1... | collective-permute-start | bytes 294920 | tf_op jit(solution)/shard_map/ppermute | solution.py:62
  63.9 11.5 %collective-permute-start.20 = (bf16[16,4608]{1,0:T(8,128)(2,1)S(1)}, bf16[16,4608]{1,0:T(8,128)(2,1)S(1)}, u32[]{:S(2)}, u32[]{:S(2)}) collective-permute-start(bf16[16,4608]{1,0:T(8,128)(2,1)S(1)} %get-tuple-element.48), channel_id=1, source_target_pairs={{0,2},{1,3},{2,0},{3,1},{4,6},{5,7},{6,4},{7,5},{8,10},{9,11},{10,... | collective-permute-start | bytes 442376 | tf_op jit(solution)/shard_map/ppermute | solution.py:57
  66.0 9.4 %collective-permute-start.21 = (bf16[16,4608]{1,0:T(8,128)(2,1)S(1)}, bf16[16,4608]{1,0:T(8,128)(2,1)S(1)}, u32[]{:S(2)}, u32[]{:S(2)}) collective-permute-start(bf16[16,4608]{1,0:T(8,128)(2,1)S(1)} %get-tuple-element.49), channel_id=1, source_target_pairs={{0,1},{1,0},{2,3},{3,2},{4,5},{5,4},{6,7},{7,6},{8,9},{9,8},{10,11... | collective-permute-start | bytes 442376 | tf_op jit(solution)/shard_map/ppermute | solution.py:57
  66.4 11.8 %collective-permute-start.22 = (bf16[16,4608]{1,0:T(8,128)(2,1)S(1)}, bf16[16,4608]{1,0:T(8,128)(2,1)S(1)}, u32[]{:S(2)}, u32[]{:S(2)}) collective-permute-start(bf16[16,4608]{1,0:T(8,128)(2,1)S(1)} %get-tuple-element.50), channel_id=1, source_target_pairs={{0,3},{1,2},{2,1},{3,0},{4,7},{5,6},{6,5},{7,4},{8,11},{9,10},{10,... | collective-permute-start | bytes 442376 | tf_op jit(solution)/shard_map/ppermute | solution.py:57
  (10 other events, 184.1 us)

commit v6 on v5

--- a/solution.py
+++ b/solution.py
@@ -16,7 +16,7 @@
 B1 = (0, 1, 2)
 WIDE = jnp.float32
 B2 = (0, 2, 3, 1)
-C1 = (0, 3, 2, 1)
+C1 = (0, 2, 3, 1)
 C2 = (0, 1, 2, 3)
 D = (0, 2, 1, 3)
 

time: 79 us -> 78.5 us (level)
    ppermute x12, starting transfers between devices: 16.4 us -> 15.5 us  [exchange(): lax.ppermute(pieces[k], axis, [(i, i ^ k) for i in range(size)])]
where the time goes in v6:
time: 78.5 us; the launch traced here: 78 us
  waiting for transfers between devices  39.1 us (50%)
  starting transfers between devices  24.7 us (31%)
  Pallas kernels  13.9 us (18%)
    ppermute x12, waiting for transfers between devices, exchange(): lax.ppermute(pieces[k], axis, [(i, i ^ k) for i in range(size)])  20.4 us
    ppermute x11, waiting for transfers between devices, swap(): lax.ppermute(piece, axis, [(i, i ^ k) for i in range(lax.axis_size(axis))])  18.7 us
    ppermute x12, starting transfers between devices, exchange(): lax.ppermute(pieces[k], axis, [(i, i ^ k) for i in range(size)])  15.5 us
    pallas_call x9, Pallas kernels, call(): pl.pallas_call(ordered, out_shape=outs, in_specs=[in_specs[i] for i in or...  13.9 us
    ppermute x11, starting transfers between devices, swap(): lax.ppermute(piece, axis, [(i, i ^ k) for i in range(lax.axis_size(axis))])  9.27 us
  transfers between devices with their start and end apart: 23, of which 16 were waited for; matrix products, arithmetic and copies ran while one was open for 0% of the time, Pallas kernels for 0%

profile of v6, /device:TPU:0, one launch (start us, length us, event | category | flops | bytes accessed | tf_op | source)
XLA Modules:
  0.0 78.0 jit_solution(10599300878516294907)
XLA Ops:
  0.0 1.6 %shard_map.73 = (bf16[4,4608]{1,0:T(4,128)(2,1)S(1)}, bf16[4,4608]{1,0:T(4,128)(2,1)S(1)}, bf16[4,4608]{1,0:T(4,128)(2,1)S(1)}, bf16[4,4608]{1,0:T(4,128)(2,1)S(1)}) custom-call(bf16[4,18432]{1,0:T(4,128)(2,1)} %refs_0_.1, f32[1,18432]{1,0:T(1,128)} %bitcast.3), custom_call_target="tpu_custom_call" | custom-call | flops 49999998976 | tf_op jit(solution)/shard_map/pallas_call | solution.py:31
  2.2 2.6 %collective-permute-start.1 = (bf16[4,4608]{1,0:T(4,128)(2,1)S(1)}, bf16[4,4608]{1,0:T(4,128)(2,1)S(1)}, u32[]{:S(2)}, u32[]{:S(2)}) collective-permute-start(bf16[4,4608]{1,0:T(4,128)(2,1)S(1)} %get-tuple-element.30), channel_id=1, source_target_pairs={{0,12},{4,8},{8,4},{12,0},{1,13},{5,9},{9,5},{13,1},{2,14},{6,10},... | collective-permute-start | bytes 110600 | tf_op jit(solution)/shard_map/ppermute | solution.py:57
  4.9 1.7 %collective-permute-done.1.refs_2_ = bf16[4,4608]{1,0:T(4,128)(2,1)S(1)} collective-permute-done((bf16[4,4608]{1,0:T(4,128)(2,1)S(1)}, bf16[4,4608]{1,0:T(4,128)(2,1)S(1)}, u32[]{:S(2)}, u32[]{:S(2)}) %collective-permute-start.1) | collective-permute-done | bytes 36896 | tf_op jit(solution)/shard_map/ppermute | solution.py:57
  6.6 2.2 %collective-permute-done.2.refs_3_ = bf16[4,4608]{1,0:T(4,128)(2,1)S(1)} collective-permute-done((bf16[4,4608]{1,0:T(4,128)(2,1)S(1)}, bf16[4,4608]{1,0:T(4,128)(2,1)S(1)}, u32[]{:S(2)}, u32[]{:S(2)}) %collective-permute-start.2) | collective-permute-done | bytes 36896 | tf_op jit(solution)/shard_map/ppermute | solution.py:57
  8.8 2.7 %collective-permute-start.4 = (bf16[16,2304]{1,0:T(8,128)(2,1)S(1)}, bf16[16,2304]{1,0:T(8,128)(2,1)S(1)}, u32[]{:S(2)}, u32[]{:S(2)}) collective-permute-start(bf16[16,2304]{1,0:T(8,128)(2,1)S(1)} %get-tuple-element.33), channel_id=1, source_target_pairs={{0,2},{1,3},{2,0},{3,1},{4,6},{5,7},{6,4},{7,5},{8,10},{9,11},{10,... | collective-permute-start | bytes 221192 | tf_op jit(solution)/shard_map/ppermute | solution.py:62
  11.8 1.6 %collective-permute-start.3 = (bf16[16,4608]{1,0:T(8,128)(2,1)S(1)}, bf16[16,4608]{1,0:T(8,128)(2,1)S(1)}, u32[]{:S(2)}, u32[]{:S(2)}) collective-permute-start(bf16[16,4608]{1,0:T(8,128)(2,1)S(1)} %get-tuple-element.32.refs_0_), channel_id=1, source_target_pairs={{0,1},{1,0},{2,3},{3,2},{4,5},{5,4},{6,7},{7,6},{8,9},{9,8},{10,11... | collective-permute-start | bytes 442376 | tf_op jit(solution)/shard_map/ppermute | solution.py:62
  13.4 3.0 %collective-permute-done.4.refs_2_ = bf16[16,2304]{1,0:T(8,128)(2,1)S(1)} collective-permute-done((bf16[16,2304]{1,0:T(8,128)(2,1)S(1)}, bf16[16,2304]{1,0:T(8,128)(2,1)S(1)}, u32[]{:S(2)}, u32[]{:S(2)}) %collective-permute-start.4) | collective-permute-done | bytes 73760 | tf_op jit(solution)/shard_map/ppermute | solution.py:62
  18.9 2.2 %collective-permute-done.6.refs_4_ = bf16[16,2304]{1,0:T(8,128)(2,1)S(1)} collective-permute-done((bf16[16,2304]{1,0:T(8,128)(2,1)S(1)}, bf16[16,2304]{1,0:T(8,128)(2,1)S(1)}, u32[]{:S(2)}, u32[]{:S(2)}) %collective-permute-start.6) | collective-permute-done | bytes 73760 | tf_op jit(solution)/shard_map/ppermute | solution.py:62
  22.1 4.6 %shard_map.75 = (f32[16,3200]{1,0:T(8,128)S(1)}, f32[16,3200]{1,0:T(8,128)S(1)}, f32[16,3200]{1,0:T(8,128)S(1)}, f32[16,3200]{1,0:T(8,128)S(1)}) custom-call(bf16[16,4608]{1,0:T(8,128)(2,1)S(1)} %get-tuple-element.32.refs_0_, bf16[16,4608]{1,0:T(8,128)(2,1)S(1)} %collective-permute-done.3.refs_1_, bf16[16,2304]{1,0:T(8,128)(2,1)S(1)} %collective-permute-done.4.refs_2_, ...), custom_call_target="tpu_custom_call" | custom-call | flops 1887436800 | bytes 29491200 | tf_op jit(solution)/shard_map/pallas_call | solution.py:31
  28.2 1.3 %collective-permute-start.9 = (f32[16,3200]{1,0:T(8,128)S(1)}, f32[16,3200]{1,0:T(8,128)S(1)}, u32[]{:S(2)}, u32[]{:S(2)}) collective-permute-start(f32[16,3200]{1,0:T(8,128)S(1)} %shard_map.76), channel_id=1, source_target_pairs={{0,8},{4,12},{8,0},{12,4},{1,9},{5,13},{9,1},{13,5},{2,10},{6,14},... | collective-permute-start | bytes 614408 | tf_op jit(solution)/shard_map/ppermute | solution.py:62
  29.5 5.9 %collective-permute-done.9.refs_1_ = f32[16,3200]{1,0:T(8,128)S(1)} collective-permute-done((f32[16,3200]{1,0:T(8,128)S(1)}, f32[16,3200]{1,0:T(8,128)S(1)}, u32[]{:S(2)}, u32[]{:S(2)}) %collective-permute-start.9) | collective-permute-done | bytes 204832 | tf_op jit(solution)/shard_map/ppermute | solution.py:62
  35.5 3.1 %collective-permute-start.11 = (bf16[4,3200]{1,0:T(4,128)(2,1)S(1)}, bf16[4,3200]{1,0:T(4,128)(2,1)S(1)}, u32[]{:S(2)}, u32[]{:S(2)}) collective-permute-start(bf16[4,3200]{1,0:T(4,128)(2,1)S(1)} %get-tuple-element.40), channel_id=1, source_target_pairs={{0,2},{1,3},{2,0},{3,1},{4,6},{5,7},{6,4},{7,5},{8,10},{9,11},{10,... | collective-permute-start | bytes 76808 | tf_op jit(solution)/shard_map/ppermute | solution.py:57
  40.3 3.8 %collective-permute-done.12.refs_2_ = bf16[4,3200]{1,0:T(4,128)(2,1)S(1)} collective-permute-done((bf16[4,3200]{1,0:T(4,128)(2,1)S(1)}, bf16[4,3200]{1,0:T(4,128)(2,1)S(1)}, u32[]{:S(2)}, u32[]{:S(2)}) %collective-permute-start.12) | collective-permute-done | bytes 25632 | tf_op jit(solution)/shard_map/ppermute | solution.py:57
  44.2 1.8 %shard_map.78 = (bf16[4,3072]{1,0:T(4,128)(2,1)S(1)}, bf16[4,3072]{1,0:T(4,128)(2,1)S(1)}, bf16[4,3072]{1,0:T(4,128)(2,1)S(1)}, bf16[4,3072]{1,0:T(4,128)(2,1)S(1)}) custom-call(bf16[4,3200]{1,0:T(4,128)(2,1)S(1)} %get-tuple-element.39.refs_0_, bf16[4,3200]{1,0:T(4,128)(2,1)S(1)} %collective-permute-done.11.refs_1_, ...), custom_call_target="tpu_custom_call" | custom-call | flops 49999998976 | bytes 4194304 | tf_op jit(solution)/shard_map/pallas_call | solution.py:31
  48.2 1.4 %collective-permute-start.16 = (bf16[4,3072]{1,0:T(4,128)(2,1)S(1)}, bf16[4,3072]{1,0:T(4,128)(2,1)S(1)}, u32[]{:S(2)}, u32[]{:S(2)}) collective-permute-start(bf16[4,3072]{1,0:T(4,128)(2,1)S(1)} %get-tuple-element.46), channel_id=1, source_target_pairs={{0,1},{1,0},{2,3},{3,2},{4,5},{5,4},{6,7},{7,6},{8,9},{9,8},{10,11... | collective-permute-start | bytes 73736 | tf_op jit(solution)/shard_map/ppermute | solution.py:57
  49.6 1.2 %collective-permute-done.14.refs_1_ = bf16[4,3072]{1,0:T(4,128)(2,1)S(1)} collective-permute-done((bf16[4,3072]{1,0:T(4,128)(2,1)S(1)}, bf16[4,3072]{1,0:T(4,128)(2,1)S(1)}, u32[]{:S(2)}, u32[]{:S(2)}) %collective-permute-start.14) | collective-permute-done | bytes 24608 | tf_op jit(solution)/shard_map/ppermute | solution.py:57
  50.8 1.8 %collective-permute-done.15.refs_2_ = bf16[4,3072]{1,0:T(4,128)(2,1)S(1)} collective-permute-done((bf16[4,3072]{1,0:T(4,128)(2,1)S(1)}, bf16[4,3072]{1,0:T(4,128)(2,1)S(1)}, u32[]{:S(2)}, u32[]{:S(2)}) %collective-permute-start.15) | collective-permute-done | bytes 24608 | tf_op jit(solution)/shard_map/ppermute | solution.py:57
  53.8 3.5 %collective-permute-done.18.refs_2_ = bf16[16,3072]{1,0:T(8,128)(2,1)S(1)} collective-permute-done((bf16[16,3072]{1,0:T(8,128)(2,1)S(1)}, bf16[16,3072]{1,0:T(8,128)(2,1)S(1)}, u32[]{:S(2)}, u32[]{:S(2)}) %collective-permute-start.18) | collective-permute-done | bytes 98336 | tf_op jit(solution)/shard_map/ppermute | solution.py:62
  57.4 1.3 %collective-permute-done.19.refs_3_ = bf16[16,3072]{1,0:T(8,128)(2,1)S(1)} collective-permute-done((bf16[16,3072]{1,0:T(8,128)(2,1)S(1)}, bf16[16,3072]{1,0:T(8,128)(2,1)S(1)}, u32[]{:S(2)}, u32[]{:S(2)}) %collective-permute-start.19) | collective-permute-done | bytes 98336 | tf_op jit(solution)/shard_map/ppermute | solution.py:62
  58.7 5.0 %shard_map.80 = (f32[16,4608]{1,0:T(8,128)S(1)}, bf16[16,4608]{1,0:T(8,128)(2,1)S(1)}, bf16[16,4608]{1,0:T(8,128)(2,1)S(1)}, bf16[16,4608]{1,0:T(8,128)(2,1)S(1)}) custom-call(bf16[16,3072]{1,0:T(8,128)(2,1)S(1)} %shard_map.79.refs_0_, bf16[16,3072]{1,0:T(8,128)(2,1)S(1)} %collective-permute-done.17.refs_1_, ...), custom_call_target="tpu_custom_call" | custom-call | flops 1811939328 | bytes 28311552 | tf_op jit(solution)/shard_map/pallas_call | solution.py:31
  63.7 1.4 %collective-permute-start.20 = (bf16[16,4608]{1,0:T(8,128)(2,1)S(1)}, bf16[16,4608]{1,0:T(8,128)(2,1)S(1)}, u32[]{:S(2)}, u32[]{:S(2)}) collective-permute-start(bf16[16,4608]{1,0:T(8,128)(2,1)S(1)} %get-tuple-element.48), channel_id=1, source_target_pairs={{0,2},{1,3},{2,0},{3,1},{4,6},{5,7},{6,4},{7,5},{8,10},{9,11},{10,... | collective-permute-start | bytes 442376 | tf_op jit(solution)/shard_map/ppermute | solution.py:57
  66.3 1.8 %collective-permute-start.22 = (bf16[16,4608]{1,0:T(8,128)(2,1)S(1)}, bf16[16,4608]{1,0:T(8,128)(2,1)S(1)}, u32[]{:S(2)}, u32[]{:S(2)}) collective-permute-start(bf16[16,4608]{1,0:T(8,128)(2,1)S(1)} %get-tuple-element.50), channel_id=1, source_target_pairs={{0,3},{1,2},{2,1},{3,0},{4,7},{5,6},{6,5},{7,4},{8,11},{9,10},{10,... | collective-permute-start | bytes 442376 | tf_op jit(solution)/shard_map/ppermute | solution.py:57
  68.2 6.7 %collective-permute-done.20.refs_1_ = bf16[16,4608]{1,0:T(8,128)(2,1)S(1)} collective-permute-done((bf16[16,4608]{1,0:T(8,128)(2,1)S(1)}, bf16[16,4608]{1,0:T(8,128)(2,1)S(1)}, u32[]{:S(2)}, u32[]{:S(2)}) %collective-permute-start.20) | collective-permute-done | bytes 147488 | tf_op jit(solution)/shard_map/ppermute | solution.py:57
  74.9 2.4 %collective-permute-done.22.refs_3_ = bf16[16,4608]{1,0:T(8,128)(2,1)S(1)} collective-permute-done((bf16[16,4608]{1,0:T(8,128)(2,1)S(1)}, bf16[16,4608]{1,0:T(8,128)(2,1)S(1)}, u32[]{:S(2)}, u32[]{:S(2)}) %collective-permute-start.22) | collective-permute-done | bytes 147488 | tf_op jit(solution)/shard_map/ppermute | solution.py:57
  (54 shorter events, 13.2 us)
Async XLA Ops:
  1.7 42.5 %copy-start.1 = (bf16[4,1024,256]{2,1,0:T(8,128)(2,1)S(1)}, bf16[4,1024,256]{2,1,0:T(8,128)(2,1)}, u32[]{:S(2)}) copy-start(bf16[4,1024,256]{2,1,0:T(8,128)(2,1)} %refs_4_.2) | copy-start | bytes 6291460
  1.7 3.2 %collective-permute-start = (bf16[4,4608]{1,0:T(4,128)(2,1)S(1)}, bf16[4,4608]{1,0:T(4,128)(2,1)S(1)}, u32[]{:S(2)}, u32[]{:S(2)}) collective-permute-start(bf16[4,4608]{1,0:T(4,128)(2,1)S(1)} %get-tuple-element.29), channel_id=1, source_target_pairs={{0,4},{4,0},{8,12},{12,8},{1,5},{5,1},{9,13},{13,9},{2,6},{6,2},{1... | collective-permute-start | bytes 110600 | tf_op jit(solution)/shard_map/ppermute | solution.py:57
  2.2 4.4 %collective-permute-start.1 = (bf16[4,4608]{1,0:T(4,128)(2,1)S(1)}, bf16[4,4608]{1,0:T(4,128)(2,1)S(1)}, u32[]{:S(2)}, u32[]{:S(2)}) collective-permute-start(bf16[4,4608]{1,0:T(4,128)(2,1)S(1)} %get-tuple-element.30), channel_id=1, source_target_pairs={{0,12},{4,8},{8,4},{12,0},{1,13},{5,9},{9,5},{13,1},{2,14},{6,10},... | collective-permute-start | bytes 110600 | tf_op jit(solution)/shard_map/ppermute | solution.py:57
  4.8 4.0 %collective-permute-start.2 = (bf16[4,4608]{1,0:T(4,128)(2,1)S(1)}, bf16[4,4608]{1,0:T(4,128)(2,1)S(1)}, u32[]{:S(2)}, u32[]{:S(2)}) collective-permute-start(bf16[4,4608]{1,0:T(4,128)(2,1)S(1)} %get-tuple-element.31), channel_id=1, source_target_pairs={{0,8},{4,12},{8,0},{12,4},{1,9},{5,13},{9,1},{13,5},{2,10},{6,14},... | collective-permute-start | bytes 110600 | tf_op jit(solution)/shard_map/ppermute | solution.py:57
  8.8 7.6 %collective-permute-start.4 = (bf16[16,2304]{1,0:T(8,128)(2,1)S(1)}, bf16[16,2304]{1,0:T(8,128)(2,1)S(1)}, u32[]{:S(2)}, u32[]{:S(2)}) collective-permute-start(bf16[16,2304]{1,0:T(8,128)(2,1)S(1)} %get-tuple-element.33), channel_id=1, source_target_pairs={{0,2},{1,3},{2,0},{3,1},{4,6},{5,7},{6,4},{7,5},{8,10},{9,11},{10,... | collective-permute-start | bytes 221192 | tf_op jit(solution)/shard_map/ppermute | solution.py:62
  11.5 6.3 %collective-permute-start.5 = (bf16[16,2304]{1,0:T(8,128)(2,1)S(1)}, bf16[16,2304]{1,0:T(8,128)(2,1)S(1)}, u32[]{:S(2)}, u32[]{:S(2)}) collective-permute-start(bf16[16,2304]{1,0:T(8,128)(2,1)S(1)} %get-tuple-element.34), channel_id=1, source_target_pairs={{0,2},{1,3},{2,0},{3,1},{4,6},{5,7},{6,4},{7,5},{8,10},{9,11},{10,... | collective-permute-start | bytes 221192 | tf_op jit(solution)/shard_map/ppermute | solution.py:62
  11.8 10.3 %collective-permute-start.3 = (bf16[16,4608]{1,0:T(8,128)(2,1)S(1)}, bf16[16,4608]{1,0:T(8,128)(2,1)S(1)}, u32[]{:S(2)}, u32[]{:S(2)}) collective-permute-start(bf16[16,4608]{1,0:T(8,128)(2,1)S(1)} %get-tuple-element.32.refs_0_), channel_id=1, source_target_pairs={{0,1},{1,0},{2,3},{3,2},{4,5},{5,4},{6,7},{7,6},{8,9},{9,8},{10,11... | collective-permute-start | bytes 442376 | tf_op jit(solution)/shard_map/ppermute | solution.py:62
  16.4 4.7 %collective-permute-start.6 = (bf16[16,2304]{1,0:T(8,128)(2,1)S(1)}, bf16[16,2304]{1,0:T(8,128)(2,1)S(1)}, u32[]{:S(2)}, u32[]{:S(2)}) collective-permute-start(bf16[16,2304]{1,0:T(8,128)(2,1)S(1)} %collective-permute-done.4.refs_2_), channel_id=1, source_target_pairs={{0,1},{1,0},{2,3},{3,2},{4,5},{5,4},{6,7},{7,6},{8,9},{9,8},{10,11... | collective-permute-start | bytes 221192 | tf_op jit(solution)/shard_map/ppermute | solution.py:62
  17.7 4.4 %collective-permute-start.7 = (bf16[16,2304]{1,0:T(8,128)(2,1)S(1)}, bf16[16,2304]{1,0:T(8,128)(2,1)S(1)}, u32[]{:S(2)}, u32[]{:S(2)}) collective-permute-start(bf16[16,2304]{1,0:T(8,128)(2,1)S(1)} %collective-permute-done.5.refs_3_), channel_id=1, source_target_pairs={{0,1},{1,0},{2,3},{3,2},{4,5},{5,4},{6,7},{7,6},{8,9},{9,8},{10,11... | collective-permute-start | bytes 221192 | tf_op jit(solution)/shard_map/ppermute | solution.py:62
  26.7 1.5 %collective-permute-start.8 = (f32[16,3200]{1,0:T(8,128)S(1)}, f32[16,3200]{1,0:T(8,128)S(1)}, u32[]{:S(2)}, u32[]{:S(2)}) collective-permute-start(f32[16,3200]{1,0:T(8,128)S(1)} %get-tuple-element.37), channel_id=1, source_target_pairs={{0,4},{4,0},{8,12},{12,8},{1,5},{5,1},{9,13},{13,9},{2,6},{6,2},{1... | collective-permute-start | bytes 614408 | tf_op jit(solution)/shard_map/ppermute | solution.py:62
  26.8 2.7 %collective-permute-start.10 = (f32[16,3200]{1,0:T(8,128)S(1)}, f32[16,3200]{1,0:T(8,128)S(1)}, u32[]{:S(2)}, u32[]{:S(2)}) collective-permute-start(f32[16,3200]{1,0:T(8,128)S(1)} %get-tuple-element.38), channel_id=1, source_target_pairs={{0,4},{4,0},{8,12},{12,8},{1,5},{5,1},{9,13},{13,9},{2,6},{6,2},{1... | collective-permute-start | bytes 614408 | tf_op jit(solution)/shard_map/ppermute | solution.py:62
  28.2 7.2 %collective-permute-start.9 = (f32[16,3200]{1,0:T(8,128)S(1)}, f32[16,3200]{1,0:T(8,128)S(1)}, u32[]{:S(2)}, u32[]{:S(2)}) collective-permute-start(f32[16,3200]{1,0:T(8,128)S(1)} %shard_map.76), channel_id=1, source_target_pairs={{0,8},{4,12},{8,0},{12,4},{1,9},{5,13},{9,1},{13,5},{2,10},{6,14},... | collective-permute-start | bytes 614408 | tf_op jit(solution)/shard_map/ppermute | solution.py:62
  35.5 4.9 %collective-permute-start.11 = (bf16[4,3200]{1,0:T(4,128)(2,1)S(1)}, bf16[4,3200]{1,0:T(4,128)(2,1)S(1)}, u32[]{:S(2)}, u32[]{:S(2)}) collective-permute-start(bf16[4,3200]{1,0:T(4,128)(2,1)S(1)} %get-tuple-element.40), channel_id=1, source_target_pairs={{0,2},{1,3},{2,0},{3,1},{4,6},{5,7},{6,4},{7,5},{8,10},{9,11},{10,... | collective-permute-start | bytes 76808 | tf_op jit(solution)/shard_map/ppermute | solution.py:57
  38.5 5.6 %collective-permute-start.12 = (bf16[4,3200]{1,0:T(4,128)(2,1)S(1)}, bf16[4,3200]{1,0:T(4,128)(2,1)S(1)}, u32[]{:S(2)}, u32[]{:S(2)}) collective-permute-start(bf16[4,3200]{1,0:T(4,128)(2,1)S(1)} %get-tuple-element.41), channel_id=1, source_target_pairs={{0,3},{1,2},{2,1},{3,0},{4,7},{5,6},{6,5},{7,4},{8,11},{9,10},{10,... | collective-permute-start | bytes 76808 | tf_op jit(solution)/shard_map/ppermute | solution.py:57
  39.3 4.9 %collective-permute-start.13 = (bf16[4,3200]{1,0:T(4,128)(2,1)S(1)}, bf16[4,3200]{1,0:T(4,128)(2,1)S(1)}, u32[]{:S(2)}, u32[]{:S(2)}) collective-permute-start(bf16[4,3200]{1,0:T(4,128)(2,1)S(1)} %get-tuple-element.42), channel_id=1, source_target_pairs={{0,1},{1,0},{2,3},{3,2},{4,5},{5,4},{6,7},{7,6},{8,9},{9,8},{10,11... | collective-permute-start | bytes 76808 | tf_op jit(solution)/shard_map/ppermute | solution.py:57
  46.0 4.8 %collective-permute-start.14 = (bf16[4,3072]{1,0:T(4,128)(2,1)S(1)}, bf16[4,3072]{1,0:T(4,128)(2,1)S(1)}, u32[]{:S(2)}, u32[]{:S(2)}) collective-permute-start(bf16[4,3072]{1,0:T(4,128)(2,1)S(1)} %get-tuple-element.44), channel_id=1, source_target_pairs={{0,2},{1,3},{2,0},{3,1},{4,6},{5,7},{6,4},{7,5},{8,10},{9,11},{10,... | collective-permute-start | bytes 73736 | tf_op jit(solution)/shard_map/ppermute | solution.py:57
  47.0 5.6 %collective-permute-start.15 = (bf16[4,3072]{1,0:T(4,128)(2,1)S(1)}, bf16[4,3072]{1,0:T(4,128)(2,1)S(1)}, u32[]{:S(2)}, u32[]{:S(2)}) collective-permute-start(bf16[4,3072]{1,0:T(4,128)(2,1)S(1)} %get-tuple-element.45), channel_id=1, source_target_pairs={{0,3},{1,2},{2,1},{3,0},{4,7},{5,6},{6,5},{7,4},{8,11},{9,10},{10,... | collective-permute-start | bytes 73736 | tf_op jit(solution)/shard_map/ppermute | solution.py:57
  48.2 4.4 %collective-permute-start.16 = (bf16[4,3072]{1,0:T(4,128)(2,1)S(1)}, bf16[4,3072]{1,0:T(4,128)(2,1)S(1)}, u32[]{:S(2)}, u32[]{:S(2)}) collective-permute-start(bf16[4,3072]{1,0:T(4,128)(2,1)S(1)} %get-tuple-element.46), channel_id=1, source_target_pairs={{0,1},{1,0},{2,3},{3,2},{4,5},{5,4},{6,7},{7,6},{8,9},{9,8},{10,11... | collective-permute-start | bytes 73736 | tf_op jit(solution)/shard_map/ppermute | solution.py:57
  52.7 4.7 %collective-permute-start.18 = (bf16[16,3072]{1,0:T(8,128)(2,1)S(1)}, bf16[16,3072]{1,0:T(8,128)(2,1)S(1)}, u32[]{:S(2)}, u32[]{:S(2)}) collective-permute-start(bf16[16,3072]{1,0:T(8,128)(2,1)S(1)} %shard_map.79.refs_0_), channel_id=1, source_target_pairs={{0,8},{4,12},{8,0},{12,4},{1,9},{5,13},{9,1},{13,5},{2,10},{6,14},... | collective-permute-start | bytes 294920 | tf_op jit(solution)/shard_map/ppermute | solution.py:62
  53.8 3.5 %collective-permute-start.17 = (bf16[16,3072]{1,0:T(8,128)(2,1)S(1)}, bf16[16,3072]{1,0:T(8,128)(2,1)S(1)}, u32[]{:S(2)}, u32[]{:S(2)}) collective-permute-start(bf16[16,3072]{1,0:T(8,128)(2,1)S(1)} %shard_map.79.refs_0_), channel_id=1, source_target_pairs={{0,4},{4,0},{8,12},{12,8},{1,5},{5,1},{9,13},{13,9},{2,6},{6,2},{1... | collective-permute-start | bytes 294920 | tf_op jit(solution)/shard_map/ppermute | solution.py:62
  57.4 1.3 %collective-permute-start.19 = (bf16[16,3072]{1,0:T(8,128)(2,1)S(1)}, bf16[16,3072]{1,0:T(8,128)(2,1)S(1)}, u32[]{:S(2)}, u32[]{:S(2)}) collective-permute-start(bf16[16,3072]{1,0:T(8,128)(2,1)S(1)} %collective-permute-done.18.refs_2_), channel_id=1, source_target_pairs={{0,4},{4,0},{8,12},{12,8},{1,5},{5,1},{9,13},{13,9},{2,6},{6,2},{1... | collective-permute-start | bytes 294920 | tf_op jit(solution)/shard_map/ppermute | solution.py:62
  63.7 11.1 %collective-permute-start.20 = (bf16[16,4608]{1,0:T(8,128)(2,1)S(1)}, bf16[16,4608]{1,0:T(8,128)(2,1)S(1)}, u32[]{:S(2)}, u32[]{:S(2)}) collective-permute-start(bf16[16,4608]{1,0:T(8,128)(2,1)S(1)} %get-tuple-element.48), channel_id=1, source_target_pairs={{0,2},{1,3},{2,0},{3,1},{4,6},{5,7},{6,4},{7,5},{8,10},{9,11},{10,... | collective-permute-start | bytes 442376 | tf_op jit(solution)/shard_map/ppermute | solution.py:57
  65.1 9.7 %collective-permute-start.21 = (bf16[16,4608]{1,0:T(8,128)(2,1)S(1)}, bf16[16,4608]{1,0:T(8,128)(2,1)S(1)}, u32[]{:S(2)}, u32[]{:S(2)}) collective-permute-start(bf16[16,4608]{1,0:T(8,128)(2,1)S(1)} %get-tuple-element.49), channel_id=1, source_target_pairs={{0,1},{1,0},{2,3},{3,2},{4,5},{5,4},{6,7},{7,6},{8,9},{9,8},{10,11... | collective-permute-start | bytes 442376 | tf_op jit(solution)/shard_map/ppermute | solution.py:57
  66.3 10.9 %collective-permute-start.22 = (bf16[16,4608]{1,0:T(8,128)(2,1)S(1)}, bf16[16,4608]{1,0:T(8,128)(2,1)S(1)}, u32[]{:S(2)}, u32[]{:S(2)}) collective-permute-start(bf16[16,4608]{1,0:T(8,128)(2,1)S(1)} %get-tuple-element.50), channel_id=1, source_target_pairs={{0,3},{1,2},{2,1},{3,0},{4,7},{5,6},{6,5},{7,4},{8,11},{9,10},{10,... | collective-permute-start | bytes 442376 | tf_op jit(solution)/shard_map/ppermute | solution.py:57
  (10 other events, 183.2 us)

commit v7 on v6

--- a/solution.py
+++ b/solution.py
@@ -139,13 +139,18 @@
         out[...] = total[j * each : (j + 1) * each].astype(jnp.bfloat16)
 
 
+def turn_body(key_ref, out_ref):
+    for s in range(key_ref.shape[0]):
+        out_ref[s] = key_ref[s].T
+
+
 def attend_body(blocks, heads, *refs):
     pieces, (key_ref, value_ref, length_ref) = refs[:blocks], refs[blocks : blocks + 3]
     outs = refs[blocks + 3 : 2 * blocks + 3]
     row_ref, query_ref, mixed_ref = refs[2 * blocks + 3 :]
     me = lax.axis_index("yz")
     part = pieces[0].shape[1]
-    seqs, slots, head = key_ref.shape
+    seqs, head, slots = key_ref.shape
     scale = 1.0 / jnp.sqrt(jnp.float32(head))
     for j, piece in enumerate(pieces):
         row_ref[:, pl.ds(pl.multiple_of((me ^ j) * part, 128), part)] = piece[...].astype(jnp.float32)
@@ -162,7 +167,7 @@
         lax.dot_general(
             queries[s].astype(jnp.bfloat16),
             key_ref[s],
-            (((1,), (1,)), ((), ())),
+            (((1,), (0,)), ((), ())),
             preferred_element_type=jnp.float32,
         )
         for s in range(seqs)
@@ -190,7 +195,14 @@
 def attend(pieces, cache_keys, cache_values, cache_lengths, width):
     seqs, slots, head = cache_keys.shape
     blocks, heads = len(pieces), width // head
-    keys = pltpu.with_memory_space_constraint(cache_keys, pltpu.VMEM)
+    keys = call(
+        turn_body,
+        struct((seqs, head, slots)),
+        [VMEM],
+        [near(cache_keys)],
+        flops=seqs * slots * head,
+        traffic=4 * seqs * slots * head,
+    )
     values = pltpu.with_memory_space_constraint(cache_values, pltpu.VMEM)
     return call(
         functools.partial(attend_body, blocks, heads),

time: 78.5 us -> 79.3 us (1.010)
  local copies, waits for them, and re-layouts: 0.06 us -> 3.11 us
  waiting for transfers between devices: 39.1 us -> 36.7 us
    unnamed x22 -> x36, local copies, waits for them, and re-layouts: 0.06 us -> 3.11 us
    ppermute x12, waiting for transfers between devices: 20.4 us -> 18 us  [exchange(): lax.ppermute(pieces[k], axis, [(i, i ^ k) for i in range(size)])]
    pallas_call x9 -> x10, Pallas kernels: 13.9 us -> 14.3 us  [call(): pl.pallas_call(ordered, out_shape=outs, in_specs=[in_specs[i] for i in or...]
  transfers between devices with their start and end apart: 23 -> 23, of which waited for: 16 -> 14; matrix products, arithmetic and copies ran while one was open for 0% -> 0% of each run, Pallas kernels for 0% -> 1%
where the time goes in v7:
time: 79.3 us; the launch traced here: 79.1 us
  waiting for transfers between devices  36.7 us (46%)
  starting transfers between devices  24.8 us (31%)
  Pallas kernels  14.3 us (18%)
  local copies, waits for them, and re-layouts  3.11 us (4%)
    ppermute x11, waiting for transfers between devices, swap(): lax.ppermute(piece, axis, [(i, i ^ k) for i in range(lax.axis_size(axis))])  18.7 us
    ppermute x12, waiting for transfers between devices, exchange(): lax.ppermute(pieces[k], axis, [(i, i ^ k) for i in range(size)])  18 us
    ppermute x12, starting transfers between devices, exchange(): lax.ppermute(pieces[k], axis, [(i, i ^ k) for i in range(size)])  15.5 us
    pallas_call x10, Pallas kernels, call(): pl.pallas_call(ordered, out_shape=outs, in_specs=[in_specs[i] for i in or...  14.3 us
    ppermute x11, starting transfers between devices, swap(): lax.ppermute(piece, axis, [(i, i ^ k) for i in range(lax.axis_size(axis))])  9.26 us
    unnamed x36, local copies, waits for them, and re-layouts  3.11 us
  transfers between devices with their start and end apart: 23, of which 14 were waited for; matrix products, arithmetic and copies ran while one was open for 0% of the time, Pallas kernels for 1%

profile of v7, /device:TPU:0, one launch (start us, length us, event | category | flops | bytes accessed | tf_op | source)
XLA Modules:
  0.0 79.1 jit_solution(474410071002923041)
XLA Ops:
  0.0 1.6 %shard_map.73 = (bf16[4,4608]{1,0:T(4,128)(2,1)S(1)}, bf16[4,4608]{1,0:T(4,128)(2,1)S(1)}, bf16[4,4608]{1,0:T(4,128)(2,1)S(1)}, bf16[4,4608]{1,0:T(4,128)(2,1)S(1)}) custom-call(bf16[4,18432]{1,0:T(4,128)(2,1)} %refs_0_.2, f32[1,18432]{1,0:T(1,128)} %bitcast.5), custom_call_target="tpu_custom_call" | custom-call | flops 49999998976 | tf_op jit(solution)/shard_map/pallas_call | solution.py:31
  2.2 2.6 %collective-permute-start.1 = (bf16[4,4608]{1,0:T(4,128)(2,1)S(1)}, bf16[4,4608]{1,0:T(4,128)(2,1)S(1)}, u32[]{:S(2)}, u32[]{:S(2)}) collective-permute-start(bf16[4,4608]{1,0:T(4,128)(2,1)S(1)} %get-tuple-element.30), channel_id=1, source_target_pairs={{0,12},{4,8},{8,4},{12,0},{1,13},{5,9},{9,5},{13,1},{2,14},{6,10},... | collective-permute-start | bytes 110600 | tf_op jit(solution)/shard_map/ppermute | solution.py:57
  4.9 1.7 %collective-permute-done.1.refs_2_ = bf16[4,4608]{1,0:T(4,128)(2,1)S(1)} collective-permute-done((bf16[4,4608]{1,0:T(4,128)(2,1)S(1)}, bf16[4,4608]{1,0:T(4,128)(2,1)S(1)}, u32[]{:S(2)}, u32[]{:S(2)}) %collective-permute-start.1) | collective-permute-done | bytes 36896 | tf_op jit(solution)/shard_map/ppermute | solution.py:57
  6.6 2.2 %collective-permute-done.2.refs_3_ = bf16[4,4608]{1,0:T(4,128)(2,1)S(1)} collective-permute-done((bf16[4,4608]{1,0:T(4,128)(2,1)S(1)}, bf16[4,4608]{1,0:T(4,128)(2,1)S(1)}, u32[]{:S(2)}, u32[]{:S(2)}) %collective-permute-start.2) | collective-permute-done | bytes 36896 | tf_op jit(solution)/shard_map/ppermute | solution.py:57
  8.9 2.7 %collective-permute-start.4 = (bf16[16,2304]{1,0:T(8,128)(2,1)S(1)}, bf16[16,2304]{1,0:T(8,128)(2,1)S(1)}, u32[]{:S(2)}, u32[]{:S(2)}) collective-permute-start(bf16[16,2304]{1,0:T(8,128)(2,1)S(1)} %get-tuple-element.33), channel_id=1, source_target_pairs={{0,2},{1,3},{2,0},{3,1},{4,6},{5,7},{6,4},{7,5},{8,10},{9,11},{10,... | collective-permute-start | bytes 221192 | tf_op jit(solution)/shard_map/ppermute | solution.py:62
  11.9 1.6 %collective-permute-start.3 = (bf16[16,4608]{1,0:T(8,128)(2,1)S(1)}, bf16[16,4608]{1,0:T(8,128)(2,1)S(1)}, u32[]{:S(2)}, u32[]{:S(2)}) collective-permute-start(bf16[16,4608]{1,0:T(8,128)(2,1)S(1)} %get-tuple-element.32.refs_0_), channel_id=1, source_target_pairs={{0,1},{1,0},{2,3},{3,2},{4,5},{5,4},{6,7},{7,6},{8,9},{9,8},{10,11... | collective-permute-start | bytes 442376 | tf_op jit(solution)/shard_map/ppermute | solution.py:62
  13.4 3.0 %collective-permute-done.4.refs_2_ = bf16[16,2304]{1,0:T(8,128)(2,1)S(1)} collective-permute-done((bf16[16,2304]{1,0:T(8,128)(2,1)S(1)}, bf16[16,2304]{1,0:T(8,128)(2,1)S(1)}, u32[]{:S(2)}, u32[]{:S(2)}) %collective-permute-start.4) | collective-permute-done | bytes 73760 | tf_op jit(solution)/shard_map/ppermute | solution.py:62
  19.0 2.2 %collective-permute-done.6.refs_4_ = bf16[16,2304]{1,0:T(8,128)(2,1)S(1)} collective-permute-done((bf16[16,2304]{1,0:T(8,128)(2,1)S(1)}, bf16[16,2304]{1,0:T(8,128)(2,1)S(1)}, u32[]{:S(2)}, u32[]{:S(2)}) %collective-permute-start.6) | collective-permute-done | bytes 73760 | tf_op jit(solution)/shard_map/ppermute | solution.py:62
  22.2 4.6 %shard_map.75 = (f32[16,3200]{1,0:T(8,128)S(1)}, f32[16,3200]{1,0:T(8,128)S(1)}, f32[16,3200]{1,0:T(8,128)S(1)}, f32[16,3200]{1,0:T(8,128)S(1)}) custom-call(bf16[16,4608]{1,0:T(8,128)(2,1)S(1)} %get-tuple-element.32.refs_0_, bf16[16,4608]{1,0:T(8,128)(2,1)S(1)} %collective-permute-done.3.refs_1_, bf16[16,2304]{1,0:T(8,128)(2,1)S(1)} %collective-permute-done.4.refs_2_, ...), custom_call_target="tpu_custom_call" | custom-call | flops 1887436800 | bytes 29491200 | tf_op jit(solution)/shard_map/pallas_call | solution.py:31
  28.3 1.3 %collective-permute-start.9 = (f32[16,3200]{1,0:T(8,128)S(1)}, f32[16,3200]{1,0:T(8,128)S(1)}, u32[]{:S(2)}, u32[]{:S(2)}) collective-permute-start(f32[16,3200]{1,0:T(8,128)S(1)} %shard_map.76), channel_id=1, source_target_pairs={{0,8},{4,12},{8,0},{12,4},{1,9},{5,13},{9,1},{13,5},{2,10},{6,14},... | collective-permute-start | bytes 614408 | tf_op jit(solution)/shard_map/ppermute | solution.py:62
  29.6 5.9 %collective-permute-done.9.refs_1_ = f32[16,3200]{1,0:T(8,128)S(1)} collective-permute-done((f32[16,3200]{1,0:T(8,128)S(1)}, f32[16,3200]{1,0:T(8,128)S(1)}, u32[]{:S(2)}, u32[]{:S(2)}) %collective-permute-start.9) | collective-permute-done | bytes 204832 | tf_op jit(solution)/shard_map/ppermute | solution.py:62
  35.6 3.1 %collective-permute-start.11 = (bf16[4,3200]{1,0:T(4,128)(2,1)S(1)}, bf16[4,3200]{1,0:T(4,128)(2,1)S(1)}, u32[]{:S(2)}, u32[]{:S(2)}) collective-permute-start(bf16[4,3200]{1,0:T(4,128)(2,1)S(1)} %get-tuple-element.40), channel_id=1, source_target_pairs={{0,2},{1,3},{2,0},{3,1},{4,6},{5,7},{6,4},{7,5},{8,10},{9,11},{10,... | collective-permute-start | bytes 76808 | tf_op jit(solution)/shard_map/ppermute | solution.py:57
  40.5 3.8 %collective-permute-done.12.refs_2_ = bf16[4,3200]{1,0:T(4,128)(2,1)S(1)} collective-permute-done((bf16[4,3200]{1,0:T(4,128)(2,1)S(1)}, bf16[4,3200]{1,0:T(4,128)(2,1)S(1)}, u32[]{:S(2)}, u32[]{:S(2)}) %collective-permute-start.12) | collective-permute-done | bytes 25632 | tf_op jit(solution)/shard_map/ppermute | solution.py:57
  44.3 1.6 %shard_map.79 = (bf16[4,3072]{1,0:T(4,128)(2,1)S(1)}, bf16[4,3072]{1,0:T(4,128)(2,1)S(1)}, bf16[4,3072]{1,0:T(4,128)(2,1)S(1)}, bf16[4,3072]{1,0:T(4,128)(2,1)S(1)}) custom-call(bf16[4,3200]{1,0:T(4,128)(2,1)S(1)} %get-tuple-element.39.refs_0_, bf16[4,3200]{1,0:T(4,128)(2,1)S(1)} %collective-permute-done.11.refs_1_, ...), custom_call_target="tpu_custom_call" | custom-call | flops 49999998976 | bytes 4194304 | tf_op jit(solution)/shard_map/pallas_call | solution.py:31
  48.1 1.4 %collective-permute-start.16 = (bf16[4,3072]{1,0:T(4,128)(2,1)S(1)}, bf16[4,3072]{1,0:T(4,128)(2,1)S(1)}, u32[]{:S(2)}, u32[]{:S(2)}) collective-permute-start(bf16[4,3072]{1,0:T(4,128)(2,1)S(1)} %get-tuple-element.46), channel_id=1, source_target_pairs={{0,1},{1,0},{2,3},{3,2},{4,5},{5,4},{6,7},{7,6},{8,9},{9,8},{10,11... | collective-permute-start | bytes 73736 | tf_op jit(solution)/shard_map/ppermute | solution.py:57
  49.5 1.2 %collective-permute-done.14.refs_1_ = bf16[4,3072]{1,0:T(4,128)(2,1)S(1)} collective-permute-done((bf16[4,3072]{1,0:T(4,128)(2,1)S(1)}, bf16[4,3072]{1,0:T(4,128)(2,1)S(1)}, u32[]{:S(2)}, u32[]{:S(2)}) %collective-permute-start.14) | collective-permute-done | bytes 24608 | tf_op jit(solution)/shard_map/ppermute | solution.py:57
  50.7 1.8 %collective-permute-done.15.refs_2_ = bf16[4,3072]{1,0:T(4,128)(2,1)S(1)} collective-permute-done((bf16[4,3072]{1,0:T(4,128)(2,1)S(1)}, bf16[4,3072]{1,0:T(4,128)(2,1)S(1)}, u32[]{:S(2)}, u32[]{:S(2)}) %collective-permute-start.15) | collective-permute-done | bytes 24608 | tf_op jit(solution)/shard_map/ppermute | solution.py:57
  53.8 3.5 %collective-permute-done.18.refs_2_ = bf16[16,3072]{1,0:T(8,128)(2,1)S(1)} collective-permute-done((bf16[16,3072]{1,0:T(8,128)(2,1)S(1)}, bf16[16,3072]{1,0:T(8,128)(2,1)S(1)}, u32[]{:S(2)}, u32[]{:S(2)}) %collective-permute-start.18) | collective-permute-done | bytes 98336 | tf_op jit(solution)/shard_map/ppermute | solution.py:62
  57.3 1.3 %collective-permute-done.19.refs_3_ = bf16[16,3072]{1,0:T(8,128)(2,1)S(1)} collective-permute-done((bf16[16,3072]{1,0:T(8,128)(2,1)S(1)}, bf16[16,3072]{1,0:T(8,128)(2,1)S(1)}, u32[]{:S(2)}, u32[]{:S(2)}) %collective-permute-start.19) | collective-permute-done | bytes 98336 | tf_op jit(solution)/shard_map/ppermute | solution.py:62
  61.7 5.0 %shard_map.81 = (f32[16,4608]{1,0:T(8,128)S(1)}, bf16[16,4608]{1,0:T(8,128)(2,1)S(1)}, bf16[16,4608]{1,0:T(8,128)(2,1)S(1)}, bf16[16,4608]{1,0:T(8,128)(2,1)S(1)}) custom-call(bf16[16,3072]{1,0:T(8,128)(2,1)S(1)} %shard_map.80.refs_0_, bf16[16,3072]{1,0:T(8,128)(2,1)S(1)} %collective-permute-done.17.refs_1_, ...), custom_call_target="tpu_custom_call" | custom-call | flops 1811939328 | bytes 28311552 | tf_op jit(solution)/shard_map/pallas_call | solution.py:31
  66.6 1.4 %collective-permute-start.20 = (bf16[16,4608]{1,0:T(8,128)(2,1)S(1)}, bf16[16,4608]{1,0:T(8,128)(2,1)S(1)}, u32[]{:S(2)}, u32[]{:S(2)}) collective-permute-start(bf16[16,4608]{1,0:T(8,128)(2,1)S(1)} %get-tuple-element.48), channel_id=1, source_target_pairs={{0,2},{1,3},{2,0},{3,1},{4,6},{5,7},{6,4},{7,5},{8,10},{9,11},{10,... | collective-permute-start | bytes 442376 | tf_op jit(solution)/shard_map/ppermute | solution.py:57
  68.1 1.2 %collective-permute-start.21 = (bf16[16,4608]{1,0:T(8,128)(2,1)S(1)}, bf16[16,4608]{1,0:T(8,128)(2,1)S(1)}, u32[]{:S(2)}, u32[]{:S(2)}) collective-permute-start(bf16[16,4608]{1,0:T(8,128)(2,1)S(1)} %get-tuple-element.49), channel_id=1, source_target_pairs={{0,1},{1,0},{2,3},{3,2},{4,5},{5,4},{6,7},{7,6},{8,9},{9,8},{10,11... | collective-permute-start | bytes 442376 | tf_op jit(solution)/shard_map/ppermute | solution.py:57
  69.3 1.8 %collective-permute-start.22 = (bf16[16,4608]{1,0:T(8,128)(2,1)S(1)}, bf16[16,4608]{1,0:T(8,128)(2,1)S(1)}, u32[]{:S(2)}, u32[]{:S(2)}) collective-permute-start(bf16[16,4608]{1,0:T(8,128)(2,1)S(1)} %get-tuple-element.50), channel_id=1, source_target_pairs={{0,3},{1,2},{2,1},{3,0},{4,7},{5,6},{6,5},{7,4},{8,11},{9,10},{10,... | collective-permute-start | bytes 442376 | tf_op jit(solution)/shard_map/ppermute | solution.py:57
  71.1 7.3 %collective-permute-done.20.refs_1_ = bf16[16,4608]{1,0:T(8,128)(2,1)S(1)} collective-permute-done((bf16[16,4608]{1,0:T(8,128)(2,1)S(1)}, bf16[16,4608]{1,0:T(8,128)(2,1)S(1)}, u32[]{:S(2)}, u32[]{:S(2)}) %collective-permute-start.20) | collective-permute-done | bytes 147488 | tf_op jit(solution)/shard_map/ppermute | solution.py:57
  (70 shorter events, 15.1 us)
Async XLA Ops:
  0.0 22.2 %slice-start.5 = ((s8[29491200]{0:T(1024)(128)(4,1)}), s8[4194304]{0:T(1024)(128)(4,1)S(1)}, s32[]{:S(2)}) async-start(s8[29491200]{0:T(1024)(128)(4,1)} %bitcast.1), calls=%async_computation.5 | async-start | bytes 8388608
  1.7 3.2 %collective-permute-start = (bf16[4,4608]{1,0:T(4,128)(2,1)S(1)}, bf16[4,4608]{1,0:T(4,128)(2,1)S(1)}, u32[]{:S(2)}, u32[]{:S(2)}) collective-permute-start(bf16[4,4608]{1,0:T(4,128)(2,1)S(1)} %get-tuple-element.29), channel_id=1, source_target_pairs={{0,4},{4,0},{8,12},{12,8},{1,5},{5,1},{9,13},{13,9},{2,6},{6,2},{1... | collective-permute-start | bytes 110600 | tf_op jit(solution)/shard_map/ppermute | solution.py:57
  2.2 4.4 %collective-permute-start.1 = (bf16[4,4608]{1,0:T(4,128)(2,1)S(1)}, bf16[4,4608]{1,0:T(4,128)(2,1)S(1)}, u32[]{:S(2)}, u32[]{:S(2)}) collective-permute-start(bf16[4,4608]{1,0:T(4,128)(2,1)S(1)} %get-tuple-element.30), channel_id=1, source_target_pairs={{0,12},{4,8},{8,4},{12,0},{1,13},{5,9},{9,5},{13,1},{2,14},{6,10},... | collective-permute-start | bytes 110600 | tf_op jit(solution)/shard_map/ppermute | solution.py:57
  4.8 4.0 %collective-permute-start.2 = (bf16[4,4608]{1,0:T(4,128)(2,1)S(1)}, bf16[4,4608]{1,0:T(4,128)(2,1)S(1)}, u32[]{:S(2)}, u32[]{:S(2)}) collective-permute-start(bf16[4,4608]{1,0:T(4,128)(2,1)S(1)} %get-tuple-element.31), channel_id=1, source_target_pairs={{0,8},{4,12},{8,0},{12,4},{1,9},{5,13},{9,1},{13,5},{2,10},{6,14},... | collective-permute-start | bytes 110600 | tf_op jit(solution)/shard_map/ppermute | solution.py:57
  8.9 7.6 %collective-permute-start.4 = (bf16[16,2304]{1,0:T(8,128)(2,1)S(1)}, bf16[16,2304]{1,0:T(8,128)(2,1)S(1)}, u32[]{:S(2)}, u32[]{:S(2)}) collective-permute-start(bf16[16,2304]{1,0:T(8,128)(2,1)S(1)} %get-tuple-element.33), channel_id=1, source_target_pairs={{0,2},{1,3},{2,0},{3,1},{4,6},{5,7},{6,4},{7,5},{8,10},{9,11},{10,... | collective-permute-start | bytes 221192 | tf_op jit(solution)/shard_map/ppermute | solution.py:62
  11.5 6.3 %collective-permute-start.5 = (bf16[16,2304]{1,0:T(8,128)(2,1)S(1)}, bf16[16,2304]{1,0:T(8,128)(2,1)S(1)}, u32[]{:S(2)}, u32[]{:S(2)}) collective-permute-start(bf16[16,2304]{1,0:T(8,128)(2,1)S(1)} %get-tuple-element.34), channel_id=1, source_target_pairs={{0,2},{1,3},{2,0},{3,1},{4,6},{5,7},{6,4},{7,5},{8,10},{9,11},{10,... | collective-permute-start | bytes 221192 | tf_op jit(solution)/shard_map/ppermute | solution.py:62
  11.9 10.3 %collective-permute-start.3 = (bf16[16,4608]{1,0:T(8,128)(2,1)S(1)}, bf16[16,4608]{1,0:T(8,128)(2,1)S(1)}, u32[]{:S(2)}, u32[]{:S(2)}) collective-permute-start(bf16[16,4608]{1,0:T(8,128)(2,1)S(1)} %get-tuple-element.32.refs_0_), channel_id=1, source_target_pairs={{0,1},{1,0},{2,3},{3,2},{4,5},{5,4},{6,7},{7,6},{8,9},{9,8},{10,11... | collective-permute-start | bytes 442376 | tf_op jit(solution)/shard_map/ppermute | solution.py:62
  16.4 4.7 %collective-permute-start.6 = (bf16[16,2304]{1,0:T(8,128)(2,1)S(1)}, bf16[16,2304]{1,0:T(8,128)(2,1)S(1)}, u32[]{:S(2)}, u32[]{:S(2)}) collective-permute-start(bf16[16,2304]{1,0:T(8,128)(2,1)S(1)} %collective-permute-done.4.refs_2_), channel_id=1, source_target_pairs={{0,1},{1,0},{2,3},{3,2},{4,5},{5,4},{6,7},{7,6},{8,9},{9,8},{10,11... | collective-permute-start | bytes 221192 | tf_op jit(solution)/shard_map/ppermute | solution.py:62
  17.8 4.4 %collective-permute-start.7 = (bf16[16,2304]{1,0:T(8,128)(2,1)S(1)}, bf16[16,2304]{1,0:T(8,128)(2,1)S(1)}, u32[]{:S(2)}, u32[]{:S(2)}) collective-permute-start(bf16[16,2304]{1,0:T(8,128)(2,1)S(1)} %collective-permute-done.5.refs_3_), channel_id=1, source_target_pairs={{0,1},{1,0},{2,3},{3,2},{4,5},{5,4},{6,7},{7,6},{8,9},{9,8},{10,11... | collective-permute-start | bytes 221192 | tf_op jit(solution)/shard_map/ppermute | solution.py:62
  26.8 1.5 %collective-permute-start.8 = (f32[16,3200]{1,0:T(8,128)S(1)}, f32[16,3200]{1,0:T(8,128)S(1)}, u32[]{:S(2)}, u32[]{:S(2)}) collective-permute-start(f32[16,3200]{1,0:T(8,128)S(1)} %get-tuple-element.37), channel_id=1, source_target_pairs={{0,4},{4,0},{8,12},{12,8},{1,5},{5,1},{9,13},{13,9},{2,6},{6,2},{1... | collective-permute-start | bytes 614408 | tf_op jit(solution)/shard_map/ppermute | solution.py:62
  26.9 2.7 %collective-permute-start.10 = (f32[16,3200]{1,0:T(8,128)S(1)}, f32[16,3200]{1,0:T(8,128)S(1)}, u32[]{:S(2)}, u32[]{:S(2)}) collective-permute-start(f32[16,3200]{1,0:T(8,128)S(1)} %get-tuple-element.38), channel_id=1, source_target_pairs={{0,4},{4,0},{8,12},{12,8},{1,5},{5,1},{9,13},{13,9},{2,6},{6,2},{1... | collective-permute-start | bytes 614408 | tf_op jit(solution)/shard_map/ppermute | solution.py:62
  28.3 7.2 %collective-permute-start.9 = (f32[16,3200]{1,0:T(8,128)S(1)}, f32[16,3200]{1,0:T(8,128)S(1)}, u32[]{:S(2)}, u32[]{:S(2)}) collective-permute-start(f32[16,3200]{1,0:T(8,128)S(1)} %shard_map.76), channel_id=1, source_target_pairs={{0,8},{4,12},{8,0},{12,4},{1,9},{5,13},{9,1},{13,5},{2,10},{6,14},... | collective-permute-start | bytes 614408 | tf_op jit(solution)/shard_map/ppermute | solution.py:62
  35.6 4.9 %collective-permute-start.11 = (bf16[4,3200]{1,0:T(4,128)(2,1)S(1)}, bf16[4,3200]{1,0:T(4,128)(2,1)S(1)}, u32[]{:S(2)}, u32[]{:S(2)}) collective-permute-start(bf16[4,3200]{1,0:T(4,128)(2,1)S(1)} %get-tuple-element.40), channel_id=1, source_target_pairs={{0,2},{1,3},{2,0},{3,1},{4,6},{5,7},{6,4},{7,5},{8,10},{9,11},{10,... | collective-permute-start | bytes 76808 | tf_op jit(solution)/shard_map/ppermute | solution.py:57
  38.6 5.6 %collective-permute-start.12 = (bf16[4,3200]{1,0:T(4,128)(2,1)S(1)}, bf16[4,3200]{1,0:T(4,128)(2,1)S(1)}, u32[]{:S(2)}, u32[]{:S(2)}) collective-permute-start(bf16[4,3200]{1,0:T(4,128)(2,1)S(1)} %get-tuple-element.41), channel_id=1, source_target_pairs={{0,3},{1,2},{2,1},{3,0},{4,7},{5,6},{6,5},{7,4},{8,11},{9,10},{10,... | collective-permute-start | bytes 76808 | tf_op jit(solution)/shard_map/ppermute | solution.py:57
  39.4 4.9 %collective-permute-start.13 = (bf16[4,3200]{1,0:T(4,128)(2,1)S(1)}, bf16[4,3200]{1,0:T(4,128)(2,1)S(1)}, u32[]{:S(2)}, u32[]{:S(2)}) collective-permute-start(bf16[4,3200]{1,0:T(4,128)(2,1)S(1)} %get-tuple-element.42), channel_id=1, source_target_pairs={{0,1},{1,0},{2,3},{3,2},{4,5},{5,4},{6,7},{7,6},{8,9},{9,8},{10,11... | collective-permute-start | bytes 76808 | tf_op jit(solution)/shard_map/ppermute | solution.py:57
  45.9 4.8 %collective-permute-start.14 = (bf16[4,3072]{1,0:T(4,128)(2,1)S(1)}, bf16[4,3072]{1,0:T(4,128)(2,1)S(1)}, u32[]{:S(2)}, u32[]{:S(2)}) collective-permute-start(bf16[4,3072]{1,0:T(4,128)(2,1)S(1)} %get-tuple-element.44), channel_id=1, source_target_pairs={{0,2},{1,3},{2,0},{3,1},{4,6},{5,7},{6,4},{7,5},{8,10},{9,11},{10,... | collective-permute-start | bytes 73736 | tf_op jit(solution)/shard_map/ppermute | solution.py:57
  46.9 5.6 %collective-permute-start.15 = (bf16[4,3072]{1,0:T(4,128)(2,1)S(1)}, bf16[4,3072]{1,0:T(4,128)(2,1)S(1)}, u32[]{:S(2)}, u32[]{:S(2)}) collective-permute-start(bf16[4,3072]{1,0:T(4,128)(2,1)S(1)} %get-tuple-element.45), channel_id=1, source_target_pairs={{0,3},{1,2},{2,1},{3,0},{4,7},{5,6},{6,5},{7,4},{8,11},{9,10},{10,... | collective-permute-start | bytes 73736 | tf_op jit(solution)/shard_map/ppermute | solution.py:57
  48.1 4.4 %collective-permute-start.16 = (bf16[4,3072]{1,0:T(4,128)(2,1)S(1)}, bf16[4,3072]{1,0:T(4,128)(2,1)S(1)}, u32[]{:S(2)}, u32[]{:S(2)}) collective-permute-start(bf16[4,3072]{1,0:T(4,128)(2,1)S(1)} %get-tuple-element.46), channel_id=1, source_target_pairs={{0,1},{1,0},{2,3},{3,2},{4,5},{5,4},{6,7},{7,6},{8,9},{9,8},{10,11... | collective-permute-start | bytes 73736 | tf_op jit(solution)/shard_map/ppermute | solution.py:57
  52.6 4.7 %collective-permute-start.18 = (bf16[16,3072]{1,0:T(8,128)(2,1)S(1)}, bf16[16,3072]{1,0:T(8,128)(2,1)S(1)}, u32[]{:S(2)}, u32[]{:S(2)}) collective-permute-start(bf16[16,3072]{1,0:T(8,128)(2,1)S(1)} %shard_map.80.refs_0_), channel_id=1, source_target_pairs={{0,8},{4,12},{8,0},{12,4},{1,9},{5,13},{9,1},{13,5},{2,10},{6,14},... | collective-permute-start | bytes 294920 | tf_op jit(solution)/shard_map/ppermute | solution.py:62
  53.7 3.6 %collective-permute-start.17 = (bf16[16,3072]{1,0:T(8,128)(2,1)S(1)}, bf16[16,3072]{1,0:T(8,128)(2,1)S(1)}, u32[]{:S(2)}, u32[]{:S(2)}) collective-permute-start(bf16[16,3072]{1,0:T(8,128)(2,1)S(1)} %shard_map.80.refs_0_), channel_id=1, source_target_pairs={{0,4},{4,0},{8,12},{12,8},{1,5},{5,1},{9,13},{13,9},{2,6},{6,2},{1... | collective-permute-start | bytes 294920 | tf_op jit(solution)/shard_map/ppermute | solution.py:62
  57.3 1.3 %collective-permute-start.19 = (bf16[16,3072]{1,0:T(8,128)(2,1)S(1)}, bf16[16,3072]{1,0:T(8,128)(2,1)S(1)}, u32[]{:S(2)}, u32[]{:S(2)}) collective-permute-start(bf16[16,3072]{1,0:T(8,128)(2,1)S(1)} %collective-permute-done.18.refs_2_), channel_id=1, source_target_pairs={{0,4},{4,0},{8,12},{12,8},{1,5},{5,1},{9,13},{13,9},{2,6},{6,2},{1... | collective-permute-start | bytes 294920 | tf_op jit(solution)/shard_map/ppermute | solution.py:62
  66.6 11.8 %collective-permute-start.20 = (bf16[16,4608]{1,0:T(8,128)(2,1)S(1)}, bf16[16,4608]{1,0:T(8,128)(2,1)S(1)}, u32[]{:S(2)}, u32[]{:S(2)}) collective-permute-start(bf16[16,4608]{1,0:T(8,128)(2,1)S(1)} %get-tuple-element.48), channel_id=1, source_target_pairs={{0,2},{1,3},{2,0},{3,1},{4,6},{5,7},{6,4},{7,5},{8,10},{9,11},{10,... | collective-permute-start | bytes 442376 | tf_op jit(solution)/shard_map/ppermute | solution.py:57
  68.1 10.3 %collective-permute-start.21 = (bf16[16,4608]{1,0:T(8,128)(2,1)S(1)}, bf16[16,4608]{1,0:T(8,128)(2,1)S(1)}, u32[]{:S(2)}, u32[]{:S(2)}) collective-permute-start(bf16[16,4608]{1,0:T(8,128)(2,1)S(1)} %get-tuple-element.49), channel_id=1, source_target_pairs={{0,1},{1,0},{2,3},{3,2},{4,5},{5,4},{6,7},{7,6},{8,9},{9,8},{10,11... | collective-permute-start | bytes 442376 | tf_op jit(solution)/shard_map/ppermute | solution.py:57
  69.3 9.1 %collective-permute-start.22 = (bf16[16,4608]{1,0:T(8,128)(2,1)S(1)}, bf16[16,4608]{1,0:T(8,128)(2,1)S(1)}, u32[]{:S(2)}, u32[]{:S(2)}) collective-permute-start(bf16[16,4608]{1,0:T(8,128)(2,1)S(1)} %get-tuple-element.50), channel_id=1, source_target_pairs={{0,3},{1,2},{2,1},{3,0},{4,7},{5,6},{6,5},{7,4},{8,11},{9,10},{10,... | collective-permute-start | bytes 442376 | tf_op jit(solution)/shard_map/ppermute | solution.py:57
  (17 other events, 231.1 us)
